TPU v7x, 32 devices: a whole 2x2x4 slice. The times are simulated.
32 devices in a mesh: section: 4 (over z), expert: 2 (over core), tensor: 4 (over y, x).
Axes of the slice: x: 2, y: 2, z: 4, core: 2. Of those that a mesh axis runs over, the one named last changes fastest.
Arguments:
- tokens: bfloat16 [4096, 6144], P(('section', 'expert'), 'tensor'), may hold values from -6 to 6
- norm_gain: float32 [2, 6144], P(None, 'tensor'), may hold values from 0.5 to 1.5
- router: float32 [2, 6144, 8], P(None, 'tensor'), may hold values from -0.078125 to 0.078125
- w_gate: bfloat16 [4, 2, 6144, 4096], P('section', 'expert', None, 'tensor'), may hold values from -0.078125 to 0.078125
- w_up: bfloat16 [4, 2, 6144, 4096], P('section', 'expert', None, 'tensor'), may hold values from -0.078125 to 0.078125
- w_down: bfloat16 [4, 2, 4096, 6144], P('section', 'expert', 'tensor'), may hold values from -0.0625 to 0.0625
- expert_ids: int32 [2, 4096, 2], P(None, ('section', 'expert')), may hold values from 0 to 7, all different within a row
- lengths: int32 [4, 8], P(None, 'expert'), may hold values from 32 to 128
Outputs:
- encoded: bfloat16 [4096, 6144], P(('section', 'expert'), 'tensor')
All inputs are finite; a program needn't handle non-finite values.
Results may differ from a plain program's by a relative error of at most 0.006.
Values may be sent and summed in bfloat16 or wider, within the bound.
No kernel may reach another device: no remote copies, remote signals or barrier semaphores. Data moves between devices by JAX's collectives and lax.ppermute only.
A program may use at most 128 MiB of HBM per device.

v0:
```python
import jax
import jax.numpy as jnp
from jax import lax
from jax.sharding import PartitionSpec as P

D = 6144
E = 8
EXP_WIN = 2
SEQ_LEN = 128
STEPS = 2
CAP = 64


norm_eps = 1e-05


def swapped(x, axis, bit):
    return lax.ppermute(x, axis, [(i, i ^ 1 << bit) for i in range(lax.axis_size(axis))])


def from_behind(x, axis, by):
    peers = lax.axis_size(axis)
    return lax.ppermute(x, axis, [(i, (i + by) % peers) for i in range(peers)])


def route_tables(choice_ids, seq_lens, gate_logits):
    token_count = choice_ids.shape[0]
    expert_range = jnp.arange(E, dtype=jnp.int32)
    match_ids = choice_ids[:, :, None] == expert_range[None, None, :]
    one_hot = match_ids.astype(jnp.float32)
    picked = jnp.sum(gate_logits[:, None, :] * one_hot, axis=2)
    first_weight = jax.nn.sigmoid(picked[:, 0] - picked[:, 1])
    second_weight = jax.nn.sigmoid(picked[:, 1] - picked[:, 0])
    dense_gates = (
        first_weight[:, None] * one_hot[:, 0, :] + second_weight[:, None] * one_hot[:, 1, :]
    )
    dense_gates = dense_gates[:, :EXP_WIN]
    positions = jnp.arange(token_count, dtype=jnp.int32)
    live_rows = positions % SEQ_LEN < jnp.repeat(seq_lens, SEQ_LEN, total_repeat_length=token_count)
    named = jnp.any(match_ids, axis=1)[:, :EXP_WIN] & live_rows[:, None]
    named_int = named.astype(jnp.int32)
    earlier = jnp.cumsum(named_int, axis=0) - named_int
    slot_range = jnp.arange(CAP, dtype=jnp.int32)
    placed = named[None, :, :] & (earlier[None, :, :] == slot_range[:, None, None])
    route_table = jnp.transpose(placed.astype(jnp.float32), (2, 0, 1))
    return (route_table, route_table * jnp.transpose(dense_gates)[:, None, :])


def moe_layer(
    layer_rows, gain_row, router_matrix, gate_w, up_w, down_w, choice_ids, seq_lens, expert_count
):
    as_float = layer_rows.astype(jnp.float32)
    scaled = as_float * gain_row[None, :]
    part_logits = jnp.dot(scaled, router_matrix, precision=lax.Precision.HIGHEST)
    square_sum, logit_sum = lax.psum((jnp.sum(as_float * as_float, axis=1), part_logits), "tensor")
    inv_rms = lax.rsqrt(square_sum / D + norm_eps)
    normed = (scaled * inv_rms[:, None]).astype(jnp.bfloat16)
    gate_logits = inv_rms[:, None] * logit_sum
    route_table, weighted = route_tables(choice_ids, seq_lens, gate_logits)
    fsplit_count = expert_count // EXP_WIN
    table_narrow = route_table.astype(jnp.bfloat16)
    feature_count = normed.shape[1]
    picked_rows = jnp.einsum(
        "ecr,rd->ecd", table_narrow, normed, preferred_element_type=jnp.float32
    ).astype(jnp.bfloat16)
    widened = jnp.broadcast_to(picked_rows[:, None], (EXP_WIN, fsplit_count, CAP, feature_count))
    arrived = lax.all_to_all(
        widened.reshape(expert_count, CAP, feature_count),
        "expert",
        split_axis=0,
        concat_axis=1,
        tiled=True,
    )
    partner = swapped(arrived, "section", 0)
    held_rows = jnp.concatenate([arrived, partner], axis=1)
    feature_piece = lax.all_gather(held_rows, "tensor", axis=2, tiled=True)
    col_count = feature_piece.shape[2]
    gate_part = lax.slice_in_dim(gate_w, 0, col_count, axis=1)
    up_part = lax.slice_in_dim(up_w, 0, col_count, axis=1)
    gate_more = jnp.einsum(
        "snd,sdf->snf", feature_piece, gate_part, preferred_element_type=jnp.float32
    )
    up_more = jnp.einsum("snd,sdf->snf", feature_piece, up_part, preferred_element_type=jnp.float32)
    hidden = (jax.nn.silu(gate_more) * up_more).astype(jnp.bfloat16)
    partial_out = jnp.einsum("snf,sfd->snd", hidden, down_w, preferred_element_type=jnp.float32)
    summed = lax.psum_scatter(
        partial_out.astype(jnp.bfloat16), "tensor", scatter_dimension=2, tiled=True
    )
    own_count = summed.shape[1] // 2
    own_part = summed[:, :own_count]
    other_part = summed[:, own_count:]
    from_partner = swapped(other_part, "section", 0)
    slab_out = (own_part.astype(jnp.float32) + from_partner.astype(jnp.float32)).astype(
        jnp.bfloat16
    )
    returned = lax.all_to_all(slab_out, "expert", split_axis=1, concat_axis=0, tiled=True)
    half_width = returned.shape[2]
    per_expert = jnp.sum(
        returned.reshape(EXP_WIN, fsplit_count, CAP, half_width).astype(jnp.float32), axis=1
    )
    mixture = jnp.einsum("ecr,ecd->rd", weighted, per_expert, precision=lax.Precision.HIGHEST)
    return (as_float + mixture).astype(jnp.bfloat16)


def on_device(tokens, norm_gain, router, w_gate, w_up, w_down, expert_ids, lengths):
    section_count = lax.axis_size("section")
    section_place = lax.axis_index("section")
    expert_count = lax.axis_size("expert")
    layer_place = section_place // 2
    gain_row = lax.dynamic_index_in_dim(norm_gain, layer_place, 0, keepdims=False)
    router_matrix = lax.dynamic_index_in_dim(router, layer_place, 0, keepdims=False)
    current = tokens
    for step_index in range(STEPS):
        micro_batch = (section_place - 2 * step_index) % section_count
        seq_lens = lax.dynamic_index_in_dim(lengths, micro_batch, 0, keepdims=False)
        current = moe_layer(
            current,
            gain_row,
            router_matrix,
            w_gate[0],
            w_up[0],
            w_down[0],
            expert_ids[step_index],
            seq_lens,
            expert_count,
        )
        if step_index + 1 < STEPS:
            current = from_behind(current, "section", 2)
    return current


def solution(mesh):
    in_specs = (
        P(("section", "expert"), "tensor"),
        P(None, "tensor"),
        P(None, "tensor", None),
        P("section", "expert", None, "tensor"),
        P("section", "expert", None, "tensor"),
        P("section", "expert", "tensor", None),
        P(None, ("section", "expert"), None),
        P(None, "expert"),
    )
    out_specs = P(("section", "expert"), "tensor")
    return jax.shard_map(
        on_device, mesh=mesh, in_specs=in_specs, out_specs=out_specs, check_vma=False
    )
```

profile of v0, /device:TPU:0, one launch (start us, length us, event | category | flops | bytes accessed | tf_op | source)
XLA Modules:
  0.0 439.4 jit_solution(13651161327817163588)
XLA Ops:
  6.6 1.9 fusion.30
  10.0 4.3 fusion.25
  14.2 17.7 %all-reduce.1 = (f32[512]{0:T(512)S(1)}, f32[512,8]{0,1:T(8,128)S(1)}) all-reduce(f32[512]{0:T(512)S(1)} %fusion.30, f32[512,8]{0,1:T(8,128)S(1)} %fusion.25), channel_id=1, replica_groups=mesh['section'=4,'expert'=2,'tensor'=4] {'tensor'}, use_global_device_ids=true, to_apply=%region_4.6 | all-reduce | flops 4608 | bytes 36864 | tf_op jit(solution)/shard_map/psum | solution.py:55
  32.7 2.5 select_compare_fusion.1
  37.0 4.0 all_to_all.42
  41.1 1.6 collective-permute-start
  42.7 9.6 %collective-permute-done = bf16[1,128,1536]{2,1,0:T(8,128)(2,1)S(1)} collective-permute-done((bf16[1,128,1536]{2,1,0:T(8,128)(2,1)S(1)}, bf16[1,128,1536]{2,1,0:T(8,128)(2,1)S(1)}, u32[]{:S(2)}, u32[]{:S(2)}) %collective-permute-start) | collective-permute-done | bytes 393248 | tf_op jit(solution)/shard_map/ppermute | solution.py:18
  53.2 43.5 %all-gather.3.cloned.1.call-done = bf16[1,256,6144]{2,1,0:T(8,128)(2,1)} async-done(((bf16[1,256,1536]{2,1,0:T(8,128)(2,1)}), bf16[1,256,6144]{2,1,0:T(8,128)(2,1)}) %all-gather.3.cloned.1.call-update) | async-done | bytes 3145744 | tf_op jit(solution)/shard_map/all_gather | solution.py:76
  96.7 7.3 %fusion.6 = f32[256,1024]{1,0:T(8,128)S(1)} fusion(bf16[1,1,6144,1024]{3,2,1,0:T(8,128)(2,1)} %param.18, bf16[1,256,6144]{2,1,0:T(8,128)(2,1)} %all-gather.3.cloned.1.call-done), kind=kOutput, calls=%fused_computation.6 | convolution fusion | flops 3221225472 | bytes 16777216 | tf_op jit(solution)/shard_map/snd,sdf->snf/dot_general | solution.py:83
  104.1 17.4 %fusion.21 = bf16[1,256,6144]{2,1,0:T(8,128)(2,1)} fusion(bf16[1,1,1024,6144]{3,2,1,0:T(8,128)(2,1)} %param.19, f32[256,1024]{1,0:T(8,128)S(1)} %fusion.6, bf16[1,1,6144,1024]{3,2,1,0:T(8,128)(2,1)} %param.17, bf16[1,256,6144]{2,1,0:T(8,128)(2,1)} %all-gather.3.cloned.1.call-done), kind=kOutput, calls=%fused_computation.15 | convolution fusion | flops 6445596672 | bytes 32505856 | tf_op jit(solution)/shard_map/snf,sfd->snd/dot_general | solution.py:85
  121.8 43.8 %reduce-scatter.3.cloned.1.call-done = bf16[1,256,1536]{2,1,0:T(8,128)(2,1)} async-done(((bf16[1,256,6144]{2,1,0:T(8,128)(2,1)}), bf16[1,256,1536]{2,1,0:T(8,128)(2,1)}) %reduce-scatter.3.cloned.1.call-update) | async-done | bytes 786448 | tf_op jit(solution)/shard_map/reduce_scatter | solution.py:86
  166.7 1.6 collective-permute-start.1
  168.3 9.3 %collective-permute-done.1 = bf16[1,128,1536]{2,1,0:T(8,128)(2,1)S(1)} collective-permute-done((bf16[1,128,1536]{2,1,0:T(8,128)(2,1)S(1)}, bf16[1,128,1536]{2,1,0:T(8,128)(2,1)S(1)}, u32[]{:S(2)}, u32[]{:S(2)}) %collective-permute-start.1) | collective-permute-done | bytes 393248 | tf_op jit(solution)/shard_map/ppermute | solution.py:18
  179.8 2.9 reduce.9
  183.0 4.0 all_to_all.43
  187.5 1.6 fusion.31
  189.1 2.5 collective-permute-start.2
  191.5 2.5 select_compare_fusion
  195.2 65.0 %collective-permute-done.2 = bf16[512,1536]{1,0:T(8,128)(2,1)S(1)} collective-permute-done((bf16[512,1536]{1,0:T(8,128)(2,1)S(1)}, bf16[512,1536]{1,0:T(8,128)(2,1)S(1)}, u32[]{:S(2)}, u32[]{:S(2)}) %collective-permute-start.2) | collective-permute-done | bytes 1572896 | tf_op jit(solution)/shard_map/ppermute | solution.py:23
  260.6 2.9 fusion.27
  263.5 15.2 %all-reduce = (f32[512]{0:T(512)S(1)}, f32[512,8]{0,1:T(8,128)S(1)}) all-reduce(f32[512]{0:T(512)S(1)} %fusion.32, f32[512,8]{0,1:T(8,128)S(1)} %fusion.27), channel_id=1, replica_groups=mesh['section'=4,'expert'=2,'tensor'=4] {'tensor'}, use_global_device_ids=true, to_apply=%region_12.14 | all-reduce | flops 4608 | bytes 36864 | tf_op jit(solution)/shard_map/psum | solution.py:55
  279.4 4.0 all_to_all.44
  283.9 10.7 %collective-permute-done.3 = bf16[1,128,1536]{2,1,0:T(8,128)(2,1)S(1)} collective-permute-done((bf16[1,128,1536]{2,1,0:T(8,128)(2,1)S(1)}, bf16[1,128,1536]{2,1,0:T(8,128)(2,1)S(1)}, u32[]{:S(2)}, u32[]{:S(2)}) %collective-permute-start.3) | collective-permute-done | bytes 393248 | tf_op jit(solution)/shard_map/ppermute | solution.py:18
  295.8 43.8 %all-gather.5.cloned.1.call-done = bf16[1,256,6144]{2,1,0:T(8,128)(2,1)} async-done(((bf16[1,256,1536]{2,1,0:T(8,128)(2,1)}), bf16[1,256,6144]{2,1,0:T(8,128)(2,1)}) %all-gather.5.cloned.1.call-update) | async-done | bytes 3145744 | tf_op jit(solution)/shard_map/all_gather | solution.py:76
  339.6 7.3 %fusion.4 = f32[256,1024]{1,0:T(8,128)S(1)} fusion(bf16[1,1,6144,1024]{3,2,1,0:T(8,128)(2,1)} %param.18, bf16[1,256,6144]{2,1,0:T(8,128)(2,1)} %all-gather.5.cloned.1.call-done), kind=kOutput, calls=%fused_computation.4 | convolution fusion | flops 3221225472 | bytes 16777216 | tf_op jit(solution)/shard_map/snd,sdf->snf/dot_general | solution.py:83
  346.9 17.4 %fusion.18 = bf16[1,256,6144]{2,1,0:T(8,128)(2,1)} fusion(bf16[1,1,1024,6144]{3,2,1,0:T(8,128)(2,1)} %param.19, f32[256,1024]{1,0:T(8,128)S(1)} %fusion.4, bf16[1,1,6144,1024]{3,2,1,0:T(8,128)(2,1)} %param.17, bf16[1,256,6144]{2,1,0:T(8,128)(2,1)} %all-gather.5.cloned.1.call-done), kind=kOutput, calls=%fused_computation.14 | convolution fusion | flops 6445596672 | bytes 32505856 | tf_op jit(solution)/shard_map/snf,sfd->snd/dot_general | solution.py:85
  364.4 44.1 %reduce-scatter.5.cloned.1.call-done = bf16[1,256,1536]{2,1,0:T(8,128)(2,1)} async-done(((bf16[1,256,6144]{2,1,0:T(8,128)(2,1)}), bf16[1,256,1536]{2,1,0:T(8,128)(2,1)}) %reduce-scatter.5.cloned.1.call-update) | async-done | bytes 786448 | tf_op jit(solution)/shard_map/reduce_scatter | solution.py:86
  409.5 1.6 collective-permute-start.4
  411.1 9.3 %collective-permute-done.4 = bf16[1,128,1536]{2,1,0:T(8,128)(2,1)S(1)} collective-permute-done((bf16[1,128,1536]{2,1,0:T(8,128)(2,1)S(1)}, bf16[1,128,1536]{2,1,0:T(8,128)(2,1)S(1)}, u32[]{:S(2)}, u32[]{:S(2)}) %collective-permute-start.4) | collective-permute-done | bytes 393248 | tf_op jit(solution)/shard_map/ppermute | solution.py:18
  422.2 3.0 reduce.10
  425.5 4.2 all_to_all.45
  430.1 2.7 fusion.33
  (66 shorter events, 16.5 us)
Async XLA Ops:
  6.5 3.4 copy-start
  6.5 29.8 %copy-start.2 = (bf16[512,1536]{1,0:T(8,128)(2,1)S(1)}, bf16[512,1536]{1,0:T(8,128)(2,1)}, u32[]{:S(2)}) copy-start(bf16[512,1536]{1,0:T(8,128)(2,1)} %param.14) | copy-start | bytes 4718596
  6.5 25.4 %copy-start.3 = (s32[4,4]{1,0:T(4,128)S(1)}, s32[4,4]{1,0:T(4,128)}, u32[]{:S(2)}) copy-start(s32[4,4]{1,0:T(4,128)} %param.21) | copy-start | bytes 196
  6.5 90.2 %all-gather.3.cloned.1.call-start = ((), (), s32[]{:S(2)}) async-start(), calls=%async_computation.6 | async-start | bytes 3932160 | tf_op jit(solution)/shard_map/all_gather | solution.py:76
  41.1 11.2 %collective-permute-start = (bf16[1,128,1536]{2,1,0:T(8,128)(2,1)S(1)}, bf16[1,128,1536]{2,1,0:T(8,128)(2,1)S(1)}, u32[]{:S(2)}, u32[]{:S(2)}) collective-permute-start(bf16[1,128,1536]{2,1,0:T(8,128)(2,1)S(1)} %bitcast.184), channel_id=1, source_target_pairs={{0,8},{8,0},{16,24},{24,16},{1,9},{9,1},{17,25},{25,17},{2,10},{10... | collective-permute-start | bytes 1179656 | tf_op jit(solution)/shard_map/ppermute | solution.py:18
  53.2 112.4 %reduce-scatter.3.cloned.1.call-start = ((), (), s32[]{:S(2)}) async-start(), calls=%async_computation.7 | async-start | bytes 3932160 | tf_op jit(solution)/shard_map/reduce_scatter | solution.py:86
  121.5 218.1 %all-gather.5.cloned.1.call-start = ((), (), s32[]{:S(2)}) async-start(), calls=%async_computation.8 | async-start | bytes 3932160 | tf_op jit(solution)/shard_map/all_gather | solution.py:76
  166.7 10.9 %collective-permute-start.1 = (bf16[1,128,1536]{2,1,0:T(8,128)(2,1)S(1)}, bf16[1,128,1536]{2,1,0:T(8,128)(2,1)S(1)}, u32[]{:S(2)}, u32[]{:S(2)}) collective-permute-start(bf16[1,128,1536]{2,1,0:T(8,128)(2,1)S(1)} %slice.142), channel_id=1, source_target_pairs={{0,8},{8,0},{16,24},{24,16},{1,9},{9,1},{17,25},{25,17},{2,10},{10... | collective-permute-start | bytes 1179656 | tf_op jit(solution)/shard_map/ppermute | solution.py:18
  189.1 71.1 %collective-permute-start.2 = (bf16[512,1536]{1,0:T(8,128)(2,1)S(1)}, bf16[512,1536]{1,0:T(8,128)(2,1)S(1)}, u32[]{:S(2)}, u32[]{:S(2)}) collective-permute-start(bf16[512,1536]{1,0:T(8,128)(2,1)S(1)} %fusion.31), channel_id=1, source_target_pairs={{0,16},{8,24},{16,0},{24,8},{1,17},{9,25},{17,1},{25,9},{2,18},{10... | collective-permute-start | bytes 4718600 | tf_op jit(solution)/shard_map/ppermute | solution.py:23
  283.4 11.2 %collective-permute-start.3 = (bf16[1,128,1536]{2,1,0:T(8,128)(2,1)S(1)}, bf16[1,128,1536]{2,1,0:T(8,128)(2,1)S(1)}, u32[]{:S(2)}, u32[]{:S(2)}) collective-permute-start(bf16[1,128,1536]{2,1,0:T(8,128)(2,1)S(1)} %bitcast.186), channel_id=1, source_target_pairs={{0,8},{8,0},{16,24},{24,16},{1,9},{9,1},{17,25},{25,17},{2,10},{10... | collective-permute-start | bytes 1179656 | tf_op jit(solution)/shard_map/ppermute | solution.py:18
  295.5 113.0 %reduce-scatter.5.cloned.1.call-start = ((), (), s32[]{:S(2)}) async-start(), calls=%async_computation.9 | async-start | bytes 3932160 | tf_op jit(solution)/shard_map/reduce_scatter | solution.py:86
  409.5 10.9 %collective-permute-start.4 = (bf16[1,128,1536]{2,1,0:T(8,128)(2,1)S(1)}, bf16[1,128,1536]{2,1,0:T(8,128)(2,1)S(1)}, u32[]{:S(2)}, u32[]{:S(2)}) collective-permute-start(bf16[1,128,1536]{2,1,0:T(8,128)(2,1)S(1)} %slice.152), channel_id=1, source_target_pairs={{0,8},{8,0},{16,24},{24,16},{1,9},{9,1},{17,25},{25,17},{2,10},{10... | collective-permute-start | bytes 1179656 | tf_op jit(solution)/shard_map/ppermute | solution.py:18
  425.5 7.4 %copy-start.1 = (f32[2,1536,8]{1,2,0:T(8,128)S(1)}, f32[2,1536,8]{1,2,0:T(8,128)}, u32[]{:S(2)}) copy-start(f32[2,1536,8]{1,2,0:T(8,128)} %param.16) | copy-start | bytes 294916
Sparse Core Ops, SparseCore 0:
  53.3 43.3 all-gather.2
  121.6 43.9 reduce-scatter.2
  295.6 43.8 all-gather.4
  364.5 43.9 reduce-scatter.4
where the time goes:
time: 440 us; the launch traced here: 439 us
  waiting for transfers between devices  279 us (63%)
  matrix products  62.3 us (14%)
  blocking collectives  49.2 us (11%)
  other arithmetic  19.2 us (4%)
  between operations  13.5 us (3%)
  starting transfers between devices  8.17 us (2%)
  local copies, waits for them, and re-layouts  7.79 us (2%)
    reduce_scatter x2, waiting for transfers between devices, moe_layer(): lax.psum_scatter(partial_out.astype(jnp.bfloat16), 'tensor', scatter_dime...  87.9 us
    all_gather x2, waiting for transfers between devices, moe_layer(): feature_piece = lax.all_gather(held_rows, 'tensor', axis=2, tiled=True)  87.3 us
    ppermute x1, waiting for transfers between devices, from_behind(): return lax.ppermute(x, axis, [(i, (i + by) % peers) for i in range(peers)])  65 us
    ppermute x4, waiting for transfers between devices, swapped(): lax.ppermute(x, axis, [(i, i ^ 1 << bit) for i in range(lax.axis_size(axi...  38.9 us
    dot_general x2, matrix products, moe_layer(): jnp.einsum('snf,sfd->snd', hidden, down_w, preferred_element_type=jnp.flo...  34.9 us
    psum x2, blocking collectives, moe_layer(): lax.psum((jnp.sum(as_float * as_float, axis=1), part_logits), 'tensor')  32.9 us
    dot_general x2, matrix products, moe_layer(): jnp.einsum('snd,sdf->snf', feature_piece, up_part, preferred_element_type...  14.7 us
  transfers between devices with their start and end apart: 9, of which 9 were waited for; matrix products, arithmetic and copies ran while one was open for 1% of the time, Pallas kernels for 0%

commit v1 on v0

v1 whole, which is shorter than its diff:
```python
import functools

import jax
import jax.numpy as jnp
from jax import lax
from jax.experimental import pallas as pl
from jax.experimental.pallas import tpu as pltpu
from jax.sharding import PartitionSpec as P

D = 6144
E = 8
EXP_WIN = 2
SEQ_LEN = 128
CAP = 64
PARTS = 3

norm_eps = 1e-05
VMEM_BYTES = 48 * 1024 * 1024

bf16 = jnp.bfloat16
f32 = jnp.float32


def params():
    return pltpu.CompilerParams(vmem_limit_bytes=VMEM_BYTES)


def swapped(x, dim):
    axis, bit = dim
    return lax.ppermute(x, axis, [(i, i ^ (1 << bit)) for i in range(lax.axis_size(axis))])


def ahead(x, by, cross=False):
    sections, cores = lax.axis_size("section"), lax.axis_size("expert")
    perm = []
    for s in range(sections):
        for c in range(cores):
            there = (s + by) % sections * cores + (c ^ 1 if cross else c)
            perm.append((s * cores + c, there))
    return lax.ppermute(x, ("section", "expert"), perm)


def nt(a, b):
    return lax.dot_general(a, b, (((1,), (1,)), ((), ())), preferred_element_type=f32)


def tn(a, b):
    return lax.dot_general(a, b, (((0,), (0,)), ((), ())), preferred_element_type=f32)


def one_hot_rows(slot_row):
    rows = slot_row.shape[1]
    places = lax.broadcasted_iota(jnp.int32, (CAP, rows), 0).astype(f32)
    return places == slot_row


def prologue_kernel(core, lens, ids_ref, x_ref, slots_ref, own_ref, other_ref):
    rows = ids_ref.shape[1]
    groups_len = rows // SEQ_LEN
    place = lax.broadcasted_iota(jnp.int32, (1, rows), 1)
    me = core[0]
    named = []
    for step in range(2):
        limit = jnp.zeros((1, rows), jnp.int32)
        for q in range(groups_len):
            limit = jnp.where(place // SEQ_LEN == q, lens[step * groups_len + q], limit)
        live = place % SEQ_LEN < limit
        first = ids_ref[2 * step : 2 * step + 1, :]
        second = ids_ref[2 * step + 1 : 2 * step + 2, :]
        for which in range(2):
            expert = me if which == 0 else 1 - me
            hit = ((first == expert) | (second == expert)) & live
            named.append(jnp.where(hit, 1.0, 0.0))
    named.append(jnp.zeros((4, rows), f32))
    named = jnp.concatenate(named, axis=0)
    r = lax.broadcasted_iota(jnp.int32, (rows, rows), 0)
    c = lax.broadcasted_iota(jnp.int32, (rows, rows), 1)
    before = jnp.where(r < c, 1.0, 0.0).astype(bf16)
    earlier = jnp.dot(named.astype(bf16), before, preferred_element_type=f32)
    slots = jnp.where((named > 0.5) & (earlier < CAP), earlier, -1.0)
    slots_ref[...] = slots
    table = jnp.concatenate(
        [one_hot_rows(slots[0:1]), one_hot_rows(slots[1:2])], axis=0
    )
    table = jnp.where(table, 1.0, 0.0).astype(bf16)
    width = x_ref.shape[1] // PARTS
    for p in range(PARTS):
        got = jnp.dot(table, x_ref[:, p * width : (p + 1) * width], preferred_element_type=f32)
        got = got.astype(bf16)
        own_ref[p] = got[:CAP]
        other_ref[p] = got[CAP:]


def prologue(core, lens, ids_rows, x):
    rows, feats = x.shape
    piece = jax.ShapeDtypeStruct((PARTS, CAP, feats // PARTS), bf16)
    return pl.pallas_call(
        prologue_kernel,
        name="prologue",
        out_shape=(jax.ShapeDtypeStruct((8, rows), f32), piece, piece),
        in_specs=[
            pl.BlockSpec(memory_space=pltpu.SMEM),
            pl.BlockSpec(memory_space=pltpu.SMEM),
            pl.BlockSpec(memory_space=pltpu.VMEM),
            pl.BlockSpec(memory_space=pltpu.VMEM),
        ],
        compiler_params=params(),
    )(core, lens, ids_rows, x)


def row_stats(x_bf, gain, router_t):
    r = router_t * gain
    r1 = r.astype(bf16)
    rest = r - r1.astype(f32)
    r2 = rest.astype(bf16)
    r3 = (rest - r2.astype(f32)).astype(bf16)
    logits = (nt(r3, x_bf) + nt(r2, x_bf)) + nt(r1, x_bf)
    xf = x_bf.astype(f32)
    sq = xf * xf
    hi = sq.astype(bf16)
    lo = (sq - hi.astype(f32)).astype(bf16)
    ones = jnp.ones((8, x_bf.shape[1]), bf16)
    return logits, nt(ones, hi) + nt(ones, lo)


def stats_kernel(x_ref, gain_ref, router_ref, out_ref):
    logits, sq = row_stats(x_ref[...], gain_ref[...], router_ref[...])
    out_ref[:8] = logits
    out_ref[8:] = sq


def stats(x, gain_row, router_t):
    return pl.pallas_call(
        stats_kernel,
        name="stats",
        out_shape=jax.ShapeDtypeStruct((16, x.shape[0]), f32),
        compiler_params=params(),
    )(x, gain_row, router_t)


def row_weights(stat, first, second, me):
    inv = lax.rsqrt(stat[8:9] / D + norm_eps)
    logits = stat[:8] * inv
    names = lax.broadcasted_iota(jnp.int32, logits.shape, 0)
    a = jnp.sum(jnp.where(names == first, logits, 0.0), axis=0, keepdims=True)
    b = jnp.sum(jnp.where(names == second, logits, 0.0), axis=0, keepdims=True)
    wa = jax.nn.sigmoid(a - b)
    wb = jax.nn.sigmoid(b - a)
    out = []
    for which in range(2):
        expert = me if which == 0 else 1 - me
        out.append(jnp.where(first == expert, wa, 0.0) + jnp.where(second == expert, wb, 0.0))
    return out


def weight_table(weights, slots):
    parts = []
    for w, slot in zip(weights, slots):
        hot = one_hot_rows(slot)
        hi = w.astype(bf16).astype(f32)
        lo = w - hi
        parts.append(jnp.where(hot, hi, 0.0).astype(bf16))
        parts.append(jnp.where(hot, lo, 0.0).astype(bf16))
    return jnp.concatenate(parts, axis=0)


def stacked(own, other):
    return jnp.concatenate([own, own, other, other], axis=0)


def prepare_kernel(core, stat_ref, ids_ref, slots_ref, next_ref, x_ref, aux_ref, base_ref, mix_ref):
    me = core[0]
    w_own, w_other = row_weights(stat_ref[...], ids_ref[0:1, :], ids_ref[1:2, :], me)
    s_own, s_other = slots_ref[0:1, :], slots_ref[1:2, :]
    aux_ref[...] = jnp.concatenate(
        [w_own, w_other, s_own, s_other, jnp.zeros((4, w_own.shape[1]), f32)], axis=0
    )
    table = weight_table((w_own, w_other), (s_own, s_other))
    pick = jnp.concatenate([one_hot_rows(next_ref[2:3, :]), one_hot_rows(next_ref[3:4, :])], axis=0)
    pick = jnp.where(pick, 1.0, 0.0).astype(bf16)
    mix_ref[...] = nt(pick, table).astype(bf16)
    width = x_ref.shape[1] // PARTS
    for p in range(PARTS):
        got = jnp.dot(pick, x_ref[:, p * width : (p + 1) * width], preferred_element_type=f32)
        base_ref[p] = got.astype(bf16)


def prepare(core, stat, ids_rows, slots, next_slots, x):
    rows, feats = x.shape
    vmem = pl.BlockSpec(memory_space=pltpu.VMEM)
    return pl.pallas_call(
        prepare_kernel,
        name="prepare",
        out_shape=(
            jax.ShapeDtypeStruct((8, rows), f32),
            jax.ShapeDtypeStruct((PARTS, 2 * CAP, feats // PARTS), bf16),
            jax.ShapeDtypeStruct((2 * CAP, 4 * CAP), bf16),
        ),
        in_specs=[pl.BlockSpec(memory_space=pltpu.SMEM)] + [vmem] * 5,
        compiler_params=params(),
    )(core, stat, ids_rows, slots, next_slots, x)


def repick_kernel(mix_ref, base_ref, own_ref, other_ref, to_own_ref, to_other_ref):
    rows = jnp.dot(
        mix_ref[...], stacked(own_ref[...], other_ref[...]), preferred_element_type=f32
    )
    rows = (base_ref[...].astype(f32) + rows).astype(bf16)
    to_own_ref[...] = rows[:CAP]
    to_other_ref[...] = rows[CAP:]


def repick(mix, base, own, other):
    piece = jax.ShapeDtypeStruct(own.shape, bf16)
    return pl.pallas_call(
        repick_kernel, name="repick", out_shape=(piece, piece), compiler_params=params()
    )(mix, base, own, other)


def between_kernel(x_ref, aux_ref, own_ref, other_ref, gain_ref, router_ref, new_ref, stat_ref):
    table = weight_table((aux_ref[0:1, :], aux_ref[1:2, :]), (aux_ref[2:3, :], aux_ref[3:4, :]))
    width = x_ref.shape[1] // PARTS
    logits = None
    for p in range(PARTS):
        cols = slice(p * width, (p + 1) * width)
        mixed = tn(table, stacked(own_ref[p], other_ref[p]))
        new = (x_ref[:, cols].astype(f32) + mixed).astype(bf16)
        new_ref[:, cols] = new
        l, s = row_stats(new, gain_ref[:, cols], router_ref[:, cols])
        logits = l if logits is None else logits + l
        sq = s if p == 0 else sq + s
    stat_ref[:8] = logits
    stat_ref[8:] = sq


def between(x, aux, own, other, gain_row, router_t):
    return pl.pallas_call(
        between_kernel,
        name="between",
        out_shape=(
            jax.ShapeDtypeStruct(x.shape, bf16),
            jax.ShapeDtypeStruct((16, x.shape[0]), f32),
        ),
        compiler_params=params(),
    )(x, aux, own, other, gain_row, router_t)


def last_kernel(core, x_ref, stat_ref, ids_ref, slots_ref, own_ref, other_ref, out_ref):
    me = core[0]
    weights = row_weights(stat_ref[...], ids_ref[2:3, :], ids_ref[3:4, :], me)
    table = weight_table(weights, (slots_ref[2:3, :], slots_ref[3:4, :]))
    width = x_ref.shape[1] // PARTS
    for p in range(PARTS):
        cols = slice(p * width, (p + 1) * width)
        mixed = tn(table, stacked(own_ref[p], other_ref[p]))
        out_ref[:, cols] = (x_ref[:, cols].astype(f32) + mixed).astype(bf16)


def last(core, x, stat, ids_rows, slots, own, other):
    vmem = pl.BlockSpec(memory_space=pltpu.VMEM)
    return pl.pallas_call(
        last_kernel,
        name="last",
        out_shape=jax.ShapeDtypeStruct(x.shape, bf16),
        in_specs=[pl.BlockSpec(memory_space=pltpu.SMEM)] + [vmem] * 6,
        compiler_params=params(),
    )(core, x, stat, ids_rows, slots, own, other)


def cube_orders(slices):
    bits = slices.bit_length() - 1
    dims = [("tensor", b) for b in range(bits)] + [("section", 0)]
    n = len(dims)
    return [[dims[(i + p * max(1, n // PARTS)) % n] for i in range(n)] for p in range(PARTS)]


def gather_cube(blocks, orders):
    held = [b[None] for b in blocks]
    for k in range(len(orders[0])):
        came = [swapped(held[p], orders[p][k]) for p in range(PARTS)]
        held = [jnp.concatenate([held[p], came[p]], axis=0) for p in range(PARTS)]
    return held


def sum_cube(keep, send, orders):
    keep = [k.astype(f32) for k in keep]
    rounds = len(orders[0])
    for k in range(rounds - 1, -1, -1):
        came = [swapped(send[p], orders[p][k]).astype(f32) for p in range(PARTS)]
        total = [keep[p] + came[p] for p in range(PARTS)]
        half = total[0].shape[0] // 2
        if k > 0:
            send = [t[half:].astype(bf16) for t in total]
            keep = [t[:half] for t in total]
    return [t[0].astype(bf16) for t in total]


def block_place(order, slices, r, z):
    place = 0
    for k, (axis, bit) in enumerate(order):
        on = z if axis == "section" else (r >> bit) & 1
        place |= on << k
    return place


def block_place_traced(order, r, z):
    place = 0
    for k, (axis, bit) in enumerate(order):
        on = z if axis == "section" else (r >> bit) & 1
        place = place + (on << k)
    return place


def experts_kernel(slices, orders, me, *refs):
    ins = refs[: 2 * PARTS]
    gain_ref, gate_ref, up_ref, down_ref = refs[2 * PARTS : 2 * PARTS + 4]
    outs = refs[2 * PARTS + 4 : 4 * PARTS + 4]
    gate_acc, up_acc, sq_acc, hidden = refs[4 * PARTS + 4 :]
    step = pl.program_id(0)
    chunks = PARTS * slices
    rows = ins[0].shape[1]

    @pl.when(step == 0)
    def _():
        gate_acc[...] = jnp.zeros_like(gate_acc)
        up_acc[...] = jnp.zeros_like(up_acc)
        sq_acc[...] = jnp.zeros_like(sq_acc)

    for p in range(PARTS):

        @pl.when((step >= p * slices) & (step < (p + 1) * slices))
        def _():
            x = jnp.concatenate([ins[2 * p][0], ins[2 * p + 1][0]], axis=0).astype(f32)
            sq_acc[...] += jnp.sum(x * x, axis=1, keepdims=True)
            xg = (x * gain_ref[0]).astype(bf16)
            gate_acc[...] += jnp.dot(xg, gate_ref[...], preferred_element_type=f32)
            up_acc[...] += jnp.dot(xg, up_ref[...], preferred_element_type=f32)

    @pl.when(step == chunks - 1)
    def _():
        inv = lax.rsqrt(sq_acc[...] / D + norm_eps)
        gate = gate_acc[...] * inv
        up = up_acc[...] * inv
        hidden[...] = (gate / (1.0 + jnp.exp(-gate)) * up).astype(bf16)

    for p in range(PARTS):

        @pl.when((step >= chunks + p * slices) & (step < chunks + (p + 1) * slices))
        def _():
            r = step - (chunks + p * slices)
            out = jnp.dot(hidden[...], down_ref[...], preferred_element_type=f32).astype(bf16)
            half = outs[2 * p].shape[0]
            for z in range(2):
                place = block_place_traced(orders[p], r, z)
                block = out[z * rows : (z + 1) * rows]
                if orders[p][-1][0] == "section":
                    outs[2 * p + z][place - z * half] = block
                else:

                    @pl.when(place < half)
                    def _():
                        outs[2 * p][place] = block

                    @pl.when(place >= half)
                    def _():
                        outs[2 * p + 1][place - half] = block


def experts(me, held, gain_all, gate_w, up_w, down_w, orders):
    blocks, rows, width = held[0].shape
    slices = blocks // 2
    chunks = PARTS * slices
    hidden_count = gate_w.shape[1]

    def part_and_slice(chunk):
        return chunk // slices, chunk % slices

    def row_map(p, z):
        def index(step, me):
            r = jnp.clip(step - p * slices, 0, slices - 1)
            return (block_place_traced(orders[p], r, z), 0, 0)

        return index

    def weight_place(chunk, me):
        p, r = part_and_slice(chunk)
        return (me[0] ^ r) * PARTS + p

    def in_map(step, me):
        return (weight_place(jnp.minimum(step, chunks - 1), me), 0)

    def gain_map(step, me):
        return (weight_place(jnp.minimum(step, chunks - 1), me), 0, 0)

    def down_map(step, me):
        return (0, weight_place(jnp.maximum(step - chunks, 0), me))

    in_specs = []
    operands = []
    for p in range(PARTS):
        for z in range(2):
            in_specs.append(pl.BlockSpec((1, rows, width), row_map(p, z)))
            operands.append(held[p])
    in_specs += [
        pl.BlockSpec((1, 1, width), gain_map),
        pl.BlockSpec((width, hidden_count), in_map),
        pl.BlockSpec((width, hidden_count), in_map),
        pl.BlockSpec((hidden_count, width), down_map),
    ]
    out_shape = [jax.ShapeDtypeStruct((blocks // 2, rows, width), bf16)] * (2 * PARTS)
    out_specs = [
        pl.BlockSpec((blocks // 2, rows, width), lambda step, me: (0, 0, 0))
    ] * (2 * PARTS)
    flops = 2 * 2 * rows * D * hidden_count * 3
    outs = pl.pallas_call(
        functools.partial(experts_kernel, slices, orders),
        name="experts",
        out_shape=out_shape,
        grid_spec=pltpu.PrefetchScalarGridSpec(
            num_scalar_prefetch=1,
            grid=(2 * chunks,),
            in_specs=in_specs,
            out_specs=out_specs,
            scratch_shapes=[
                pltpu.VMEM((2 * rows, hidden_count), f32),
                pltpu.VMEM((2 * rows, hidden_count), f32),
                pltpu.VMEM((2 * rows, 1), f32),
                pltpu.VMEM((2 * rows, hidden_count), bf16),
            ],
        ),
        compiler_params=params(),
        cost_estimate=pl.CostEstimate(
            flops=flops,
            bytes_accessed=3 * D * hidden_count * 2 + 4 * rows * D * 2,
            transcendentals=2 * rows * hidden_count,
        ),
    )(me, *operands, gain_all, gate_w, up_w, down_w)
    return outs[0::2], outs[1::2]


def tensor_sum(stat):
    for b in range(lax.axis_size("tensor").bit_length() - 1):
        stat = stat + swapped(stat, ("tensor", b))
    return stat


def on_device(tokens, norm_gain, router, w_gate, w_up, w_down, expert_ids, lengths):
    sections = lax.axis_size("section")
    slices = lax.axis_size("tensor")
    section = lax.axis_index("section")
    core = lax.axis_index("expert").astype(jnp.int32)[None]
    me = lax.axis_index("tensor").astype(jnp.int32)[None]
    layer = section // 2
    rows, feats = tokens.shape
    width = feats // PARTS
    across = ("expert", 0)

    gain_row = lax.dynamic_index_in_dim(norm_gain, layer, 0, keepdims=True)
    router_t = lax.dynamic_index_in_dim(router, layer, 0, keepdims=False).T
    ids_rows = jnp.transpose(expert_ids, (0, 2, 1)).reshape(4, rows)
    lens = jnp.concatenate(
        [
            lax.dynamic_index_in_dim(lengths, section, 0, keepdims=False),
            lax.dynamic_index_in_dim(lengths, (section - 2) % sections, 0, keepdims=False),
        ]
    )
    gain_all = lax.all_gather(gain_row[0], "tensor", axis=0, tiled=True)
    gain_all = gain_all.reshape(slices * PARTS, 1, width)
    orders = cube_orders(slices)
    gate_w, up_w, down_w = w_gate[0, 0], w_up[0, 0], w_down[0, 0]

    slots, own, other = prologue(core, lens, ids_rows, tokens)
    block = jnp.concatenate([own, swapped(other, across)], axis=1)
    held = gather_cube([block[p] for p in range(PARTS)], orders)

    far_tokens = ahead(tokens, 2)
    next_slots = ahead(slots, -2)
    stat = tensor_sum(stats(tokens, gain_row, router_t))
    aux, base, mix = prepare(core, stat, ids_rows, slots, next_slots, tokens)
    far_aux = ahead(aux, 2)

    keep, send = experts(me, held, gain_all, gate_w, up_w, down_w, orders)
    summed = sum_cube(keep, send, orders)

    mine = [s[:CAP] for s in summed]
    theirs = [swapped(s[CAP:], across) for s in summed]
    blocks = []
    for p in range(PARTS):
        to_own, to_other = repick(mix, base[p], mine[p], theirs[p])
        blocks.append(jnp.concatenate([ahead(to_own, 2), ahead(to_other, 2, True)], axis=0))
    held = gather_cube(blocks, orders)

    moved = ahead(jnp.stack([jnp.stack(mine), jnp.stack(theirs)]), 2)
    state, stat = between(far_tokens, far_aux, moved[0], moved[1], gain_row, router_t)
    stat = tensor_sum(stat)

    keep, send = experts(me, held, gain_all, gate_w, up_w, down_w, orders)
    summed = sum_cube(keep, send, orders)
    mine = jnp.stack([s[:CAP] for s in summed])
    theirs = swapped(jnp.stack([s[CAP:] for s in summed]), across)
    return last(core, state, stat, ids_rows, slots, mine, theirs)


def solution(mesh):
    in_specs = (
        P(("section", "expert"), "tensor"),
        P(None, "tensor"),
        P(None, "tensor", None),
        P("section", "expert", None, "tensor"),
        P("section", "expert", None, "tensor"),
        P("section", "expert", "tensor", None),
        P(None, ("section", "expert"), None),
        P(None, "expert"),
    )
    out_specs = P(("section", "expert"), "tensor")
    return jax.shard_map(
        on_device, mesh=mesh, in_specs=in_specs, out_specs=out_specs, check_vma=False
    )
```

time: 440 us -> 299 us (0.68)
  waiting for transfers between devices: 279 us -> 143 us
  Pallas kernels: 0 us -> 64.1 us
  matrix products: 62.3 us -> 0 us
  starting transfers between devices: 8.17 us -> 67.9 us
  blocking collectives: 49.2 us -> 10.2 us
  between operations: 13.5 us -> 0.64 us
  other arithmetic: 19.2 us -> 7.98 us
    ppermute x4 -> x45, waiting for transfers between devices: 38.9 us -> 134 us  [swapped(): lax.ppermute(x, axis, [(i, i ^ 1 << bit) for i in range(lax.axis_size(axi...]
    reduce_scatter x2 -> x0, waiting for transfers between devices: 87.9 us -> none  [moe_layer(): lax.psum_scatter(partial_out.astype(jnp.bfloat16), 'tensor', scatter_dime...]
    all_gather x2 -> x0, waiting for transfers between devices: 87.3 us -> none  [moe_layer(): feature_piece = lax.all_gather(held_rows, 'tensor', axis=2, tiled=True)]
    pallas_call x0 -> x10, Pallas kernels: none -> 64.1 us  [the longest x2 55.3 us: experts(): pl.pallas_call(functools.partial(experts_kernel, slices, orders), name='e...]
    dot_general x10 -> x0, matrix products: 62.3 us -> none  [the longest x2 34.9 us: moe_layer(): jnp.einsum('snf,sfd->snd', hidden, down_w, preferred_element_type=jnp.flo...]
    ppermute x1 -> x10, waiting for transfers between devices: 65 us -> 8.9 us  [ahead(): return lax.ppermute(x, ('section', 'expert'), perm)]
    ppermute x4 -> x45, starting transfers between devices: 5.17 us -> 48.8 us  [swapped(): lax.ppermute(x, axis, [(i, i ^ 1 << bit) for i in range(lax.axis_size(axi...]
    psum x2 -> x0, blocking collectives: 32.9 us -> none  [moe_layer(): lax.psum((jnp.sum(as_float * as_float, axis=1), part_logits), 'tensor')]
  transfers between devices with their start and end apart: 9 -> 55, of which waited for: 9 -> 28; matrix products, arithmetic and copies ran while one was open for 1% -> 2% of each run, Pallas kernels for 0% -> 2%
where the time goes in v1:
time: 299 us; the launch traced here: 298 us
  waiting for transfers between devices  143 us (48%)
  starting transfers between devices  67.9 us (23%)
  Pallas kernels  64.1 us (21%)
  blocking collectives  10.2 us (3%)
  other arithmetic  7.98 us (3%)
  local copies, waits for them, and re-layouts  3.46 us (1%)
    ppermute x45, waiting for transfers between devices, swapped(): lax.ppermute(x, axis, [(i, i ^ 1 << bit) for i in range(lax.axis_size(axi...  134 us
    pallas_call x2, Pallas kernels, experts(): pl.pallas_call(functools.partial(experts_kernel, slices, orders), name='e...  55.3 us
    ppermute x45, starting transfers between devices, swapped(): lax.ppermute(x, axis, [(i, i ^ 1 << bit) for i in range(lax.axis_size(axi...  48.8 us
    ppermute x10, starting transfers between devices, ahead(): return lax.ppermute(x, ('section', 'expert'), perm)  19.2 us
    all_gather x1, blocking collectives, on_device(): gain_all = lax.all_gather(gain_row[0], 'tensor', axis=0, tiled=True)  10.2 us
    ppermute x10, waiting for transfers between devices, ahead(): return lax.ppermute(x, ('section', 'expert'), perm)  8.9 us
    concatenate x18, other arithmetic, gather_cube(): held = [jnp.concatenate([held[p], came[p]], axis=0) for p in range(PARTS)]  6.17 us
  transfers between devices with their start and end apart: 55, of which 28 were waited for; matrix products, arithmetic and copies ran while one was open for 2% of the time, Pallas kernels for 2%

profile of v1, /device:TPU:0, one launch (start us, length us, event | category | flops | bytes accessed | tf_op | source)
XLA Modules:
  0.0 297.6 jit_solution(13438374345391511264)
XLA Ops:
  5.7 3.0 %collective-permute-start.12 = (bf16[1,128,512]{2,1,0:T(8,128)(2,1)S(1)}, bf16[1,128,512]{2,1,0:T(8,128)(2,1)S(1)}, u32[]{:S(2)}, u32[]{:S(2)}) collective-permute-start(bf16[1,128,512]{2,1,0:T(8,128)(2,1)S(1)} %get-tuple-element.62), channel_id=1, source_target_pairs={{0,8},{8,0},{16,24},{24,16},{1,9},{9,1},{17,25},{25,17},{2,10},{10... | collective-permute-start | bytes 393224 | tf_op jit(solution)/shard_map/ppermute | solution.py:30
  10.2 2.3 collective-permute-done.12
  16.5 6.8 %collective-permute-done.6 = bf16[1,128,512]{2,1,0:T(8,128)(2,1)S(1)} collective-permute-done((bf16[1,128,512]{2,1,0:T(8,128)(2,1)S(1)}, bf16[1,128,512]{2,1,0:T(8,128)(2,1)S(1)}, u32[]{:S(2)}, u32[]{:S(2)}) %collective-permute-start.6) | collective-permute-done | bytes 131104 | tf_op jit(solution)/shard_map/ppermute | solution.py:30
  27.0 5.6 %collective-permute-done.7 = bf16[2,128,512]{2,1,0:T(8,128)(2,1)S(1)} collective-permute-done((bf16[2,128,512]{2,1,0:T(8,128)(2,1)S(1)}, bf16[2,128,512]{2,1,0:T(8,128)(2,1)S(1)}, u32[]{:S(2)}, u32[]{:S(2)}) %collective-permute-start.7) | collective-permute-done | bytes 262176 | tf_op jit(solution)/shard_map/ppermute | solution.py:30
  34.2 10.2 %all-gather = f32[1,6144]{1,0:T(1,128)S(1)} all-gather(f32[1,1536]{1,0:T(1,128)S(1)} %constant_dynamic-slice_fusion.2.gain_ref), channel_id=2, replica_groups=mesh['section'=4,'expert'=2,'tensor'=4] {'tensor'}, dimensions={1}, use_global_device_ids=true | all-gather | bytes 30720 | tf_op jit(solution)/shard_map/all_gather | solution.py:467
  48.8 27.6 %experts.2 = (bf16[4,128,512]{2,1,0:T(8,128)(2,1)S(1)}, bf16[4,128,512]{2,1,0:T(8,128)(2,1)S(1)}, bf16[4,128,512]{2,1,0:T(8,128)(2,1)S(1)}, bf16[4,128,512]{2,1,...) custom-call(s32[1]{0:T(128)} %bitcast.6.me, ...), custom_call_target="tpu_custom_call" | custom-call | flops 9663676416 | bytes 44040192 | tf_op jit(solution)/shard_map/experts/pallas_call | solution.py:415
  78.1 2.2 stats.1
  80.8 3.4 %collective-permute-done.1 = f32[16,512]{1,0:T(8,128)S(1)} collective-permute-done((f32[16,512]{1,0:T(8,128)S(1)}, f32[16,512]{1,0:T(8,128)S(1)}, u32[]{:S(2)}, u32[]{:S(2)}) %collective-permute-start.1) | collective-permute-done | bytes 32800 | tf_op jit(solution)/shard_map/ppermute | solution.py:30
  84.7 3.0 collective-permute-start.3
  93.4 5.5 %collective-permute-done.18 = bf16[4,128,512]{2,1,0:T(8,128)(2,1)S(1)} collective-permute-done((bf16[4,128,512]{2,1,0:T(8,128)(2,1)S(1)}, bf16[4,128,512]{2,1,0:T(8,128)(2,1)S(1)}, u32[]{:S(2)}, u32[]{:S(2)}) %collective-permute-start.18) | collective-permute-done | bytes 524320 | tf_op jit(solution)/shard_map/ppermute | solution.py:30
  100.8 2.7 collective-permute-done.15
  107.4 2.7 collective-permute-done.16
  112.1 3.1 %collective-permute-done.17 = bf16[1,128,512]{2,1,0:T(8,128)(2,1)S(1)} collective-permute-done((bf16[1,128,512]{2,1,0:T(8,128)(2,1)S(1)}, bf16[1,128,512]{2,1,0:T(8,128)(2,1)S(1)}, u32[]{:S(2)}, u32[]{:S(2)}) %collective-permute-start.17) | collective-permute-done | bytes 131104 | tf_op jit(solution)/shard_map/ppermute | solution.py:30
  115.5 2.2 collective-permute-start.40
  122.1 3.6 %collective-permute-done.41 = bf16[64,512]{1,0:T(8,128)(2,1)S(1)} collective-permute-done((bf16[64,512]{1,0:T(8,128)(2,1)S(1)}, bf16[64,512]{1,0:T(8,128)(2,1)S(1)}, u32[]{:S(2)}, u32[]{:S(2)}) %collective-permute-start.41) | collective-permute-done | bytes 65568 | tf_op jit(solution)/shard_map/ppermute | solution.py:40
  125.7 2.4 collective-permute-start.42
  134.7 3.2 %collective-permute-done.31 = bf16[64,512]{1,0:T(8,128)(2,1)S(1)} collective-permute-done((bf16[64,512]{1,0:T(8,128)(2,1)S(1)}, bf16[64,512]{1,0:T(8,128)(2,1)S(1)}, u32[]{:S(2)}, u32[]{:S(2)}) %collective-permute-start.31) | collective-permute-done | bytes 65568 | tf_op jit(solution)/shard_map/ppermute | solution.py:40
  139.3 5.2 %collective-permute-done.32 = bf16[1,128,512]{2,1,0:T(8,128)(2,1)S(1)} collective-permute-done((bf16[1,128,512]{2,1,0:T(8,128)(2,1)S(1)}, bf16[1,128,512]{2,1,0:T(8,128)(2,1)S(1)}, u32[]{:S(2)}, u32[]{:S(2)}) %collective-permute-start.32) | collective-permute-done | bytes 131104 | tf_op jit(solution)/shard_map/ppermute | solution.py:30
  148.3 5.6 %collective-permute-done.33 = bf16[2,128,512]{2,1,0:T(8,128)(2,1)S(1)} collective-permute-done((bf16[2,128,512]{2,1,0:T(8,128)(2,1)S(1)}, bf16[2,128,512]{2,1,0:T(8,128)(2,1)S(1)}, u32[]{:S(2)}, u32[]{:S(2)}) %collective-permute-start.33) | collective-permute-done | bytes 262176 | tf_op jit(solution)/shard_map/ppermute | solution.py:30
  154.0 9.2 %collective-permute-done.44 = bf16[4,128,512]{2,1,0:T(8,128)(2,1)S(1)} collective-permute-done((bf16[4,128,512]{2,1,0:T(8,128)(2,1)S(1)}, bf16[4,128,512]{2,1,0:T(8,128)(2,1)S(1)}, u32[]{:S(2)}, u32[]{:S(2)}) %collective-permute-start.44) | collective-permute-done | bytes 524320 | tf_op jit(solution)/shard_map/ppermute | solution.py:30
  164.5 27.7 %experts.3 = (bf16[4,128,512]{2,1,0:T(8,128)(2,1)S(1)}, bf16[4,128,512]{2,1,0:T(8,128)(2,1)S(1)}, bf16[4,128,512]{2,1,0:T(8,128)(2,1)S(1)}, bf16[4,128,512]{2,1,...) custom-call(s32[1]{0:T(128)} %bitcast.6.me, ...), custom_call_target="tpu_custom_call" | custom-call | flops 9663676416 | bytes 44040192 | tf_op jit(solution)/shard_map/experts/pallas_call | solution.py:415
  192.3 5.8 %collective-permute-start = (bf16[512,1536]{1,0:T(8,128)(2,1)S(1)}, bf16[512,1536]{1,0:T(8,128)(2,1)S(1)}, u32[]{:S(2)}, u32[]{:S(2)}) collective-permute-start(bf16[512,1536]{1,0:T(8,128)(2,1)S(1)} %copy-done.3), channel_id=1, source_target_pairs={{0,16},{4,20},{8,24},{12,28},{16,0},{20,4},{24,8},{28,12},{1,17},{... | collective-permute-start | bytes 4718600 | tf_op jit(solution)/shard_map/ppermute | solution.py:40
  199.5 3.0 collective-permute-start.27
  202.4 13.0 %collective-permute-done.45 = bf16[4,128,512]{2,1,0:T(8,128)(2,1)S(1)} collective-permute-done((bf16[4,128,512]{2,1,0:T(8,128)(2,1)S(1)}, bf16[4,128,512]{2,1,0:T(8,128)(2,1)S(1)}, u32[]{:S(2)}, u32[]{:S(2)}) %collective-permute-start.45) | collective-permute-done | bytes 524320 | tf_op jit(solution)/shard_map/ppermute | solution.py:30
  217.9 11.4 %collective-permute-done.51 = bf16[4,128,512]{2,1,0:T(8,128)(2,1)S(1)} collective-permute-done((bf16[4,128,512]{2,1,0:T(8,128)(2,1)S(1)}, bf16[4,128,512]{2,1,0:T(8,128)(2,1)S(1)}, u32[]{:S(2)}, u32[]{:S(2)}) %collective-permute-start.51) | collective-permute-done | bytes 524320 | tf_op jit(solution)/shard_map/ppermute | solution.py:30
  229.5 2.6 collective-permute-done.46
  233.4 16.9 %collective-permute-done.49 = bf16[2,128,512]{2,1,0:T(8,128)(2,1)S(1)} collective-permute-done((bf16[2,128,512]{2,1,0:T(8,128)(2,1)S(1)}, bf16[2,128,512]{2,1,0:T(8,128)(2,1)S(1)}, u32[]{:S(2)}, u32[]{:S(2)}) %collective-permute-start.49) | collective-permute-done | bytes 262176 | tf_op jit(solution)/shard_map/ppermute | solution.py:30
  255.3 2.5 collective-permute-start.53
  257.9 27.1 %collective-permute-done.53 = bf16[1,128,512]{2,1,0:T(8,128)(2,1)S(1)} collective-permute-done((bf16[1,128,512]{2,1,0:T(8,128)(2,1)S(1)}, bf16[1,128,512]{2,1,0:T(8,128)(2,1)S(1)}, u32[]{:S(2)}, u32[]{:S(2)}) %collective-permute-start.53) | collective-permute-done | bytes 131104 | tf_op jit(solution)/shard_map/ppermute | solution.py:30
  285.2 2.7 between.1
  289.2 2.7 collective-permute-done.28
  292.4 3.4 %collective-permute-done.29 = f32[16,512]{1,0:T(8,128)S(1)} collective-permute-done((f32[16,512]{1,0:T(8,128)S(1)}, f32[16,512]{1,0:T(8,128)S(1)}, u32[]{:S(2)}, u32[]{:S(2)}) %collective-permute-start.29) | collective-permute-done | bytes 32800 | tf_op jit(solution)/shard_map/ppermute | solution.py:30
  (175 shorter events, 68.8 us)
Async XLA Ops:
  12.5 12.2 %collective-permute-start.13 = (bf16[2,128,512]{2,1,0:T(8,128)(2,1)S(1)}, bf16[2,128,512]{2,1,0:T(8,128)(2,1)S(1)}, u32[]{:S(2)}, u32[]{:S(2)}) collective-permute-start(bf16[2,128,512]{2,1,0:T(8,128)(2,1)S(1)} %pad_maximum_fusion.15), channel_id=1, source_target_pairs={{0,1},{1,0},{2,3},{3,2},{4,5},{5,4},{6,7},{7,6},{8,9},{9,8},{10,11... | collective-permute-start | bytes 786440 | tf_op jit(solution)/shard_map/ppermute | solution.py:30
  14.3 9.0 %collective-permute-start.6 = (bf16[1,128,512]{2,1,0:T(8,128)(2,1)S(1)}, bf16[1,128,512]{2,1,0:T(8,128)(2,1)S(1)}, u32[]{:S(2)}, u32[]{:S(2)}) collective-permute-start(bf16[1,128,512]{2,1,0:T(8,128)(2,1)S(1)} %get-tuple-element.64), channel_id=1, source_target_pairs={{0,1},{1,0},{2,3},{3,2},{4,5},{5,4},{6,7},{7,6},{8,9},{9,8},{10,11... | collective-permute-start | bytes 393224 | tf_op jit(solution)/shard_map/ppermute | solution.py:30
  14.7 10.8 %collective-permute-start.10 = (bf16[2,128,512]{2,1,0:T(8,128)(2,1)S(1)}, bf16[2,128,512]{2,1,0:T(8,128)(2,1)S(1)}, u32[]{:S(2)}, u32[]{:S(2)}) collective-permute-start(bf16[2,128,512]{2,1,0:T(8,128)(2,1)S(1)} %pad_maximum_fusion.14), channel_id=1, source_target_pairs={{0,8},{8,0},{16,24},{24,16},{1,9},{9,1},{17,25},{25,17},{2,10},{10... | collective-permute-start | bytes 786440 | tf_op jit(solution)/shard_map/ppermute | solution.py:30
  23.3 9.3 %collective-permute-start.7 = (bf16[2,128,512]{2,1,0:T(8,128)(2,1)S(1)}, bf16[2,128,512]{2,1,0:T(8,128)(2,1)S(1)}, u32[]{:S(2)}, u32[]{:S(2)}) collective-permute-start(bf16[2,128,512]{2,1,0:T(8,128)(2,1)S(1)} %pad_maximum_fusion.13), channel_id=1, source_target_pairs={{0,2},{1,3},{2,0},{3,1},{4,6},{5,7},{6,4},{7,5},{8,10},{9,11},{10,... | collective-permute-start | bytes 786440 | tf_op jit(solution)/shard_map/ppermute | solution.py:30
  24.8 19.6 %collective-permute-start.14 = (bf16[4,128,512]{2,1,0:T(8,128)(2,1)S(1)}, bf16[4,128,512]{2,1,0:T(8,128)(2,1)}, u32[]{:S(2)}, u32[]{:S(2)}) collective-permute-start(bf16[4,128,512]{2,1,0:T(8,128)(2,1)S(1)} %pad_maximum_fusion.8), channel_id=1, source_target_pairs={{0,2},{1,3},{2,0},{3,1},{4,6},{5,7},{6,4},{7,5},{8,10},{9,11},{10,... | collective-permute-start | bytes 1572872 | tf_op jit(solution)/shard_map/ppermute | solution.py:30
  25.6 21.0 %collective-permute-start.11 = (bf16[4,128,512]{2,1,0:T(8,128)(2,1)S(1)}, bf16[4,128,512]{2,1,0:T(8,128)(2,1)}, u32[]{:S(2)}, u32[]{:S(2)}) collective-permute-start(bf16[4,128,512]{2,1,0:T(8,128)(2,1)S(1)} %pad_maximum_fusion.7), channel_id=1, source_target_pairs={{0,1},{1,0},{2,3},{3,2},{4,5},{5,4},{6,7},{7,6},{8,9},{9,8},{10,11... | collective-permute-start | bytes 1572872 | tf_op jit(solution)/shard_map/ppermute | solution.py:30
  32.7 15.0 %collective-permute-start.8 = (bf16[4,128,512]{2,1,0:T(8,128)(2,1)S(1)}, bf16[4,128,512]{2,1,0:T(8,128)(2,1)}, u32[]{:S(2)}, u32[]{:S(2)}) collective-permute-start(bf16[4,128,512]{2,1,0:T(8,128)(2,1)S(1)} %pad_maximum_fusion.6), channel_id=1, source_target_pairs={{0,8},{8,0},{16,24},{24,16},{1,9},{9,1},{17,25},{25,17},{2,10},{10... | collective-permute-start | bytes 1572872 | tf_op jit(solution)/shard_map/ppermute | solution.py:30
  76.5 15.2 %collective-permute-start.21 = (bf16[4,128,512]{2,1,0:T(8,128)(2,1)S(1)}, bf16[4,128,512]{2,1,0:T(8,128)(2,1)S(1)}, u32[]{:S(2)}, u32[]{:S(2)}) collective-permute-start(bf16[4,128,512]{2,1,0:T(8,128)(2,1)S(1)} %get-tuple-element.40), channel_id=1, source_target_pairs={{0,2},{1,3},{2,0},{3,1},{4,6},{5,7},{6,4},{7,5},{8,10},{9,11},{10,... | collective-permute-start | bytes 1572872 | tf_op jit(solution)/shard_map/ppermute | solution.py:30
  87.6 11.3 %collective-permute-start.18 = (bf16[4,128,512]{2,1,0:T(8,128)(2,1)S(1)}, bf16[4,128,512]{2,1,0:T(8,128)(2,1)S(1)}, u32[]{:S(2)}, u32[]{:S(2)}) collective-permute-start(bf16[4,128,512]{2,1,0:T(8,128)(2,1)S(1)} %get-tuple-element.38), channel_id=1, source_target_pairs={{0,1},{1,0},{2,3},{3,2},{4,5},{5,4},{6,7},{7,6},{8,9},{9,8},{10,11... | collective-permute-start | bytes 1572872 | tf_op jit(solution)/shard_map/ppermute | solution.py:30
  90.0 13.5 %collective-permute-start.15 = (bf16[4,128,512]{2,1,0:T(8,128)(2,1)S(1)}, bf16[4,128,512]{2,1,0:T(8,128)(2,1)S(1)}, u32[]{:S(2)}, u32[]{:S(2)}) collective-permute-start(bf16[4,128,512]{2,1,0:T(8,128)(2,1)S(1)} %get-tuple-element.36), channel_id=1, source_target_pairs={{0,8},{8,0},{16,24},{24,16},{1,9},{9,1},{17,25},{25,17},{2,10},{10... | collective-permute-start | bytes 1572872 | tf_op jit(solution)/shard_map/ppermute | solution.py:30
  91.9 12.9 %collective-permute-start.22 = (bf16[2,128,512]{2,1,0:T(8,128)(2,1)S(1)}, bf16[2,128,512]{2,1,0:T(8,128)(2,1)S(1)}, u32[]{:S(2)}, u32[]{:S(2)}) collective-permute-start(bf16[2,128,512]{2,1,0:T(8,128)(2,1)S(1)} %slice.309), channel_id=1, source_target_pairs={{0,1},{1,0},{2,3},{3,2},{4,5},{5,4},{6,7},{7,6},{8,9},{9,8},{10,11... | collective-permute-start | bytes 786440 | tf_op jit(solution)/shard_map/ppermute | solution.py:30
  117.6 8.0 %collective-permute-start.41 = (bf16[64,512]{1,0:T(8,128)(2,1)S(1)}, bf16[64,512]{1,0:T(8,128)(2,1)S(1)}, u32[]{:S(2)}, u32[]{:S(2)}) collective-permute-start(bf16[64,512]{1,0:T(8,128)(2,1)S(1)} %get-tuple-element.50), channel_id=1, source_target_pairs={{0,20},{4,16},{8,28},{12,24},{16,4},{20,0},{24,12},{28,8},{1,21},{... | collective-permute-start | bytes 196616 | tf_op jit(solution)/shard_map/ppermute | solution.py:40
  117.7 10.4 %collective-permute-start.24 = (bf16[64,512]{1,0:T(8,128)(2,1)S(1)}, bf16[64,512]{1,0:T(8,128)(2,1)S(1)}, u32[]{:S(2)}, u32[]{:S(2)}) collective-permute-start(bf16[64,512]{1,0:T(8,128)(2,1)S(1)} %get-tuple-element.78), channel_id=1, source_target_pairs={{0,4},{4,0},{1,5},{5,1},{2,6},{6,2},{3,7},{7,3},{8,12},{12,8},{9,1... | collective-permute-start | bytes 196616 | tf_op jit(solution)/shard_map/ppermute | solution.py:30
  118.9 12.4 %collective-permute-start.35 = (bf16[64,512]{1,0:T(8,128)(2,1)S(1)}, bf16[64,512]{1,0:T(8,128)(2,1)S(1)}, u32[]{:S(2)}, u32[]{:S(2)}) collective-permute-start(bf16[64,512]{1,0:T(8,128)(2,1)S(1)} %get-tuple-element.47), channel_id=1, source_target_pairs={{0,16},{4,20},{8,24},{12,28},{16,0},{20,4},{24,8},{28,12},{1,17},{... | collective-permute-start | bytes 196616 | tf_op jit(solution)/shard_map/ppermute | solution.py:40
  121.0 10.2 %collective-permute-start.36 = (bf16[64,512]{1,0:T(8,128)(2,1)S(1)}, bf16[64,512]{1,0:T(8,128)(2,1)S(1)}, u32[]{:S(2)}, u32[]{:S(2)}) collective-permute-start(bf16[64,512]{1,0:T(8,128)(2,1)S(1)} %get-tuple-element.48), channel_id=1, source_target_pairs={{0,20},{4,16},{8,28},{12,24},{16,4},{20,0},{24,12},{28,8},{1,21},{... | collective-permute-start | bytes 196616 | tf_op jit(solution)/shard_map/ppermute | solution.py:40
  133.5 12.8 %collective-permute-start.43 = (bf16[2,128,512]{2,1,0:T(8,128)(2,1)S(1)}, bf16[2,128,512]{2,1,0:T(8,128)(2,1)S(1)}, u32[]{:S(2)}, u32[]{:S(2)}) collective-permute-start(bf16[2,128,512]{2,1,0:T(8,128)(2,1)S(1)} %pad_maximum_fusion.18), channel_id=1, source_target_pairs={{0,1},{1,0},{2,3},{3,2},{4,5},{5,4},{6,7},{7,6},{8,9},{9,8},{10,11... | collective-permute-start | bytes 786440 | tf_op jit(solution)/shard_map/ppermute | solution.py:30
  139.2 8.1 %collective-permute-start.38 = (bf16[2,128,512]{2,1,0:T(8,128)(2,1)S(1)}, bf16[2,128,512]{2,1,0:T(8,128)(2,1)S(1)}, u32[]{:S(2)}, u32[]{:S(2)}) collective-permute-start(bf16[2,128,512]{2,1,0:T(8,128)(2,1)S(1)} %pad_maximum_fusion.17), channel_id=1, source_target_pairs={{0,8},{8,0},{16,24},{24,16},{1,9},{9,1},{17,25},{25,17},{2,10},{10... | collective-permute-start | bytes 786440 | tf_op jit(solution)/shard_map/ppermute | solution.py:30
  144.6 9.3 %collective-permute-start.33 = (bf16[2,128,512]{2,1,0:T(8,128)(2,1)S(1)}, bf16[2,128,512]{2,1,0:T(8,128)(2,1)S(1)}, u32[]{:S(2)}, u32[]{:S(2)}) collective-permute-start(bf16[2,128,512]{2,1,0:T(8,128)(2,1)S(1)} %pad_maximum_fusion.16), channel_id=1, source_target_pairs={{0,2},{1,3},{2,0},{3,1},{4,6},{5,7},{6,4},{7,5},{8,10},{9,11},{10,... | collective-permute-start | bytes 786440 | tf_op jit(solution)/shard_map/ppermute | solution.py:30
  146.3 16.9 %collective-permute-start.44 = (bf16[4,128,512]{2,1,0:T(8,128)(2,1)S(1)}, bf16[4,128,512]{2,1,0:T(8,128)(2,1)S(1)}, u32[]{:S(2)}, u32[]{:S(2)}) collective-permute-start(bf16[4,128,512]{2,1,0:T(8,128)(2,1)S(1)} %pad_maximum_fusion.11), channel_id=1, source_target_pairs={{0,2},{1,3},{2,0},{3,1},{4,6},{5,7},{6,4},{7,5},{8,10},{9,11},{10,... | collective-permute-start | bytes 1572872 | tf_op jit(solution)/shard_map/ppermute | solution.py:30
  147.4 16.9 %collective-permute-start.39 = (bf16[4,128,512]{2,1,0:T(8,128)(2,1)S(1)}, bf16[4,128,512]{2,1,0:T(8,128)(2,1)S(1)}, u32[]{:S(2)}, u32[]{:S(2)}) collective-permute-start(bf16[4,128,512]{2,1,0:T(8,128)(2,1)S(1)} %pad_maximum_fusion.10), channel_id=1, source_target_pairs={{0,1},{1,0},{2,3},{3,2},{4,5},{5,4},{6,7},{7,6},{8,9},{9,8},{10,11... | collective-permute-start | bytes 1572872 | tf_op jit(solution)/shard_map/ppermute | solution.py:30
  153.9 10.5 %collective-permute-start.34 = (bf16[4,128,512]{2,1,0:T(8,128)(2,1)S(1)}, bf16[4,128,512]{2,1,0:T(8,128)(2,1)S(1)}, u32[]{:S(2)}, u32[]{:S(2)}) collective-permute-start(bf16[4,128,512]{2,1,0:T(8,128)(2,1)S(1)} %pad_maximum_fusion.9), channel_id=1, source_target_pairs={{0,8},{8,0},{16,24},{24,16},{1,9},{9,1},{17,25},{25,17},{2,10},{10... | collective-permute-start | bytes 1572872 | tf_op jit(solution)/shard_map/ppermute | solution.py:30
  192.2 23.1 %collective-permute-start.45 = (bf16[4,128,512]{2,1,0:T(8,128)(2,1)S(1)}, bf16[4,128,512]{2,1,0:T(8,128)(2,1)S(1)}, u32[]{:S(2)}, u32[]{:S(2)}) collective-permute-start(bf16[4,128,512]{2,1,0:T(8,128)(2,1)S(1)} %get-tuple-element.52), channel_id=1, source_target_pairs={{0,8},{8,0},{16,24},{24,16},{1,9},{9,1},{17,25},{25,17},{2,10},{10... | collective-permute-start | bytes 1572872 | tf_op jit(solution)/shard_map/ppermute | solution.py:30
  192.3 92.9 %collective-permute-start = (bf16[512,1536]{1,0:T(8,128)(2,1)S(1)}, bf16[512,1536]{1,0:T(8,128)(2,1)S(1)}, u32[]{:S(2)}, u32[]{:S(2)}) collective-permute-start(bf16[512,1536]{1,0:T(8,128)(2,1)S(1)} %copy-done.3), channel_id=1, source_target_pairs={{0,16},{4,20},{8,24},{12,28},{16,0},{20,4},{24,8},{28,12},{1,17},{... | collective-permute-start | bytes 4718600 | tf_op jit(solution)/shard_map/ppermute | solution.py:40
  198.1 87.1 %collective-permute-start.4 = (f32[8,512]{1,0:T(8,128)S(1)}, f32[8,512]{1,0:T(8,128)S(1)}, u32[]{:S(2)}, u32[]{:S(2)}) collective-permute-start(f32[8,512]{1,0:T(8,128)S(1)} %get-tuple-element.32), channel_id=1, source_target_pairs={{0,16},{4,20},{8,24},{12,28},{16,0},{20,4},{24,8},{28,12},{1,17},{... | collective-permute-start | bytes 49160 | tf_op jit(solution)/shard_map/ppermute | solution.py:40
  198.1 19.1 %collective-permute-start.48 = (bf16[4,128,512]{2,1,0:T(8,128)(2,1)S(1)}, bf16[4,128,512]{2,1,0:T(8,128)(2,1)S(1)}, u32[]{:S(2)}, u32[]{:S(2)}) collective-permute-start(bf16[4,128,512]{2,1,0:T(8,128)(2,1)S(1)} %get-tuple-element.54), channel_id=1, source_target_pairs={{0,1},{1,0},{2,3},{3,2},{4,5},{5,4},{6,7},{7,6},{8,9},{9,8},{10,11... | collective-permute-start | bytes 1572872 | tf_op jit(solution)/shard_map/ppermute | solution.py:30
  199.5 85.7 %collective-permute-start.27 = (bf16[2,3,64,512]{3,2,1,0:T(8,128)(2,1)S(1)}, bf16[2,3,64,512]{3,2,1,0:T(8,128)(2,1)S(1)}, u32[]{:S(2)}, u32[]{:S(2)}) collective-permute-start(bf16[2,3,64,512]{3,2,1,0:T(8,128)(2,1)S(1)} %pad_maximum_fusion.12), channel_id=1, source_target_pairs={{0,16},{4,20},{8,24},{12,28},{16,0},{20,4},{24,8},{28,12},{1,17},{... | collective-permute-start | bytes 1179656 | tf_op jit(solution)/shard_map/ppermute | solution.py:40
  215.4 13.9 %collective-permute-start.51 = (bf16[4,128,512]{2,1,0:T(8,128)(2,1)S(1)}, bf16[4,128,512]{2,1,0:T(8,128)(2,1)S(1)}, u32[]{:S(2)}, u32[]{:S(2)}) collective-permute-start(bf16[4,128,512]{2,1,0:T(8,128)(2,1)S(1)} %get-tuple-element.56), channel_id=1, source_target_pairs={{0,2},{1,3},{2,0},{3,1},{4,6},{5,7},{6,4},{7,5},{8,10},{9,11},{10,... | collective-permute-start | bytes 1572872 | tf_op jit(solution)/shard_map/ppermute | solution.py:30
  217.3 14.8 %collective-permute-start.46 = (bf16[2,128,512]{2,1,0:T(8,128)(2,1)S(1)}, bf16[2,128,512]{2,1,0:T(8,128)(2,1)S(1)}, u32[]{:S(2)}, u32[]{:S(2)}) collective-permute-start(bf16[2,128,512]{2,1,0:T(8,128)(2,1)S(1)} %slice.308), channel_id=1, source_target_pairs={{0,2},{1,3},{2,0},{3,1},{4,6},{5,7},{6,4},{7,5},{8,10},{9,11},{10,... | collective-permute-start | bytes 786440 | tf_op jit(solution)/shard_map/ppermute | solution.py:30
  229.3 21.0 %collective-permute-start.49 = (bf16[2,128,512]{2,1,0:T(8,128)(2,1)S(1)}, bf16[2,128,512]{2,1,0:T(8,128)(2,1)S(1)}, u32[]{:S(2)}, u32[]{:S(2)}) collective-permute-start(bf16[2,128,512]{2,1,0:T(8,128)(2,1)S(1)} %slice.307), channel_id=1, source_target_pairs={{0,8},{8,0},{16,24},{24,16},{1,9},{9,1},{17,25},{25,17},{2,10},{10... | collective-permute-start | bytes 786440 | tf_op jit(solution)/shard_map/ppermute | solution.py:30
  232.1 19.1 %collective-permute-start.52 = (bf16[2,128,512]{2,1,0:T(8,128)(2,1)S(1)}, bf16[2,128,512]{2,1,0:T(8,128)(2,1)S(1)}, u32[]{:S(2)}, u32[]{:S(2)}) collective-permute-start(bf16[2,128,512]{2,1,0:T(8,128)(2,1)S(1)} %slice.306), channel_id=1, source_target_pairs={{0,1},{1,0},{2,3},{3,2},{4,5},{5,4},{6,7},{7,6},{8,9},{9,8},{10,11... | collective-permute-start | bytes 786440 | tf_op jit(solution)/shard_map/ppermute | solution.py:30
  255.3 29.7 %collective-permute-start.53 = (bf16[1,128,512]{2,1,0:T(8,128)(2,1)S(1)}, bf16[1,128,512]{2,1,0:T(8,128)(2,1)S(1)}, u32[]{:S(2)}, u32[]{:S(2)}) collective-permute-start(bf16[1,128,512]{2,1,0:T(8,128)(2,1)S(1)} %slice.312), channel_id=1, source_target_pairs={{0,8},{8,0},{16,24},{24,16},{1,9},{9,1},{17,25},{25,17},{2,10},{10... | collective-permute-start | bytes 393224 | tf_op jit(solution)/shard_map/ppermute | solution.py:30
  285.1 10.7 %collective-permute-start.54 = (bf16[3,64,512]{2,1,0:T(8,128)(2,1)S(1)}, bf16[3,64,512]{2,1,0:T(8,128)(2,1)S(1)}, u32[]{:S(2)}, u32[]{:S(2)}) collective-permute-start(bf16[3,64,512]{2,1,0:T(8,128)(2,1)S(1)} %pad_maximum_fusion.20), channel_id=1, source_target_pairs={{0,4},{4,0},{1,5},{5,1},{2,6},{6,2},{3,7},{7,3},{8,12},{12,8},{9,1... | collective-permute-start | bytes 589832 | tf_op jit(solution)/shard_map/ppermute | solution.py:30
  (28 other events, 252.9 us)

commit v2 on v1

--- a/solution.py
+++ b/solution.py
@@ -15,7 +15,7 @@
 PARTS = 3
 
 norm_eps = 1e-05
-VMEM_BYTES = 48 * 1024 * 1024
+VMEM_BYTES = 10 * 1024 * 1024
 
 bf16 = jnp.bfloat16
 f32 = jnp.float32
@@ -274,20 +274,61 @@
     return [[dims[(i + p * max(1, n // PARTS)) % n] for i in range(n)] for p in range(PARTS)]
 
 
-def gather_cube(blocks, orders):
+def tied(x, *before):
+    return lax.optimization_barrier((x, before))[0]
+
+
+def link_users(orders, k, dim):
+    return [p for p in range(PARTS) if orders[p][k] == dim]
+
+
+def join_kernel(a_ref, b_ref, out_ref):
+    half = a_ref.shape[0]
+    out_ref[:half] = a_ref[...]
+    out_ref[half:] = b_ref[...]
+
+
+def join(a, b):
+    return pl.pallas_call(
+        join_kernel,
+        name="join",
+        out_shape=jax.ShapeDtypeStruct((2 * a.shape[0],) + a.shape[1:], a.dtype),
+        compiler_params=params(),
+    )(a, b)
+
+
+def readied(values, came, orders, k, last_k, before):
+    out = []
+    for p in range(PARTS):
+        deps = [] if came is None else [came[q] for q in link_users(orders, last_k, orders[p][k])]
+        deps = deps + list(before[1])
+        if orders[p][k][0] == "section":
+            deps = deps + list(before[0])
+        out.append(tied(values[p], *deps) if deps else values[p])
+    return out
+
+
+def gather_cube(blocks, orders, before, shadow=None):
     held = [b[None] for b in blocks]
-    for k in range(len(orders[0])):
-        came = [swapped(held[p], orders[p][k]) for p in range(PARTS)]
-        held = [jnp.concatenate([held[p], came[p]], axis=0) for p in range(PARTS)]
-    return held
-
-
-def sum_cube(keep, send, orders):
+    came = None
+    rounds = len(orders[0])
+    for k in range(rounds):
+        ready = readied(held, came, orders, k, k - 1, before.get(k, ((), ())))
+        came = [swapped(ready[p], orders[p][k]) for p in range(PARTS)]
+        if k < rounds - 1:
+            held = [join(held[p], came[p]) for p in range(PARTS)]
+    return held, came
+
+
+def sum_cube(keep, send, orders, before):
     keep = [k.astype(f32) for k in keep]
     rounds = len(orders[0])
+    came = None
     for k in range(rounds - 1, -1, -1):
-        came = [swapped(send[p], orders[p][k]).astype(f32) for p in range(PARTS)]
-        total = [keep[p] + came[p] for p in range(PARTS)]
+        turn = rounds - 1 - k
+        ready = readied(send, came, orders, k, k + 1, before.get(turn, ((), ())))
+        came = [swapped(ready[p], orders[p][k]) for p in range(PARTS)]
+        total = [keep[p] + came[p].astype(f32) for p in range(PARTS)]
         half = total[0].shape[0] // 2
         if k > 0:
             send = [t[half:].astype(bf16) for t in total]
@@ -295,15 +336,7 @@
     return [t[0].astype(bf16) for t in total]
 
 
-def block_place(order, slices, r, z):
-    place = 0
-    for k, (axis, bit) in enumerate(order):
-        on = z if axis == "section" else (r >> bit) & 1
-        place |= on << k
-    return place
-
-
-def block_place_traced(order, r, z):
+def block_place(order, r, z):
     place = 0
     for k, (axis, bit) in enumerate(order):
         on = z if axis == "section" else (r >> bit) & 1
@@ -311,130 +344,130 @@
     return place
 
 
+IN_CUTS = 4
+AHEAD = 5
+
+
 def experts_kernel(slices, orders, me, *refs):
-    ins = refs[: 2 * PARTS]
+    early, late = refs[:PARTS], refs[PARTS : 2 * PARTS]
     gain_ref, gate_ref, up_ref, down_ref = refs[2 * PARTS : 2 * PARTS + 4]
-    outs = refs[2 * PARTS + 4 : 4 * PARTS + 4]
-    gate_acc, up_acc, sq_acc, hidden = refs[4 * PARTS + 4 :]
-    step = pl.program_id(0)
-    chunks = PARTS * slices
-    rows = ins[0].shape[1]
-
-    @pl.when(step == 0)
-    def _():
-        gate_acc[...] = jnp.zeros_like(gate_acc)
-        up_acc[...] = jnp.zeros_like(up_acc)
-        sq_acc[...] = jnp.zeros_like(sq_acc)
-
-    for p in range(PARTS):
-
-        @pl.when((step >= p * slices) & (step < (p + 1) * slices))
-        def _():
-            x = jnp.concatenate([ins[2 * p][0], ins[2 * p + 1][0]], axis=0).astype(f32)
-            sq_acc[...] += jnp.sum(x * x, axis=1, keepdims=True)
-            xg = (x * gain_ref[0]).astype(bf16)
-            gate_acc[...] += jnp.dot(xg, gate_ref[...], preferred_element_type=f32)
-            up_acc[...] += jnp.dot(xg, up_ref[...], preferred_element_type=f32)
-
-    @pl.when(step == chunks - 1)
-    def _():
-        inv = lax.rsqrt(sq_acc[...] / D + norm_eps)
-        gate = gate_acc[...] * inv
-        up = up_acc[...] * inv
-        hidden[...] = (gate / (1.0 + jnp.exp(-gate)) * up).astype(bf16)
-
-    for p in range(PARTS):
-
-        @pl.when((step >= chunks + p * slices) & (step < chunks + (p + 1) * slices))
-        def _():
-            r = step - (chunks + p * slices)
-            out = jnp.dot(hidden[...], down_ref[...], preferred_element_type=f32).astype(bf16)
-            half = outs[2 * p].shape[0]
+    refs = refs[2 * PARTS + 4 :]
+    outs = refs[: 2 * PARTS]
+    scaled, hidden, in_w, down_w, in_sems, down_sems = refs[2 * PARTS :]
+    rows, width = early[0].shape[1:]
+    half = early[0].shape[0]
+    mine = me[0]
+    depth, tile = in_w.shape[1:]
+    tiles = hidden.shape[1] // tile
+    chunks = slices * PARTS
+
+    copies = []
+    for n in range(tiles):
+        for src in (gate_ref, up_ref):
+            for q in range(IN_CUTS):
+                i = len(copies)
+                copies.append(
+                    pltpu.make_async_copy(
+                        src.at[q * depth : (q + 1) * depth, n * tile : (n + 1) * tile],
+                        in_w.at[i],
+                        in_sems.at[i],
+                    )
+                )
+    firsts = len(copies)
+    for p in range(PARTS):
+        for r in range(slices):
+            col = pl.multiple_of(((mine ^ r) * PARTS + p) * width, width)
+            i = p * slices + r
+            copies.append(
+                pltpu.make_async_copy(
+                    down_ref.at[:, pl.ds(col, width)], down_w.at[i], down_sems.at[i]
+                )
+            )
+    for copy in copies[:AHEAD]:
+        copy.start()
+
+    def arrived(i):
+        copies[i].wait()
+        if i + AHEAD < len(copies):
+            copies[i + AHEAD].start()
+
+    squares = jnp.zeros((2 * rows, 128), f32)
+    for p in range(PARTS):
+        for r in range(slices):
+            got = []
             for z in range(2):
-                place = block_place_traced(orders[p], r, z)
+                place = block_place(orders[p], r, z)
+                got.append(early[p][place] if place < half else late[p][place - half])
+            x = jnp.concatenate(got, axis=0).astype(f32)
+            scaled[(mine ^ r) * PARTS + p] = (x * gain_ref[r, p]).astype(bf16)
+            for c in range(0, width, 128):
+                squares = squares + x[:, c : c + 128] * x[:, c : c + 128]
+    inv = lax.rsqrt(jnp.sum(squares, axis=1, keepdims=True) / D + norm_eps)
+
+    def product(first):
+        total = None
+        per = chunks // IN_CUTS
+        for q in range(IN_CUTS):
+            arrived(first + q)
+            for j in range(per):
+                term = jnp.dot(
+                    scaled[q * per + j],
+                    in_w[first + q, j * width : (j + 1) * width, :],
+                    preferred_element_type=f32,
+                )
+                total = term if total is None else total + term
+        return total * inv
+
+    for n in range(tiles):
+        gate = product(2 * n * IN_CUTS)
+        up = product((2 * n + 1) * IN_CUTS)
+        hidden[:, n * tile : (n + 1) * tile] = (gate / (1.0 + jnp.exp(-gate)) * up).astype(bf16)
+
+    for p in range(PARTS):
+        for r in range(slices):
+            arrived(firsts + p * slices + r)
+            out = jnp.dot(
+                hidden[...], down_w[p * slices + r], preferred_element_type=f32
+            ).astype(bf16)
+            for z in range(2):
+                place = block_place(orders[p], r, z)
                 block = out[z * rows : (z + 1) * rows]
-                if orders[p][-1][0] == "section":
-                    outs[2 * p + z][place - z * half] = block
+                if place < half:
+                    outs[2 * p][place] = block
                 else:
-
-                    @pl.when(place < half)
-                    def _():
-                        outs[2 * p][place] = block
-
-                    @pl.when(place >= half)
-                    def _():
-                        outs[2 * p + 1][place - half] = block
-
-
-def experts(me, held, gain_all, gate_w, up_w, down_w, orders):
-    blocks, rows, width = held[0].shape
-    slices = blocks // 2
-    chunks = PARTS * slices
+                    outs[2 * p + 1][place - half] = block
+
+
+def experts(me, early, late, gain_all, gate_w, up_w, down_w, orders):
+    half, rows, width = early[0].shape
     hidden_count = gate_w.shape[1]
-
-    def part_and_slice(chunk):
-        return chunk // slices, chunk % slices
-
-    def row_map(p, z):
-        def index(step, me):
-            r = jnp.clip(step - p * slices, 0, slices - 1)
-            return (block_place_traced(orders[p], r, z), 0, 0)
-
-        return index
-
-    def weight_place(chunk, me):
-        p, r = part_and_slice(chunk)
-        return (me[0] ^ r) * PARTS + p
-
-    def in_map(step, me):
-        return (weight_place(jnp.minimum(step, chunks - 1), me), 0)
-
-    def gain_map(step, me):
-        return (weight_place(jnp.minimum(step, chunks - 1), me), 0, 0)
-
-    def down_map(step, me):
-        return (0, weight_place(jnp.maximum(step - chunks, 0), me))
-
-    in_specs = []
-    operands = []
-    for p in range(PARTS):
-        for z in range(2):
-            in_specs.append(pl.BlockSpec((1, rows, width), row_map(p, z)))
-            operands.append(held[p])
-    in_specs += [
-        pl.BlockSpec((1, 1, width), gain_map),
-        pl.BlockSpec((width, hidden_count), in_map),
-        pl.BlockSpec((width, hidden_count), in_map),
-        pl.BlockSpec((hidden_count, width), down_map),
-    ]
-    out_shape = [jax.ShapeDtypeStruct((blocks // 2, rows, width), bf16)] * (2 * PARTS)
-    out_specs = [
-        pl.BlockSpec((blocks // 2, rows, width), lambda step, me: (0, 0, 0))
-    ] * (2 * PARTS)
-    flops = 2 * 2 * rows * D * hidden_count * 3
+    tile = min(512, hidden_count)
+    firsts = 2 * (hidden_count // tile) * IN_CUTS
+    vmem = pl.BlockSpec(memory_space=pltpu.VMEM)
+    hbm = pl.BlockSpec(memory_space=pltpu.HBM)
     outs = pl.pallas_call(
-        functools.partial(experts_kernel, slices, orders),
+        functools.partial(experts_kernel, half, orders),
         name="experts",
-        out_shape=out_shape,
-        grid_spec=pltpu.PrefetchScalarGridSpec(
-            num_scalar_prefetch=1,
-            grid=(2 * chunks,),
-            in_specs=in_specs,
-            out_specs=out_specs,
-            scratch_shapes=[
-                pltpu.VMEM((2 * rows, hidden_count), f32),
-                pltpu.VMEM((2 * rows, hidden_count), f32),
-                pltpu.VMEM((2 * rows, 1), f32),
-                pltpu.VMEM((2 * rows, hidden_count), bf16),
-            ],
-        ),
-        compiler_params=params(),
+        out_shape=[jax.ShapeDtypeStruct((half, rows, width), bf16)] * (2 * PARTS),
+        in_specs=[pl.BlockSpec(memory_space=pltpu.SMEM)]
+        + [vmem] * (2 * PARTS + 1)
+        + [hbm] * 3,
+        out_specs=[vmem] * (2 * PARTS),
+        scratch_shapes=[
+            pltpu.VMEM((half * PARTS, 2 * rows, width), bf16),
+            pltpu.VMEM((2 * rows, hidden_count), bf16),
+            pltpu.VMEM((firsts, D // IN_CUTS, tile), bf16),
+            pltpu.VMEM((half * PARTS, hidden_count, width), bf16),
+            pltpu.SemaphoreType.DMA((firsts,)),
+            pltpu.SemaphoreType.DMA((half * PARTS,)),
+        ],
+        compiler_params=pltpu.CompilerParams(vmem_limit_bytes=47 * 1024 * 1024),
         cost_estimate=pl.CostEstimate(
-            flops=flops,
+            flops=2 * 2 * rows * D * hidden_count * 3,
             bytes_accessed=3 * D * hidden_count * 2 + 4 * rows * D * 2,
             transcendentals=2 * rows * hidden_count,
         ),
-    )(me, *operands, gain_all, gate_w, up_w, down_w)
+    )(me, *early, *late, gain_all, gate_w, up_w, down_w)
     return outs[0::2], outs[1::2]
 
 
@@ -464,23 +497,34 @@
             lax.dynamic_index_in_dim(lengths, (section - 2) % sections, 0, keepdims=False),
         ]
     )
-    gain_all = lax.all_gather(gain_row[0], "tensor", axis=0, tiled=True)
-    gain_all = gain_all.reshape(slices * PARTS, 1, width)
+    gain_all = gain_row.reshape(1, PARTS, 1, width)
+    for b in range(slices.bit_length() - 1):
+        gain_all = jnp.concatenate([gain_all, swapped(gain_all, ("tensor", b))], axis=0)
     orders = cube_orders(slices)
+    rounds = len(orders[0])
     gate_w, up_w, down_w = w_gate[0, 0], w_up[0, 0], w_down[0, 0]
+    pieces = []
+    begin = 0
+    for share in (6, 6, 7, 6, 7):
+        pieces.append(tokens[begin : begin + rows * share // 32])
+        begin += rows * share // 32
 
     slots, own, other = prologue(core, lens, ids_rows, tokens)
+    far = [ahead(pieces[0], 2)]
+    far.append(ahead(tied(pieces[1], far[0]), 2))
     block = jnp.concatenate([own, swapped(other, across)], axis=1)
-    held = gather_cube([block[p] for p in range(PARTS)], orders)
-
-    far_tokens = ahead(tokens, 2)
+    waits = {1: ([far[0]], []), rounds - 1: ([far[1]], [gain_all])}
+    early, late = gather_cube([block[p] for p in range(PARTS)], orders, waits)
+
+    far.append(ahead(tied(pieces[2], *late), 2))
     next_slots = ahead(slots, -2)
     stat = tensor_sum(stats(tokens, gain_row, router_t))
     aux, base, mix = prepare(core, stat, ids_rows, slots, next_slots, tokens)
     far_aux = ahead(aux, 2)
 
-    keep, send = experts(me, held, gain_all, gate_w, up_w, down_w, orders)
-    summed = sum_cube(keep, send, orders)
+    keep, send = experts(me, early, late, gain_all, gate_w, up_w, down_w, orders)
+    far.append(ahead(tied(pieces[3], *send), 2))
+    summed = sum_cube(keep, send, orders, {0: ([], [far[2]]), rounds - 1: ([far[3]], [])})
 
     mine = [s[:CAP] for s in summed]
     theirs = [swapped(s[CAP:], across) for s in summed]
@@ -488,14 +532,17 @@
     for p in range(PARTS):
         to_own, to_other = repick(mix, base[p], mine[p], theirs[p])
         blocks.append(jnp.concatenate([ahead(to_own, 2), ahead(to_other, 2, True)], axis=0))
-    held = gather_cube(blocks, orders)
-
-    moved = ahead(jnp.stack([jnp.stack(mine), jnp.stack(theirs)]), 2)
-    state, stat = between(far_tokens, far_aux, moved[0], moved[1], gain_row, router_t)
+    slab_own = ahead(tied(jnp.stack(mine), *blocks), 2)
+    slab_other = ahead(tied(jnp.stack(theirs), slab_own), 2)
+    waits = {rounds - 2: ([slab_own], []), rounds - 1: ([slab_other], [])}
+    early, late = gather_cube(blocks, orders, waits)
+    far.append(ahead(tied(pieces[4], slab_other, *late), 2))
+
+    keep, send = experts(me, early, late, gain_all, gate_w, up_w, down_w, orders)
+    far_tokens = jnp.concatenate(far, axis=0)
+    state, stat = between(far_tokens, far_aux, slab_own, slab_other, gain_row, router_t)
     stat = tensor_sum(stat)
-
-    keep, send = experts(me, held, gain_all, gate_w, up_w, down_w, orders)
-    summed = sum_cube(keep, send, orders)
+    summed = sum_cube(keep, send, orders, {0: ([], [far[4]]), rounds - 1: ([], [stat])})
     mine = jnp.stack([s[:CAP] for s in summed])
     theirs = swapped(jnp.stack([s[CAP:] for s in summed]), across)
     return last(core, state, stat, ids_rows, slots, mine, theirs)

time: 299 us -> 227 us (0.76)
  waiting for transfers between devices: 143 us -> 107 us
  Pallas kernels: 64.1 us -> 42.9 us
  blocking collectives: 10.2 us -> 0 us
  other arithmetic: 7.98 us -> 1.75 us
    ppermute x45 -> x47, waiting for transfers between devices: 134 us -> 78.8 us  [swapped(): lax.ppermute(x, axis, [(i, i ^ 1 << bit) for i in range(lax.axis_size(axi...]
    pallas_call x2 -> x14, Pallas kernels: 55.3 us -> 33.7 us  [the longest x2 33.4 us: experts(): pl.pallas_call(functools.partial(experts_kernel, half, orders), name='exp...]
    ppermute x10 -> x15, waiting for transfers between devices: 8.9 us -> 27.8 us  [ahead(): return lax.ppermute(x, ('section', 'expert'), perm)]
    all_gather x1 -> x0, blocking collectives: 10.2 us -> none  [on_device(): gain_all = lax.all_gather(gain_row[0], 'tensor', axis=0, tiled=True)]
    concatenate x18 -> x2, other arithmetic: 6.17 us -> 0.04 us  [on_device(): jnp.concatenate([gain_all, swapped(gain_all, ('tensor', b))], axis=0)]
    ppermute x10 -> x15, starting transfers between devices: 19.2 us -> 19.7 us  [ahead(): return lax.ppermute(x, ('section', 'expert'), perm)]
    ppermute x45 -> x47, starting transfers between devices: 48.8 us -> 49.2 us  [swapped(): lax.ppermute(x, axis, [(i, i ^ 1 << bit) for i in range(lax.axis_size(axi...]
  transfers between devices with their start and end apart: 55 -> 62, of which waited for: 28 -> 39; matrix products, arithmetic and copies ran while one was open for 2% -> 2% of each run, Pallas kernels for 2% -> 18%
where the time goes in v2:
time: 227 us; the launch traced here: 226 us
  waiting for transfers between devices  107 us (47%)
  starting transfers between devices  68.9 us (30%)
  Pallas kernels  42.9 us (19%)
  local copies, waits for them, and re-layouts  5.46 us (2%)
    ppermute x47, waiting for transfers between devices, swapped(): lax.ppermute(x, axis, [(i, i ^ 1 << bit) for i in range(lax.axis_size(axi...  78.8 us
    ppermute x47, starting transfers between devices, swapped(): lax.ppermute(x, axis, [(i, i ^ 1 << bit) for i in range(lax.axis_size(axi...  49.2 us
    pallas_call x2, Pallas kernels, experts(): pl.pallas_call(functools.partial(experts_kernel, half, orders), name='exp...  33.4 us
    ppermute x15, waiting for transfers between devices, ahead(): return lax.ppermute(x, ('section', 'expert'), perm)  27.8 us
    ppermute x15, starting transfers between devices, ahead(): return lax.ppermute(x, ('section', 'expert'), perm)  19.7 us
  transfers between devices with their start and end apart: 62, of which 39 were waited for; matrix products, arithmetic and copies ran while one was open for 2% of the time, Pallas kernels for 18%

profile of v2, /device:TPU:0, one launch (start us, length us, event | category | flops | bytes accessed | tf_op | source)
XLA Modules:
  0.0 226.4 jit_solution(6541563596016907658)
XLA Ops:
  5.5 3.9 %collective-permute-start = (bf16[96,1536]{1,0:T(8,128)(2,1)S(1)}, bf16[96,1536]{1,0:T(8,128)(2,1)S(1)}, u32[]{:S(2)}, u32[]{:S(2)}) collective-permute-start(bf16[96,1536]{1,0:T(8,128)(2,1)S(1)} %get-tuple-element.133), channel_id=1, source_target_pairs={{0,16},{4,20},{8,24},{12,28},{16,0},{20,4},{24,8},{28,12},{1,17},{... | collective-permute-start | bytes 884744 | tf_op jit(solution)/shard_map/ppermute | solution.py:40
  14.1 9.0 %collective-permute-done = bf16[96,1536]{1,0:T(8,128)(2,1)S(1)} collective-permute-done((bf16[96,1536]{1,0:T(8,128)(2,1)S(1)}, bf16[96,1536]{1,0:T(8,128)(2,1)S(1)}, u32[]{:S(2)}, u32[]{:S(2)}) %collective-permute-start) | collective-permute-done | bytes 294944 | tf_op jit(solution)/shard_map/ppermute | solution.py:40
  26.3 4.1 %collective-permute-start.7 = (bf16[2,128,512]{2,1,0:T(8,128)(2,1)S(1)}, bf16[2,128,512]{2,1,0:T(8,128)(2,1)S(1)}, u32[]{:S(2)}, u32[]{:S(2)}) collective-permute-start(bf16[2,128,512]{2,1,0:T(8,128)(2,1)S(1)} %join.14.a_ref), channel_id=1, source_target_pairs={{0,8},{8,0},{16,24},{24,16},{1,9},{9,1},{17,25},{25,17},{2,10},{10... | collective-permute-start | bytes 786440 | tf_op jit(solution)/shard_map/ppermute | solution.py:30
  31.1 3.1 %collective-permute-done.8 = f32[1,3,1,512]{3,2,1,0:T(1,128)S(1)} collective-permute-done((f32[1,3,1,512]{3,2,1,0:T(1,128)S(1)}, f32[1,3,1,512]{3,2,1,0:T(1,128)S(1)}, u32[]{:S(2)}, u32[]{:S(2)}) %collective-permute-start.8) | collective-permute-done | bytes 6176 | tf_op jit(solution)/shard_map/ppermute | solution.py:30
  34.7 3.2 %collective-permute-done.9 = f32[2,3,1,512]{3,2,1,0:T(1,128)S(1)} collective-permute-done((f32[2,3,1,512]{3,2,1,0:T(1,128)S(1)}, f32[2,3,1,512]{3,2,1,0:T(1,128)S(1)}, u32[]{:S(2)}, u32[]{:S(2)}) %collective-permute-start.9) | collective-permute-done | bytes 12320 | tf_op jit(solution)/shard_map/ppermute | solution.py:30
  38.6 2.5 %collective-permute-done.7.b_ref = bf16[2,128,512]{2,1,0:T(8,128)(2,1)S(1)} collective-permute-done((bf16[2,128,512]{2,1,0:T(8,128)(2,1)S(1)}, bf16[2,128,512]{2,1,0:T(8,128)(2,1)S(1)}, u32[]{:S(2)}, u32[]{:S(2)}) %collective-permute-start.7) | collective-permute-done | bytes 262176 | tf_op jit(solution)/shard_map/ppermute | solution.py:30
  42.6 6.9 %collective-permute-done.13.refs_5_ = bf16[4,128,512]{2,1,0:T(8,128)(2,1)} collective-permute-done((bf16[4,128,512]{2,1,0:T(8,128)(2,1)S(1)}, bf16[4,128,512]{2,1,0:T(8,128)(2,1)}, u32[]{:S(2)}, u32[]{:S(2)}) %collective-permute-start.13) | collective-permute-done | bytes 524320 | tf_op jit(solution)/shard_map/ppermute | solution.py:30
  49.5 4.3 %collective-permute-done.12.refs_4_ = bf16[4,128,512]{2,1,0:T(8,128)(2,1)} collective-permute-done((bf16[4,128,512]{2,1,0:T(8,128)(2,1)S(1)}, bf16[4,128,512]{2,1,0:T(8,128)(2,1)}, u32[]{:S(2)}, u32[]{:S(2)}) %collective-permute-start.12) | collective-permute-done | bytes 524320 | tf_op jit(solution)/shard_map/ppermute | solution.py:30
  55.7 17.3 %experts.2 = (bf16[4,128,512]{2,1,0:T(8,128)(2,1)S(1)}, bf16[4,128,512]{2,1,0:T(8,128)(2,1)S(1)}, bf16[4,128,512]{2,1,0:T(8,128)(2,1)S(1)}, bf16[4,128,512]{2,1,...) custom-call(s32[1]{0:T(128)} %bitcast.5.me, ...), custom_call_target="tpu_custom_call" | custom-call | flops 9663676416 | bytes 44040192 | tf_op jit(solution)/shard_map/experts/pallas_call | solution.py:448
  79.7 5.3 %collective-permute-done.28 = f32[16,512]{1,0:T(8,128)S(1)} collective-permute-done((f32[16,512]{1,0:T(8,128)S(1)}, f32[16,512]{1,0:T(8,128)S(1)}, u32[]{:S(2)}, u32[]{:S(2)}) %collective-permute-start.28) | collective-permute-done | bytes 32800 | tf_op jit(solution)/shard_map/ppermute | solution.py:30
  86.7 2.3 %collective-permute-done.29 = f32[16,512]{1,0:T(8,128)S(1)} collective-permute-done((f32[16,512]{1,0:T(8,128)S(1)}, f32[16,512]{1,0:T(8,128)S(1)}, u32[]{:S(2)}, u32[]{:S(2)}) %collective-permute-start.29) | collective-permute-done | bytes 32800 | tf_op jit(solution)/shard_map/ppermute | solution.py:30
  89.0 5.1 %collective-permute-done.30.next_ref = f32[8,512]{1,0:T(8,128)S(1)} collective-permute-done((f32[8,512]{1,0:T(8,128)S(1)}, f32[8,512]{1,0:T(8,128)S(1)}, u32[]{:S(2)}, u32[]{:S(2)}) %collective-permute-start.30) | collective-permute-done | bytes 16416 | tf_op jit(solution)/shard_map/ppermute | solution.py:40
  95.3 3.1 %collective-permute-start.20 = (bf16[2,128,512]{2,1,0:T(8,128)(2,1)S(1)}, bf16[2,128,512]{2,1,0:T(8,128)(2,1)S(1)}, u32[]{:S(2)}, u32[]{:S(2)}) collective-permute-start(bf16[2,128,512]{2,1,0:T(8,128)(2,1)S(1)} %slice.318), channel_id=1, source_target_pairs={{0,1},{1,0},{2,3},{3,2},{4,5},{5,4},{6,7},{7,6},{8,9},{9,8},{10,11... | collective-permute-start | bytes 786440 | tf_op jit(solution)/shard_map/ppermute | solution.py:30
  100.2 3.4 %collective-permute-done.20 = bf16[2,128,512]{2,1,0:T(8,128)(2,1)S(1)} collective-permute-done((bf16[2,128,512]{2,1,0:T(8,128)(2,1)S(1)}, bf16[2,128,512]{2,1,0:T(8,128)(2,1)S(1)}, u32[]{:S(2)}, u32[]{:S(2)}) %collective-permute-start.20) | collective-permute-done | bytes 262176 | tf_op jit(solution)/shard_map/ppermute | solution.py:30
  103.7 2.5 %collective-permute-done.23 = bf16[2,128,512]{2,1,0:T(8,128)(2,1)S(1)} collective-permute-done((bf16[2,128,512]{2,1,0:T(8,128)(2,1)S(1)}, bf16[2,128,512]{2,1,0:T(8,128)(2,1)S(1)}, u32[]{:S(2)}, u32[]{:S(2)}) %collective-permute-start.23) | collective-permute-done | bytes 262176 | tf_op jit(solution)/shard_map/ppermute | solution.py:30
  112.8 2.9 %collective-permute-start.35 = (bf16[64,512]{1,0:T(8,128)(2,1)S(1)}, bf16[64,512]{1,0:T(8,128)(2,1)S(1)}, u32[]{:S(2)}, u32[]{:S(2)}) collective-permute-start(bf16[64,512]{1,0:T(8,128)(2,1)S(1)} %get-tuple-element.100), channel_id=1, source_target_pairs={{0,16},{4,20},{8,24},{12,28},{16,0},{20,4},{24,8},{28,12},{1,17},{... | collective-permute-start | bytes 196616 | tf_op jit(solution)/shard_map/ppermute | solution.py:40
  116.2 2.7 %collective-permute-start.31 = (bf16[64,512]{1,0:T(8,128)(2,1)S(1)}, bf16[64,512]{1,0:T(8,128)(2,1)S(1)}, u32[]{:S(2)}, u32[]{:S(2)}) collective-permute-start(bf16[64,512]{1,0:T(8,128)(2,1)S(1)} %get-tuple-element.96), channel_id=1, source_target_pairs={{0,16},{4,20},{8,24},{12,28},{16,0},{20,4},{24,8},{28,12},{1,17},{... | collective-permute-start | bytes 196616 | tf_op jit(solution)/shard_map/ppermute | solution.py:40
  119.1 2.6 %collective-permute-start.33 = (bf16[64,512]{1,0:T(8,128)(2,1)S(1)}, bf16[64,512]{1,0:T(8,128)(2,1)S(1)}, u32[]{:S(2)}, u32[]{:S(2)}) collective-permute-start(bf16[64,512]{1,0:T(8,128)(2,1)S(1)} %get-tuple-element.98), channel_id=1, source_target_pairs={{0,16},{4,20},{8,24},{12,28},{16,0},{20,4},{24,8},{28,12},{1,17},{... | collective-permute-start | bytes 196616 | tf_op jit(solution)/shard_map/ppermute | solution.py:40
  121.7 2.5 %collective-permute-done.35 = bf16[64,512]{1,0:T(8,128)(2,1)S(1)} collective-permute-done((bf16[64,512]{1,0:T(8,128)(2,1)S(1)}, bf16[64,512]{1,0:T(8,128)(2,1)S(1)}, u32[]{:S(2)}, u32[]{:S(2)}) %collective-permute-start.35) | collective-permute-done | bytes 65568 | tf_op jit(solution)/shard_map/ppermute | solution.py:40
  124.2 5.6 %collective-permute-done.31 = bf16[64,512]{1,0:T(8,128)(2,1)S(1)} collective-permute-done((bf16[64,512]{1,0:T(8,128)(2,1)S(1)}, bf16[64,512]{1,0:T(8,128)(2,1)S(1)}, u32[]{:S(2)}, u32[]{:S(2)}) %collective-permute-start.31) | collective-permute-done | bytes 65568 | tf_op jit(solution)/shard_map/ppermute | solution.py:40
  129.8 2.8 %collective-permute-done.33 = bf16[64,512]{1,0:T(8,128)(2,1)S(1)} collective-permute-done((bf16[64,512]{1,0:T(8,128)(2,1)S(1)}, bf16[64,512]{1,0:T(8,128)(2,1)S(1)}, u32[]{:S(2)}, u32[]{:S(2)}) %collective-permute-start.33) | collective-permute-done | bytes 65568 | tf_op jit(solution)/shard_map/ppermute | solution.py:40
  134.0 2.7 %collective-permute-start.42 = (bf16[1,128,512]{2,1,0:T(8,128)(2,1)S(1)}, bf16[1,128,512]{2,1,0:T(8,128)(2,1)S(1)}, u32[]{:S(2)}, u32[]{:S(2)}) collective-permute-start(bf16[1,128,512]{2,1,0:T(8,128)(2,1)S(1)} %bitcast.43), channel_id=1, source_target_pairs={{0,8},{8,0},{16,24},{24,16},{1,9},{9,1},{17,25},{25,17},{2,10},{10... | collective-permute-start | bytes 393224 | tf_op jit(solution)/shard_map/ppermute | solution.py:30
  138.7 2.9 %collective-permute-done.42.b_ref = bf16[1,128,512]{2,1,0:T(8,128)(2,1)S(1)} collective-permute-done((bf16[1,128,512]{2,1,0:T(8,128)(2,1)S(1)}, bf16[1,128,512]{2,1,0:T(8,128)(2,1)S(1)}, u32[]{:S(2)}, u32[]{:S(2)}) %collective-permute-start.42) | collective-permute-done | bytes 131104 | tf_op jit(solution)/shard_map/ppermute | solution.py:30
  151.7 6.2 %collective-permute-done.43.b_ref = bf16[2,128,512]{2,1,0:T(8,128)(2,1)S(1)} collective-permute-done((bf16[2,128,512]{2,1,0:T(8,128)(2,1)S(1)}, bf16[2,128,512]{2,1,0:T(8,128)(2,1)S(1)}, u32[]{:S(2)}, u32[]{:S(2)}) %collective-permute-start.43) | collective-permute-done | bytes 262176 | tf_op jit(solution)/shard_map/ppermute | solution.py:30
  158.5 2.9 %collective-permute-start.49 = (f32[8,512]{1,0:T(8,128)S(1)}, f32[8,512]{1,0:T(8,128)S(1)}, u32[]{:S(2)}, u32[]{:S(2)}) collective-permute-start(f32[8,512]{1,0:T(8,128)S(1)} %get-tuple-element.111), channel_id=1, source_target_pairs={{0,16},{4,20},{8,24},{12,28},{16,0},{20,4},{24,8},{28,12},{1,17},{... | collective-permute-start | bytes 49160 | tf_op jit(solution)/shard_map/ppermute | solution.py:40
  162.6 8.5 %collective-permute-done.46.refs_4_ = bf16[4,128,512]{2,1,0:T(8,128)(2,1)S(1)} collective-permute-done((bf16[4,128,512]{2,1,0:T(8,128)(2,1)S(1)}, bf16[4,128,512]{2,1,0:T(8,128)(2,1)S(1)}, u32[]{:S(2)}, u32[]{:S(2)}) %collective-permute-start.46) | collective-permute-done | bytes 524320 | tf_op jit(solution)/shard_map/ppermute | solution.py:30
  172.6 16.1 %experts.3 = (bf16[4,128,512]{2,1,0:T(8,128)(2,1)S(1)}, bf16[4,128,512]{2,1,0:T(8,128)(2,1)S(1)}, bf16[4,128,512]{2,1,0:T(8,128)(2,1)S(1)}, bf16[4,128,512]{2,1,...) custom-call(s32[1]{0:T(128)} %bitcast.5.me, ...), custom_call_target="tpu_custom_call" | custom-call | flops 9663676416 | bytes 44040192 | tf_op jit(solution)/shard_map/experts/pallas_call | solution.py:448
  192.0 2.9 %between.1 = (bf16[512,1536]{1,0:T(8,128)(2,1)S(1)}, f32[16,512]{1,0:T(8,128)S(1)}) custom-call(bf16[512,1536]{1,0:T(8,128)(2,1)S(1)} %constant_dynamic-update-slice_fusion.8.x_ref, f32[8,512]{1,0:T(8,128)S(1)} %collective-permute-done.49.aux_ref, bf16[3,64,512]{2,1,0:T(8,128)(2,1)S(1)} %collective-permute-done.37.own_ref, ...), custom_call_target="tpu_custom_call" | custom-call | tf_op jit(solution)/shard_map/between/pallas_call | solution.py:237
  196.9 2.3 %collective-permute-done.50 = f32[16,512]{1,0:T(8,128)S(1)} collective-permute-done((f32[16,512]{1,0:T(8,128)S(1)}, f32[16,512]{1,0:T(8,128)S(1)}, u32[]{:S(2)}, u32[]{:S(2)}) %collective-permute-start.50) | collective-permute-done | bytes 32800 | tf_op jit(solution)/shard_map/ppermute | solution.py:30
  203.9 4.2 %collective-permute-done.55 = bf16[4,128,512]{2,1,0:T(8,128)(2,1)S(1)} collective-permute-done((bf16[4,128,512]{2,1,0:T(8,128)(2,1)S(1)}, bf16[4,128,512]{2,1,0:T(8,128)(2,1)S(1)}, u32[]{:S(2)}, u32[]{:S(2)}) %collective-permute-start.55) | collective-permute-done | bytes 524320 | tf_op jit(solution)/shard_map/ppermute | solution.py:30
  210.0 5.9 %collective-permute-done.56 = bf16[2,128,512]{2,1,0:T(8,128)(2,1)S(1)} collective-permute-done((bf16[2,128,512]{2,1,0:T(8,128)(2,1)S(1)}, bf16[2,128,512]{2,1,0:T(8,128)(2,1)S(1)}, u32[]{:S(2)}, u32[]{:S(2)}) %collective-permute-start.56) | collective-permute-done | bytes 262176 | tf_op jit(solution)/shard_map/ppermute | solution.py:30
  218.0 2.9 %collective-permute-done.57 = bf16[1,128,512]{2,1,0:T(8,128)(2,1)S(1)} collective-permute-done((bf16[1,128,512]{2,1,0:T(8,128)(2,1)S(1)}, bf16[1,128,512]{2,1,0:T(8,128)(2,1)S(1)}, u32[]{:S(2)}, u32[]{:S(2)}) %collective-permute-start.57) | collective-permute-done | bytes 131104 | tf_op jit(solution)/shard_map/ppermute | solution.py:30
  (198 shorter events, 73.0 us)
Async XLA Ops:
  5.5 17.6 %collective-permute-start = (bf16[96,1536]{1,0:T(8,128)(2,1)S(1)}, bf16[96,1536]{1,0:T(8,128)(2,1)S(1)}, u32[]{:S(2)}, u32[]{:S(2)}) collective-permute-start(bf16[96,1536]{1,0:T(8,128)(2,1)S(1)} %get-tuple-element.133), channel_id=1, source_target_pairs={{0,16},{4,20},{8,24},{12,28},{16,0},{20,4},{24,8},{28,12},{1,17},{... | collective-permute-start | bytes 884744 | tf_op jit(solution)/shard_map/ppermute | solution.py:40
  9.4 13.6 %collective-permute-start.6 = (bf16[1,128,512]{2,1,0:T(8,128)(2,1)S(1)}, bf16[1,128,512]{2,1,0:T(8,128)(2,1)S(1)}, u32[]{:S(2)}, u32[]{:S(2)}) collective-permute-start(bf16[1,128,512]{2,1,0:T(8,128)(2,1)S(1)} %get-tuple-element.137.a_ref), channel_id=1, source_target_pairs={{0,8},{8,0},{16,24},{24,16},{1,9},{9,1},{17,25},{25,17},{2,10},{10... | collective-permute-start | bytes 393224 | tf_op jit(solution)/shard_map/ppermute | solution.py:30
  11.0 12.0 %collective-permute-start.3 = (bf16[1,128,512]{2,1,0:T(8,128)(2,1)S(1)}, bf16[1,128,512]{2,1,0:T(8,128)(2,1)S(1)}, u32[]{:S(2)}, u32[]{:S(2)}) collective-permute-start(bf16[1,128,512]{2,1,0:T(8,128)(2,1)S(1)} %get-tuple-element.139.a_ref), channel_id=1, source_target_pairs={{0,1},{1,0},{2,3},{3,2},{4,5},{5,4},{6,7},{7,6},{8,9},{9,8},{10,11... | collective-permute-start | bytes 393224 | tf_op jit(solution)/shard_map/ppermute | solution.py:30
  12.5 12.2 %collective-permute-start.4 = (bf16[1,128,512]{2,1,0:T(8,128)(2,1)S(1)}, bf16[1,128,512]{2,1,0:T(8,128)(2,1)S(1)}, u32[]{:S(2)}, u32[]{:S(2)}) collective-permute-start(bf16[1,128,512]{2,1,0:T(8,128)(2,1)S(1)} %get-tuple-element.138.a_ref), channel_id=1, source_target_pairs={{0,2},{1,3},{2,0},{3,1},{4,6},{5,7},{6,4},{7,5},{8,10},{9,11},{10,... | collective-permute-start | bytes 393224 | tf_op jit(solution)/shard_map/ppermute | solution.py:30
  23.0 18.5 %collective-permute-start.1 = (bf16[96,1536]{1,0:T(8,128)(2,1)}, bf16[96,1536]{1,0:T(8,128)(2,1)}, u32[]{:S(2)}, u32[]{:S(2)}) collective-permute-start(bf16[96,1536]{1,0:T(8,128)(2,1)} %get-tuple-element.67), channel_id=1, source_target_pairs={{0,16},{4,20},{8,24},{12,28},{16,0},{20,4},{24,8},{28,12},{1,17},{... | collective-permute-start | bytes 884744 | tf_op jit(solution)/shard_map/ppermute | solution.py:40
  23.1 14.9 %collective-permute-start.11 = (bf16[2,128,512]{2,1,0:T(8,128)(2,1)S(1)}, bf16[2,128,512]{2,1,0:T(8,128)(2,1)S(1)}, u32[]{:S(2)}, u32[]{:S(2)}) collective-permute-start(bf16[2,128,512]{2,1,0:T(8,128)(2,1)S(1)} %join.16.a_ref), channel_id=1, source_target_pairs={{0,1},{1,0},{2,3},{3,2},{4,5},{5,4},{6,7},{7,6},{8,9},{9,8},{10,11... | collective-permute-start | bytes 786440 | tf_op jit(solution)/shard_map/ppermute | solution.py:30
  24.7 13.3 %collective-permute-start.5 = (bf16[2,128,512]{2,1,0:T(8,128)(2,1)S(1)}, bf16[2,128,512]{2,1,0:T(8,128)(2,1)S(1)}, u32[]{:S(2)}, u32[]{:S(2)}) collective-permute-start(bf16[2,128,512]{2,1,0:T(8,128)(2,1)S(1)} %join.12.a_ref), channel_id=1, source_target_pairs={{0,2},{1,3},{2,0},{3,1},{4,6},{5,7},{6,4},{7,5},{8,10},{9,11},{10,... | collective-permute-start | bytes 786440 | tf_op jit(solution)/shard_map/ppermute | solution.py:30
  26.3 14.8 %collective-permute-start.7 = (bf16[2,128,512]{2,1,0:T(8,128)(2,1)S(1)}, bf16[2,128,512]{2,1,0:T(8,128)(2,1)S(1)}, u32[]{:S(2)}, u32[]{:S(2)}) collective-permute-start(bf16[2,128,512]{2,1,0:T(8,128)(2,1)S(1)} %join.14.a_ref), channel_id=1, source_target_pairs={{0,8},{8,0},{16,24},{24,16},{1,9},{9,1},{17,25},{25,17},{2,10},{10... | collective-permute-start | bytes 786440 | tf_op jit(solution)/shard_map/ppermute | solution.py:30
  38.0 11.4 %collective-permute-start.13 = (bf16[4,128,512]{2,1,0:T(8,128)(2,1)S(1)}, bf16[4,128,512]{2,1,0:T(8,128)(2,1)}, u32[]{:S(2)}, u32[]{:S(2)}) collective-permute-start(bf16[4,128,512]{2,1,0:T(8,128)(2,1)S(1)} %join.17.refs_2_), channel_id=1, source_target_pairs={{0,2},{1,3},{2,0},{3,1},{4,6},{5,7},{6,4},{7,5},{8,10},{9,11},{10,... | collective-permute-start | bytes 1572872 | tf_op jit(solution)/shard_map/ppermute | solution.py:30
  41.2 12.6 %collective-permute-start.12 = (bf16[4,128,512]{2,1,0:T(8,128)(2,1)S(1)}, bf16[4,128,512]{2,1,0:T(8,128)(2,1)}, u32[]{:S(2)}, u32[]{:S(2)}) collective-permute-start(bf16[4,128,512]{2,1,0:T(8,128)(2,1)S(1)} %join.15.refs_1_), channel_id=1, source_target_pairs={{0,1},{1,0},{2,3},{3,2},{4,5},{5,4},{6,7},{7,6},{8,9},{9,8},{10,11... | collective-permute-start | bytes 1572872 | tf_op jit(solution)/shard_map/ppermute | solution.py:30
  41.6 12.3 %collective-permute-start.10 = (bf16[4,128,512]{2,1,0:T(8,128)(2,1)S(1)}, bf16[4,128,512]{2,1,0:T(8,128)(2,1)}, u32[]{:S(2)}, u32[]{:S(2)}) collective-permute-start(bf16[4,128,512]{2,1,0:T(8,128)(2,1)S(1)} %join.13.refs_0_), channel_id=1, source_target_pairs={{0,8},{8,0},{16,24},{24,16},{1,9},{9,1},{17,25},{25,17},{2,10},{10... | collective-permute-start | bytes 1572872 | tf_op jit(solution)/shard_map/ppermute | solution.py:30
  53.9 19.1 %collective-permute-start.14 = (bf16[112,1536]{1,0:T(8,128)(2,1)S(1)}, bf16[112,1536]{1,0:T(8,128)(2,1)S(1)}, u32[]{:S(2)}, u32[]{:S(2)}) collective-permute-start(bf16[112,1536]{1,0:T(8,128)(2,1)S(1)} %get-tuple-element.76), channel_id=1, source_target_pairs={{0,16},{4,20},{8,24},{12,28},{16,0},{20,4},{24,8},{28,12},{1,17},{... | collective-permute-start | bytes 1032200 | tf_op jit(solution)/shard_map/ppermute | solution.py:40
  73.0 21.8 %collective-permute-start.19 = (bf16[4,128,512]{2,1,0:T(8,128)(2,1)S(1)}, bf16[4,128,512]{2,1,0:T(8,128)(2,1)S(1)}, u32[]{:S(2)}, u32[]{:S(2)}) collective-permute-start(bf16[4,128,512]{2,1,0:T(8,128)(2,1)S(1)} %get-tuple-element.86), channel_id=1, source_target_pairs={{0,1},{1,0},{2,3},{3,2},{4,5},{5,4},{6,7},{7,6},{8,9},{9,8},{10,11... | collective-permute-start | bytes 1572872 | tf_op jit(solution)/shard_map/ppermute | solution.py:30
  74.5 20.5 %collective-permute-start.16 = (bf16[4,128,512]{2,1,0:T(8,128)(2,1)S(1)}, bf16[4,128,512]{2,1,0:T(8,128)(2,1)S(1)}, u32[]{:S(2)}, u32[]{:S(2)}) collective-permute-start(bf16[4,128,512]{2,1,0:T(8,128)(2,1)S(1)} %get-tuple-element.82), channel_id=1, source_target_pairs={{0,8},{8,0},{16,24},{24,16},{1,9},{9,1},{17,25},{25,17},{2,10},{10... | collective-permute-start | bytes 1572872 | tf_op jit(solution)/shard_map/ppermute | solution.py:30
  76.3 18.9 %collective-permute-start.17 = (bf16[4,128,512]{2,1,0:T(8,128)(2,1)S(1)}, bf16[4,128,512]{2,1,0:T(8,128)(2,1)S(1)}, u32[]{:S(2)}, u32[]{:S(2)}) collective-permute-start(bf16[4,128,512]{2,1,0:T(8,128)(2,1)S(1)} %get-tuple-element.83), channel_id=1, source_target_pairs={{0,2},{1,3},{2,0},{3,1},{4,6},{5,7},{6,4},{7,5},{8,10},{9,11},{10,... | collective-permute-start | bytes 1572872 | tf_op jit(solution)/shard_map/ppermute | solution.py:30
  95.1 11.2 %collective-permute-start.23 = (bf16[2,128,512]{2,1,0:T(8,128)(2,1)S(1)}, bf16[2,128,512]{2,1,0:T(8,128)(2,1)S(1)}, u32[]{:S(2)}, u32[]{:S(2)}) collective-permute-start(bf16[2,128,512]{2,1,0:T(8,128)(2,1)S(1)} %slice.317), channel_id=1, source_target_pairs={{0,8},{8,0},{16,24},{24,16},{1,9},{9,1},{17,25},{25,17},{2,10},{10... | collective-permute-start | bytes 786440 | tf_op jit(solution)/shard_map/ppermute | solution.py:30
  112.8 11.3 %collective-permute-start.35 = (bf16[64,512]{1,0:T(8,128)(2,1)S(1)}, bf16[64,512]{1,0:T(8,128)(2,1)S(1)}, u32[]{:S(2)}, u32[]{:S(2)}) collective-permute-start(bf16[64,512]{1,0:T(8,128)(2,1)S(1)} %get-tuple-element.100), channel_id=1, source_target_pairs={{0,16},{4,20},{8,24},{12,28},{16,0},{20,4},{24,8},{28,12},{1,17},{... | collective-permute-start | bytes 196616 | tf_op jit(solution)/shard_map/ppermute | solution.py:40
  115.8 16.8 %collective-permute-start.36 = (bf16[64,512]{1,0:T(8,128)(2,1)S(1)}, bf16[64,512]{1,0:T(8,128)(2,1)S(1)}, u32[]{:S(2)}, u32[]{:S(2)}) collective-permute-start(bf16[64,512]{1,0:T(8,128)(2,1)S(1)} %get-tuple-element.101), channel_id=1, source_target_pairs={{0,20},{4,16},{8,28},{12,24},{16,4},{20,0},{24,12},{28,8},{1,21},{... | collective-permute-start | bytes 196616 | tf_op jit(solution)/shard_map/ppermute | solution.py:40
  116.2 13.6 %collective-permute-start.31 = (bf16[64,512]{1,0:T(8,128)(2,1)S(1)}, bf16[64,512]{1,0:T(8,128)(2,1)S(1)}, u32[]{:S(2)}, u32[]{:S(2)}) collective-permute-start(bf16[64,512]{1,0:T(8,128)(2,1)S(1)} %get-tuple-element.96), channel_id=1, source_target_pairs={{0,16},{4,20},{8,24},{12,28},{16,0},{20,4},{24,8},{28,12},{1,17},{... | collective-permute-start | bytes 196616 | tf_op jit(solution)/shard_map/ppermute | solution.py:40
  118.9 13.7 %collective-permute-start.32 = (bf16[64,512]{1,0:T(8,128)(2,1)S(1)}, bf16[64,512]{1,0:T(8,128)(2,1)S(1)}, u32[]{:S(2)}, u32[]{:S(2)}) collective-permute-start(bf16[64,512]{1,0:T(8,128)(2,1)S(1)} %get-tuple-element.97), channel_id=1, source_target_pairs={{0,20},{4,16},{8,28},{12,24},{16,4},{20,0},{24,12},{28,8},{1,21},{... | collective-permute-start | bytes 196616 | tf_op jit(solution)/shard_map/ppermute | solution.py:40
  119.1 13.5 %collective-permute-start.33 = (bf16[64,512]{1,0:T(8,128)(2,1)S(1)}, bf16[64,512]{1,0:T(8,128)(2,1)S(1)}, u32[]{:S(2)}, u32[]{:S(2)}) collective-permute-start(bf16[64,512]{1,0:T(8,128)(2,1)S(1)} %get-tuple-element.98), channel_id=1, source_target_pairs={{0,16},{4,20},{8,24},{12,28},{16,0},{20,4},{24,8},{28,12},{1,17},{... | collective-permute-start | bytes 196616 | tf_op jit(solution)/shard_map/ppermute | solution.py:40
  134.0 11.5 %collective-permute-start.37 = (bf16[3,64,512]{2,1,0:T(8,128)(2,1)S(1)}, bf16[3,64,512]{2,1,0:T(8,128)(2,1)S(1)}, u32[]{:S(2)}, u32[]{:S(2)}) collective-permute-start(bf16[3,64,512]{2,1,0:T(8,128)(2,1)S(1)} %pad_maximum_fusion.1), channel_id=1, source_target_pairs={{0,16},{4,20},{8,24},{12,28},{16,0},{20,4},{24,8},{28,12},{1,17},{... | collective-permute-start | bytes 589832 | tf_op jit(solution)/shard_map/ppermute | solution.py:40
  145.5 12.5 %collective-permute-start.43 = (bf16[2,128,512]{2,1,0:T(8,128)(2,1)S(1)}, bf16[2,128,512]{2,1,0:T(8,128)(2,1)S(1)}, u32[]{:S(2)}, u32[]{:S(2)}) collective-permute-start(bf16[2,128,512]{2,1,0:T(8,128)(2,1)S(1)} %join.20.a_ref), channel_id=1, source_target_pairs={{0,8},{8,0},{16,24},{24,16},{1,9},{9,1},{17,25},{25,17},{2,10},{10... | collective-permute-start | bytes 786440 | tf_op jit(solution)/shard_map/ppermute | solution.py:30
  146.6 11.8 %collective-permute-start.38 = (bf16[3,64,512]{2,1,0:T(8,128)(2,1)S(1)}, bf16[3,64,512]{2,1,0:T(8,128)(2,1)S(1)}, u32[]{:S(2)}, u32[]{:S(2)}) collective-permute-start(bf16[3,64,512]{2,1,0:T(8,128)(2,1)S(1)} %pad_maximum_fusion), channel_id=1, source_target_pairs={{0,16},{4,20},{8,24},{12,28},{16,0},{20,4},{24,8},{28,12},{1,17},{... | collective-permute-start | bytes 589832 | tf_op jit(solution)/shard_map/ppermute | solution.py:40
  150.3 12.2 %collective-permute-start.47 = (bf16[4,128,512]{2,1,0:T(8,128)(2,1)S(1)}, bf16[4,128,512]{2,1,0:T(8,128)(2,1)S(1)}, u32[]{:S(2)}, u32[]{:S(2)}) collective-permute-start(bf16[4,128,512]{2,1,0:T(8,128)(2,1)S(1)} %join.23.refs_2_), channel_id=1, source_target_pairs={{0,2},{1,3},{2,0},{3,1},{4,6},{5,7},{6,4},{7,5},{8,10},{9,11},{10,... | collective-permute-start | bytes 1572872 | tf_op jit(solution)/shard_map/ppermute | solution.py:30
  158.0 13.1 %collective-permute-start.46 = (bf16[4,128,512]{2,1,0:T(8,128)(2,1)S(1)}, bf16[4,128,512]{2,1,0:T(8,128)(2,1)S(1)}, u32[]{:S(2)}, u32[]{:S(2)}) collective-permute-start(bf16[4,128,512]{2,1,0:T(8,128)(2,1)S(1)} %join.21.refs_1_), channel_id=1, source_target_pairs={{0,1},{1,0},{2,3},{3,2},{4,5},{5,4},{6,7},{7,6},{8,9},{9,8},{10,11... | collective-permute-start | bytes 1572872 | tf_op jit(solution)/shard_map/ppermute | solution.py:30
  158.4 13.1 %collective-permute-start.44 = (bf16[4,128,512]{2,1,0:T(8,128)(2,1)S(1)}, bf16[4,128,512]{2,1,0:T(8,128)(2,1)S(1)}, u32[]{:S(2)}, u32[]{:S(2)}) collective-permute-start(bf16[4,128,512]{2,1,0:T(8,128)(2,1)S(1)} %join.19.refs_0_), channel_id=1, source_target_pairs={{0,8},{8,0},{16,24},{24,16},{1,9},{9,1},{17,25},{25,17},{2,10},{10... | collective-permute-start | bytes 1572872 | tf_op jit(solution)/shard_map/ppermute | solution.py:30
  158.5 33.5 %collective-permute-start.49 = (f32[8,512]{1,0:T(8,128)S(1)}, f32[8,512]{1,0:T(8,128)S(1)}, u32[]{:S(2)}, u32[]{:S(2)}) collective-permute-start(f32[8,512]{1,0:T(8,128)S(1)} %get-tuple-element.111), channel_id=1, source_target_pairs={{0,16},{4,20},{8,24},{12,28},{16,0},{20,4},{24,8},{28,12},{1,17},{... | collective-permute-start | bytes 49160 | tf_op jit(solution)/shard_map/ppermute | solution.py:40
  171.5 17.1 %collective-permute-start.48 = (bf16[112,1536]{1,0:T(8,128)(2,1)S(1)}, bf16[112,1536]{1,0:T(8,128)(2,1)S(1)}, u32[]{:S(2)}, u32[]{:S(2)}) collective-permute-start(bf16[112,1536]{1,0:T(8,128)(2,1)S(1)} %get-tuple-element.110), channel_id=1, source_target_pairs={{0,16},{4,20},{8,24},{12,28},{16,0},{20,4},{24,8},{28,12},{1,17},{... | collective-permute-start | bytes 1032200 | tf_op jit(solution)/shard_map/ppermute | solution.py:40
  188.6 12.9 %collective-permute-start.52 = (bf16[4,128,512]{2,1,0:T(8,128)(2,1)S(1)}, bf16[4,128,512]{2,1,0:T(8,128)(2,1)S(1)}, u32[]{:S(2)}, u32[]{:S(2)}) collective-permute-start(bf16[4,128,512]{2,1,0:T(8,128)(2,1)S(1)} %get-tuple-element.116), channel_id=1, source_target_pairs={{0,8},{8,0},{16,24},{24,16},{1,9},{9,1},{17,25},{25,17},{2,10},{10... | collective-permute-start | bytes 1572872 | tf_op jit(solution)/shard_map/ppermute | solution.py:30
  190.7 11.9 %collective-permute-start.53 = (bf16[4,128,512]{2,1,0:T(8,128)(2,1)S(1)}, bf16[4,128,512]{2,1,0:T(8,128)(2,1)S(1)}, u32[]{:S(2)}, u32[]{:S(2)}) collective-permute-start(bf16[4,128,512]{2,1,0:T(8,128)(2,1)S(1)} %get-tuple-element.118), channel_id=1, source_target_pairs={{0,2},{1,3},{2,0},{3,1},{4,6},{5,7},{6,4},{7,5},{8,10},{9,11},{10,... | collective-permute-start | bytes 1572872 | tf_op jit(solution)/shard_map/ppermute | solution.py:30
  196.0 12.1 %collective-permute-start.55 = (bf16[4,128,512]{2,1,0:T(8,128)(2,1)S(1)}, bf16[4,128,512]{2,1,0:T(8,128)(2,1)S(1)}, u32[]{:S(2)}, u32[]{:S(2)}) collective-permute-start(bf16[4,128,512]{2,1,0:T(8,128)(2,1)S(1)} %get-tuple-element.122), channel_id=1, source_target_pairs={{0,1},{1,0},{2,3},{3,2},{4,5},{5,4},{6,7},{7,6},{8,9},{9,8},{10,11... | collective-permute-start | bytes 1572872 | tf_op jit(solution)/shard_map/ppermute | solution.py:30
  (38 other events, 333.9 us)

commit v3 on v2

v3 whole, which is shorter than its diff:
```python
import functools

import jax
import jax.numpy as jnp
from jax import lax
from jax.experimental import pallas as pl
from jax.experimental.pallas import tpu as pltpu
from jax.sharding import PartitionSpec as P

D = 6144
E = 8
EXP_WIN = 2
SEQ_LEN = 128
CAP = 64
IN_PARTS = 3
OUT_PARTS = 3

norm_eps = 1e-05
VMEM_BYTES = 10 * 1024 * 1024

bf16 = jnp.bfloat16
f32 = jnp.float32


def params():
    return pltpu.CompilerParams(vmem_limit_bytes=VMEM_BYTES)


def cuts(feats, parts):
    ends = [feats // 128 * p // parts * 128 for p in range(parts + 1)]
    return list(zip(ends[:-1], ends[1:]))


def in_cuts(feats):
    units = feats // 128
    first = max(1, units // 6)
    second = (units - first) // 2
    ends = [0, first * 128, (first + second) * 128, feats]
    return list(zip(ends[:-1], ends[1:]))


def swapped(x, dim):
    axis, bit = dim
    return lax.ppermute(x, axis, [(i, i ^ (1 << bit)) for i in range(lax.axis_size(axis))])


def ahead(x, by, cross=False):
    sections, cores = lax.axis_size("section"), lax.axis_size("expert")
    perm = []
    for s in range(sections):
        for c in range(cores):
            there = (s + by) % sections * cores + (c ^ 1 if cross else c)
            perm.append((s * cores + c, there))
    return lax.ppermute(x, ("section", "expert"), perm)


def nt(a, b):
    return lax.dot_general(a, b, (((1,), (1,)), ((), ())), preferred_element_type=f32)


def tn(a, b):
    return lax.dot_general(a, b, (((0,), (0,)), ((), ())), preferred_element_type=f32)


def one_hot_rows(slot_row):
    rows = slot_row.shape[1]
    places = lax.broadcasted_iota(jnp.int32, (CAP, rows), 0).astype(f32)
    return places == slot_row


def prologue_kernel(core, lens, ids_ref, x_ref, slots_ref, own_ref, other_ref):
    rows = ids_ref.shape[1]
    groups_len = rows // SEQ_LEN
    place = lax.broadcasted_iota(jnp.int32, (1, rows), 1)
    me = core[0]
    named = []
    for step in range(2):
        limit = jnp.zeros((1, rows), jnp.int32)
        for q in range(groups_len):
            limit = jnp.where(place // SEQ_LEN == q, lens[step * groups_len + q], limit)
        live = place % SEQ_LEN < limit
        first = ids_ref[2 * step : 2 * step + 1, :]
        second = ids_ref[2 * step + 1 : 2 * step + 2, :]
        for which in range(2):
            expert = me if which == 0 else 1 - me
            hit = ((first == expert) | (second == expert)) & live
            named.append(jnp.where(hit, 1.0, 0.0))
    named.append(jnp.zeros((4, rows), f32))
    named = jnp.concatenate(named, axis=0)
    r = lax.broadcasted_iota(jnp.int32, (rows, rows), 0)
    c = lax.broadcasted_iota(jnp.int32, (rows, rows), 1)
    before = jnp.where(r < c, 1.0, 0.0).astype(bf16)
    earlier = jnp.dot(named.astype(bf16), before, preferred_element_type=f32)
    slots = jnp.where((named > 0.5) & (earlier < CAP), earlier, -1.0)
    slots_ref[...] = slots
    table = jnp.concatenate(
        [one_hot_rows(slots[0:1]), one_hot_rows(slots[1:2])], axis=0
    )
    table = jnp.where(table, 1.0, 0.0).astype(bf16)
    for a, b in cuts(x_ref.shape[1], OUT_PARTS):
        got = jnp.dot(table, x_ref[:, a:b], preferred_element_type=f32).astype(bf16)
        own_ref[:, a:b] = got[:CAP]
        other_ref[:, a:b] = got[CAP:]


def prologue(core, lens, ids_rows, x):
    rows, feats = x.shape
    piece = jax.ShapeDtypeStruct((CAP, feats), bf16)
    return pl.pallas_call(
        prologue_kernel,
        name="prologue",
        out_shape=(jax.ShapeDtypeStruct((8, rows), f32), piece, piece),
        in_specs=[
            pl.BlockSpec(memory_space=pltpu.SMEM),
            pl.BlockSpec(memory_space=pltpu.SMEM),
            pl.BlockSpec(memory_space=pltpu.VMEM),
            pl.BlockSpec(memory_space=pltpu.VMEM),
        ],
        compiler_params=params(),
    )(core, lens, ids_rows, x)


def in_three(v):
    first = v.astype(bf16)
    rest = v - first.astype(f32)
    second = rest.astype(bf16)
    return first, second, (rest - second.astype(f32)).astype(bf16)


def row_stats(x_bf, gain, router_t):
    parts = jnp.concatenate(in_three(router_t * gain), axis=0)
    got = nt(parts, x_bf)
    logits = (got[16:] + got[8:16]) + got[:8]
    xf = x_bf.astype(f32)
    squares = xf[:, :128] * xf[:, :128]
    for c in range(128, xf.shape[1], 128):
        squares = squares + xf[:, c : c + 128] * xf[:, c : c + 128]
    ones = jnp.ones((8, 128), bf16)
    first, second, third = in_three(squares)
    return logits, (nt(ones, third) + nt(ones, second)) + nt(ones, first)


def stats_kernel(x_ref, gain_ref, router_ref, out_ref):
    logits, sq = row_stats(x_ref[...], gain_ref[...], router_ref[...])
    out_ref[:8] = logits
    out_ref[8:] = sq


def stats(x, gain_row, router_t):
    return pl.pallas_call(
        stats_kernel,
        name="stats",
        out_shape=jax.ShapeDtypeStruct((16, x.shape[0]), f32),
        compiler_params=params(),
    )(x, gain_row, router_t)


def row_weights(stat, first, second, me):
    inv = lax.rsqrt(stat[8:9] / D + norm_eps)
    logits = stat[:8] * inv
    names = lax.broadcasted_iota(jnp.int32, logits.shape, 0)
    a = jnp.sum(jnp.where(names == first, logits, 0.0), axis=0, keepdims=True)
    b = jnp.sum(jnp.where(names == second, logits, 0.0), axis=0, keepdims=True)
    wa = jax.nn.sigmoid(a - b)
    wb = jax.nn.sigmoid(b - a)
    out = []
    for which in range(2):
        expert = me if which == 0 else 1 - me
        out.append(jnp.where(first == expert, wa, 0.0) + jnp.where(second == expert, wb, 0.0))
    return out


def weight_table(weights, slots):
    parts = []
    for w, slot in zip(weights, slots):
        hot = one_hot_rows(slot)
        hi = w.astype(bf16).astype(f32)
        lo = w - hi
        parts.append(jnp.where(hot, hi, 0.0).astype(bf16))
        parts.append(jnp.where(hot, lo, 0.0).astype(bf16))
    return jnp.concatenate(parts, axis=0)


def stacked(own, other):
    return jnp.concatenate([own, own, other, other], axis=0)


def prepare_kernel(core, stat_ref, ids_ref, slots_ref, next_ref, x_ref, aux_ref, base_ref, mix_ref):
    me = core[0]
    w_own, w_other = row_weights(stat_ref[...], ids_ref[0:1, :], ids_ref[1:2, :], me)
    s_own, s_other = slots_ref[0:1, :], slots_ref[1:2, :]
    aux_ref[...] = jnp.concatenate(
        [w_own, w_other, s_own, s_other, jnp.zeros((4, w_own.shape[1]), f32)], axis=0
    )
    table = weight_table((w_own, w_other), (s_own, s_other))
    pick = jnp.concatenate([one_hot_rows(next_ref[2:3, :]), one_hot_rows(next_ref[3:4, :])], axis=0)
    pick = jnp.where(pick, 1.0, 0.0).astype(bf16)
    mix_ref[...] = nt(pick, table).astype(bf16)
    for a, b in cuts(x_ref.shape[1], OUT_PARTS):
        got = jnp.dot(pick, x_ref[:, a:b], preferred_element_type=f32)
        base_ref[:, a:b] = got.astype(bf16)


def prepare(core, stat, ids_rows, slots, next_slots, x):
    rows, feats = x.shape
    vmem = pl.BlockSpec(memory_space=pltpu.VMEM)
    return pl.pallas_call(
        prepare_kernel,
        name="prepare",
        out_shape=(
            jax.ShapeDtypeStruct((8, rows), f32),
            jax.ShapeDtypeStruct((2 * CAP, feats), bf16),
            jax.ShapeDtypeStruct((2 * CAP, 4 * CAP), bf16),
        ),
        in_specs=[pl.BlockSpec(memory_space=pltpu.SMEM)] + [vmem] * 5,
        compiler_params=params(),
    )(core, stat, ids_rows, slots, next_slots, x)


def repick_kernel(mix_ref, base_ref, *refs):
    own, other = refs[:OUT_PARTS], refs[OUT_PARTS : 2 * OUT_PARTS]
    to_own_ref, to_other_ref, own_ref, other_ref = refs[2 * OUT_PARTS :]
    for p, (a, b) in enumerate(cuts(base_ref.shape[1], OUT_PARTS)):
        rows = jnp.dot(
            mix_ref[...], stacked(own[p][...], other[p][...]), preferred_element_type=f32
        )
        rows = (base_ref[:, a:b].astype(f32) + rows).astype(bf16)
        to_own_ref[:, a:b] = rows[:CAP]
        to_other_ref[:, a:b] = rows[CAP:]
        own_ref[:, a:b] = own[p][...]
        other_ref[:, a:b] = other[p][...]


def repick(mix, base, own, other):
    piece = jax.ShapeDtypeStruct((CAP, base.shape[1]), bf16)
    return pl.pallas_call(
        repick_kernel, name="repick", out_shape=(piece,) * 4, compiler_params=params()
    )(mix, base, *own, *other)


def lay_kernel(own_ref, other_ref, *outs):
    for out, (a, b) in zip(outs, in_cuts(own_ref.shape[1])):
        out[0, :CAP] = own_ref[:, a:b]
        out[0, CAP:] = other_ref[:, a:b]


def lay(own, other):
    return pl.pallas_call(
        lay_kernel,
        name="lay",
        out_shape=[
            jax.ShapeDtypeStruct((1, 2 * CAP, b - a), bf16)
            for a, b in in_cuts(own.shape[1])
        ],
        compiler_params=params(),
    )(own, other)


def between_kernel(x_ref, aux_ref, own_ref, other_ref, gain_ref, router_ref, new_ref, stat_ref):
    table = weight_table((aux_ref[0:1, :], aux_ref[1:2, :]), (aux_ref[2:3, :], aux_ref[3:4, :]))
    logits = None
    for a, b in cuts(x_ref.shape[1], OUT_PARTS):
        cols = slice(a, b)
        mixed = tn(table, stacked(own_ref[:, cols], other_ref[:, cols]))
        new = (x_ref[:, cols].astype(f32) + mixed).astype(bf16)
        new_ref[:, cols] = new
        l, s = row_stats(new, gain_ref[:, cols], router_ref[:, cols])
        logits = l if logits is None else logits + l
        sq = s if a == 0 else sq + s
    stat_ref[:8] = logits
    stat_ref[8:] = sq


def between(x, aux, own, other, gain_row, router_t):
    return pl.pallas_call(
        between_kernel,
        name="between",
        out_shape=(
            jax.ShapeDtypeStruct(x.shape, bf16),
            jax.ShapeDtypeStruct((16, x.shape[0]), f32),
        ),
        compiler_params=params(),
    )(x, aux, own, other, gain_row, router_t)


def last_kernel(core, x_ref, stat_ref, ids_ref, slots_ref, *refs):
    own, other, out_ref = refs[:OUT_PARTS], refs[OUT_PARTS : 2 * OUT_PARTS], refs[-1]
    me = core[0]
    weights = row_weights(stat_ref[...], ids_ref[2:3, :], ids_ref[3:4, :], me)
    table = weight_table(weights, (slots_ref[2:3, :], slots_ref[3:4, :]))
    for p, (a, b) in enumerate(cuts(x_ref.shape[1], OUT_PARTS)):
        cols = slice(a, b)
        mixed = tn(table, stacked(own[p][...], other[p][...]))
        out_ref[:, cols] = (x_ref[:, cols].astype(f32) + mixed).astype(bf16)


def last(core, x, stat, ids_rows, slots, own, other):
    vmem = pl.BlockSpec(memory_space=pltpu.VMEM)
    return pl.pallas_call(
        last_kernel,
        name="last",
        out_shape=jax.ShapeDtypeStruct(x.shape, bf16),
        in_specs=[pl.BlockSpec(memory_space=pltpu.SMEM)] + [vmem] * (4 + 2 * OUT_PARTS),
        compiler_params=params(),
    )(core, x, stat, ids_rows, slots, *own, *other)


def out_orders(slices):
    bits = slices.bit_length() - 1
    dims = [("tensor", b) for b in range(bits)] + [("section", 0)]
    n = len(dims)
    return [[dims[(i + p * max(1, n // OUT_PARTS)) % n] for i in range(n)] for p in range(OUT_PARTS)]


def tied(x, *before):
    return lax.optimization_barrier((x, before))[0]


def join_kernel(a_ref, b_ref, out_ref):
    half = a_ref.shape[0]
    out_ref[:half] = a_ref[...]
    out_ref[half:] = b_ref[...]


def join(a, b):
    return pl.pallas_call(
        join_kernel,
        name="join",
        out_shape=jax.ShapeDtypeStruct((2 * a.shape[0],) + a.shape[1:], a.dtype),
        compiler_params=params(),
    )(a, b)


def exchanged(values, orders, k, last, came, deps):
    out = []
    for p, order in enumerate(orders):
        before = list(deps)
        if came is not None:
            before += [came[q] for q in range(len(orders)) if orders[q][last] == order[k]]
        out.append(swapped(tied(values[p], *before) if before else values[p], order[k]))
    return out


def gather_round(held, came, orders, k, deps=()):
    if k > 0:
        held = [join(h, c) for h, c in zip(held, came)]
    return held, exchanged(held, orders, k, k - 1, came, deps)


def sum_cube(keep, send, orders, before):
    keep = [k.astype(f32) for k in keep]
    rounds = len(orders[0])
    came = first = None
    for k in range(rounds - 1, -1, -1):
        came = exchanged(send, orders, k, k + 1, came, before.get(rounds - 1 - k, ()))
        first = came if first is None else first
        total = [a + c.astype(f32) for a, c in zip(keep, came)]
        half = total[0].shape[0] // 2
        if k > 0:
            send = [t[half:].astype(bf16) for t in total]
            keep = [t[:half] for t in total]
    return [t[0].astype(bf16) for t in total], first


def block_place(order, r, z):
    place = 0
    for k, (axis, bit) in enumerate(order):
        on = z if axis == "section" else (r >> bit) & 1
        place = place + (on << k)
    return place


AHEAD = 8
GROUP = 4


def units_of(orders, half, slices, early):
    out = []
    for p, order in enumerate(orders):
        for r in range(slices):
            here = all(block_place(order, r, z) < half for z in range(2))
            if here == early:
                out.append((p, r))
    return out


class Stream:
    def __init__(self):
        self.copies = []

    def add(self, src, dst, sem):
        self.copies.append(pltpu.make_async_copy(src, dst, sem))
        return len(self.copies) - 1

    def begin(self):
        for copy in self.copies[:AHEAD]:
            copy.start()

    def arrived(self, group):
        for i in group:
            self.copies[i].wait()
            if i + AHEAD < len(self.copies):
                self.copies[i + AHEAD].start()


def packed(units, spans):
    starts = [0]
    for p, _ in units:
        starts.append(starts[-1] + spans[p][1] - spans[p][0])
    return starts


def weight_copies(stream, units, feats, mine, gate_ref, up_ref, in_w, sems):
    spans = in_cuts(feats)
    starts = packed(units, spans)
    places = []
    for which, src in enumerate((gate_ref, up_ref)):
        for u, (p, r) in enumerate(units):
            a, b = spans[p]
            row = pl.multiple_of((mine ^ r) * feats + a, 128)
            dst = in_w.at[which, starts[u] : starts[u + 1]]
            sem = sems.at[len(places)]
            places.append(stream.add(src.at[pl.ds(row, b - a)], dst, sem))
    return places


def scale_rows(units, block, gain_ref, scaled, spans, squares):
    for u, (p, r) in enumerate(units):
        a, b = spans[p]
        x = jnp.concatenate([block(p, r, 0), block(p, r, 1)], axis=0).astype(f32)
        scaled[u, :, : b - a] = (x * gain_ref[r, :, a:b]).astype(bf16)
        for c in range(0, b - a, 128):
            squares = squares + x[:, c : c + 128] * x[:, c : c + 128]
    return squares


def product(stream, places, which, units, spans, scaled, in_w, base, n, tile):
    total = base
    starts = packed(units, spans)
    first = which * len(units)
    for u, (p, r) in enumerate(units):
        a, b = spans[p]
        if n == 0 and u % GROUP == 0:
            stream.arrived(places[first + u : first + min(u + GROUP, len(units))])
        term = jnp.dot(
            scaled[u, :, : b - a],
            in_w[which, starts[u] : starts[u + 1], n : n + tile],
            preferred_element_type=f32,
        )
        total = term if total is None else total + term
    return total


def early_kernel(units, orders, feats, me, *refs):
    early = refs[:IN_PARTS]
    gain_ref, gate_ref, up_ref, gate_out, up_out, squares_out = refs[IN_PARTS : IN_PARTS + 6]
    scaled, in_w, sems = refs[IN_PARTS + 6 :]
    rows = early[0].shape[1]
    spans = in_cuts(feats)
    stream = Stream()
    places = weight_copies(stream, units, feats, me[0], gate_ref, up_ref, in_w, sems)
    stream.begin()

    def block(p, r, z):
        return early[p][block_place(orders[p], r, z)]

    squares = jnp.zeros((2 * rows, 128), f32)
    squares_out[...] = scale_rows(units, block, gain_ref, scaled, spans, squares)
    count = gate_out.shape[1]
    tile = min(512, count)
    for first, out in enumerate((gate_out, up_out)):
        for n in range(0, count, tile):
            out[:, n : n + tile] = product(
                stream, places, first, units, spans, scaled, in_w, None, n, tile
            )


def late_kernel(units, orders, sum_orders, out_spans, feats, me, *refs):
    early, late = refs[:IN_PARTS], refs[IN_PARTS : 2 * IN_PARTS]
    refs = refs[2 * IN_PARTS :]
    gain_ref, gate_in, up_in, squares_in, gate_ref, up_ref, down_ref = refs[:7]
    outs = refs[7 : 7 + 2 * OUT_PARTS]
    scaled, hidden, in_w, down_w, sems, down_sems = refs[7 + 2 * OUT_PARTS :]
    half, rows = late[0].shape[:2]
    slices = half
    mine = me[0]
    spans = in_cuts(feats)
    stream = Stream()
    places = weight_copies(stream, units, feats, mine, gate_ref, up_ref, in_w, sems)
    down_places = []
    work = [(p, r) for p in range(OUT_PARTS) for r in range(slices)]
    for p, r in work:
        a, b = out_spans[p]
        col = pl.multiple_of((mine ^ r) * feats + a, 128)
        src = down_ref.at[:, pl.ds(col, b - a)]
        dst = down_w.at[r, :, a:b]
        down_places.append(stream.add(src, dst, down_sems.at[len(down_places)]))
    stream.begin()

    def block(p, r, z):
        place = block_place(orders[p], r, z)
        return early[p][place] if place < half else late[p][place - half]

    squares = scale_rows(units, block, gain_ref, scaled, spans, squares_in[...])
    inv = lax.rsqrt(jnp.sum(squares, axis=1, keepdims=True) / D + norm_eps)
    count = hidden.shape[1]
    tile = min(512, count)
    for n in range(0, count, tile):
        cols = slice(n, n + tile)
        gate = inv * product(
            stream, places, 0, units, spans, scaled, in_w, gate_in[:, cols], n, tile
        )
        up = inv * product(
            stream, places, 1, units, spans, scaled, in_w, up_in[:, cols], n, tile
        )
        hidden[:, cols] = (gate / (1.0 + jnp.exp(-gate)) * up).astype(bf16)

    for i, (p, r) in enumerate(work):
        if i % GROUP == 0:
            stream.arrived(down_places[i : i + GROUP])
        a, b = out_spans[p]
        out = jnp.dot(hidden[...], down_w[r, :, a:b], preferred_element_type=f32).astype(bf16)
        for z in range(2):
            place = block_place(sum_orders[p], r, z)
            part = out[z * rows : (z + 1) * rows]
            outs[2 * p + place // half][place % half] = part


def expert_params():
    return pltpu.CompilerParams(vmem_limit_bytes=40 * 1024 * 1024)


def experts_early(me, early, gain_all, gate_w, up_w, orders):
    half, rows = early[0].shape[:2]
    feats = gain_all.shape[2]
    count = gate_w.shape[1]
    widest = max(b - a for a, b in in_cuts(feats))
    units = units_of(orders, half, half, True)
    vmem = pl.BlockSpec(memory_space=pltpu.VMEM)
    hbm = pl.BlockSpec(memory_space=pltpu.HBM)
    total = jax.ShapeDtypeStruct((2 * rows, count), f32)
    return pl.pallas_call(
        functools.partial(early_kernel, units, orders, feats),
        name="experts_early",
        out_shape=(total, total, jax.ShapeDtypeStruct((2 * rows, 128), f32)),
        in_specs=[pl.BlockSpec(memory_space=pltpu.SMEM)]
        + [vmem] * (IN_PARTS + 1)
        + [hbm] * 2,
        out_specs=[vmem] * 3,
        scratch_shapes=[
            pltpu.VMEM((len(units), 2 * rows, widest), bf16),
            pltpu.VMEM((2, packed(units, in_cuts(feats))[-1], count), bf16),
            pltpu.SemaphoreType.DMA((2 * len(units),)),
        ],
        compiler_params=expert_params(),
        cost_estimate=pl.CostEstimate(
            flops=2 * 2 * rows * D * count,
            bytes_accessed=2 * D * count,
            transcendentals=0,
        ),
    )(me, *early, gain_all, gate_w, up_w)


def experts_late(
    me, early, late, gain_all, sums, gate_w, up_w, down_w, orders, sum_orders, out_spans
):
    half, rows = late[0].shape[:2]
    feats = gain_all.shape[2]
    count = gate_w.shape[1]
    widest = max(b - a for a, b in in_cuts(feats))
    units = units_of(orders, half, half, False)
    vmem = pl.BlockSpec(memory_space=pltpu.VMEM)
    hbm = pl.BlockSpec(memory_space=pltpu.HBM)
    outs = pl.pallas_call(
        functools.partial(late_kernel, units, orders, sum_orders, out_spans, feats),
        name="experts_late",
        out_shape=[
            jax.ShapeDtypeStruct((half, rows, b - a), bf16)
            for a, b in out_spans
            for _ in range(2)
        ],
        in_specs=[pl.BlockSpec(memory_space=pltpu.SMEM)]
        + [vmem] * (2 * IN_PARTS + 4)
        + [hbm] * 3,
        out_specs=[vmem] * (2 * OUT_PARTS),
        scratch_shapes=[
            pltpu.VMEM((len(units), 2 * rows, widest), bf16),
            pltpu.VMEM((2 * rows, count), bf16),
            pltpu.VMEM((2, packed(units, in_cuts(feats))[-1], count), bf16),
            pltpu.VMEM((half, count, feats), bf16),
            pltpu.SemaphoreType.DMA((2 * len(units),)),
            pltpu.SemaphoreType.DMA((half * OUT_PARTS,)),
        ],
        compiler_params=expert_params(),
        cost_estimate=pl.CostEstimate(
            flops=2 * 2 * rows * D * count * 2,
            bytes_accessed=4 * D * count,
            transcendentals=2 * rows * count,
        ),
    )(me, *early, *late, gain_all, *sums, gate_w, up_w, down_w)
    return outs[0::2], outs[1::2]


def tensor_sum(stat):
    for b in range(lax.axis_size("tensor").bit_length() - 1):
        stat = stat + swapped(stat, ("tensor", b))
    return stat


def first_sums(stat, gain_row):
    rows, feats = stat.shape[1], gain_row.shape[1]
    lines = -(-feats // rows)
    gains = jnp.pad(gain_row[0], (0, lines * rows - feats)).reshape(lines, rows)
    steps = []
    for b in range(lax.axis_size("tensor").bit_length() - 1):
        count = 9 + gains.shape[0]
        parcel = jnp.concatenate([stat[:9], gains, jnp.zeros((-count % 8, rows), f32)])
        came = swapped(parcel, ("tensor", b))
        stat = stat[:9] + came[:9]
        gains = jnp.concatenate([gains, came[9:count]])
        steps.append(came)
    gains = gains.reshape(lax.axis_size("tensor"), 1, lines * rows)[:, :, :feats]
    return stat, gains, steps


def on_device(tokens, norm_gain, router, w_gate, w_up, w_down, expert_ids, lengths):
    sections = lax.axis_size("section")
    slices = lax.axis_size("tensor")
    section = lax.axis_index("section")
    core = lax.axis_index("expert").astype(jnp.int32)[None]
    me = lax.axis_index("tensor").astype(jnp.int32)[None]
    layer = section // 2
    rows, feats = tokens.shape
    across = ("expert", 0)

    gain_row = lax.dynamic_index_in_dim(norm_gain, layer, 0, keepdims=True)
    router_t = lax.dynamic_index_in_dim(router, layer, 0, keepdims=False).T
    ids_rows = jnp.transpose(expert_ids, (0, 2, 1)).reshape(4, rows)
    lens = jnp.concatenate(
        [
            lax.dynamic_index_in_dim(lengths, section, 0, keepdims=False),
            lax.dynamic_index_in_dim(lengths, (section - 2) % sections, 0, keepdims=False),
        ]
    )
    orders = sum_orders = out_orders(slices)
    rounds = len(orders[0])
    gate_w, up_w, down_w = w_gate[0, 0], w_up[0, 0], w_down[0, 0]
    pieces = []
    begin = 0
    for share in (6, 7, 12, 7):
        pieces.append(tokens[begin : begin + rows * share // 32])
        begin += rows * share // 32

    slots, own, other = prologue(core, lens, ids_rows, tokens)
    next_slots = ahead(slots, -2)
    blocks = lay(own, swapped(other, across))
    held, came = gather_round(blocks, None, orders, 0)
    stat = stats(tied(tokens, *blocks), gain_row, router_t)
    stat, gain_all, steps = first_sums(stat, gain_row)
    for k in range(1, rounds):
        deps = steps[:1] if k == 1 else [next_slots] if k == rounds - 1 else []
        held, came = gather_round(held, came, orders, k, deps)
    far = [ahead(tied(pieces[0], *held), 2)]
    sums = experts_early(me, held, gain_all, gate_w, up_w, orders)
    aux, base, mix = prepare(core, stat, ids_rows, slots, next_slots, tied(tokens, *held))
    far_aux = ahead(aux, 2)

    came = [tied(c, far[0], mix) for c in came]
    far.append(ahead(tied(pieces[1], *came), 2))
    keep, send = experts_late(
        me, held, came, gain_all, sums, gate_w, up_w, down_w, orders, sum_orders, cuts(feats, OUT_PARTS)
    )
    far.append(ahead(tied(pieces[2], *send), 2))
    summed, _ = sum_cube(keep, send, sum_orders, {0: [far[1]], rounds - 1: [far[2]]})

    mine = [s[:CAP] for s in summed]
    theirs = [swapped(s[CAP:], across) for s in summed]
    to_own, to_other, slab_own, slab_other = repick(mix, base, mine, theirs)
    blocks = lay(ahead(to_own, 2), ahead(to_other, 2, True))
    slab_own = ahead(tied(slab_own, *blocks), 2)
    held, came = gather_round(blocks, None, orders, 0)
    for k in range(1, rounds):
        held, came = gather_round(held, came, orders, k, [slab_own] if k == rounds - 1 else [])
    slab_other = ahead(tied(slab_other, *held), 2)
    sums = experts_early(me, held, gain_all, gate_w, up_w, orders)
    came = [tied(c, slab_other) for c in came]
    far.append(ahead(tied(pieces[3], *came), 2))
    keep, send = experts_late(
        me,
        held,
        came,
        gain_all,
        sums,
        gate_w,
        up_w,
        down_w,
        orders,
        sum_orders,
        cuts(feats, OUT_PARTS),
    )

    summed, first = sum_cube(keep, send, sum_orders, {0: [far[3]]})
    far_tokens = jnp.concatenate(far, axis=0)
    far_aux = tied(far_aux, *first)
    state, stat = between(far_tokens, far_aux, slab_own, slab_other, gain_row, router_t)
    stat = tensor_sum(stat)
    mine = [s[:CAP] for s in summed]
    theirs = [swapped(s[CAP:], across) for s in summed]
    return last(core, state, stat, ids_rows, slots, mine, theirs)


def solution(mesh):
    in_specs = (
        P(("section", "expert"), "tensor"),
        P(None, "tensor"),
        P(None, "tensor", None),
        P("section", "expert", None, "tensor"),
        P("section", "expert", None, "tensor"),
        P("section", "expert", "tensor", None),
        P(None, ("section", "expert"), None),
        P(None, "expert"),
    )
    out_specs = P(("section", "expert"), "tensor")
    return jax.shard_map(
        on_device, mesh=mesh, in_specs=in_specs, out_specs=out_specs, check_vma=False
    )
```

time: 227 us -> 212 us (0.934)
  waiting for transfers between devices: 107 us -> 95.6 us
  starting transfers between devices: 68.9 us -> 62 us
  Pallas kernels: 42.9 us -> 46 us
    ppermute x47, waiting for transfers between devices: 78.8 us -> 70.8 us  [swapped(): lax.ppermute(x, axis, [(i, i ^ 1 << bit) for i in range(lax.axis_size(axi...]
    pallas_call x5 -> x7, Pallas kernels: 33.9 us -> 40.1 us  [the longest x2 27.4 us: experts_late(): pl.pallas_call(functools.partial(late_kernel, units, orders, sum_orders,...]
    ppermute x15 -> x10, starting transfers between devices: 19.7 us -> 15.6 us  [ahead(): return lax.ppermute(x, ('section', 'expert'), perm)]
    ppermute x15 -> x10, waiting for transfers between devices: 27.8 us -> 24.8 us  [ahead(): return lax.ppermute(x, ('section', 'expert'), perm)]
    ppermute x47, starting transfers between devices: 49.2 us -> 46.4 us  [swapped(): lax.ppermute(x, axis, [(i, i ^ 1 << bit) for i in range(lax.axis_size(axi...]
  transfers between devices with their start and end apart: 62 -> 57, of which waited for: 39 -> 35; matrix products, arithmetic and copies ran while one was open for 2% -> 2% of each run, Pallas kernels for 18% -> 20%
where the time goes in v3:
time: 212 us
  waiting for transfers between devices  95.6 us (45%)
  starting transfers between devices  62 us (29%)
  Pallas kernels  46 us (22%)
  local copies, waits for them, and re-layouts  5.93 us (3%)
    ppermute x47, waiting for transfers between devices, swapped(): lax.ppermute(x, axis, [(i, i ^ 1 << bit) for i in range(lax.axis_size(axi...  70.8 us
    ppermute x47, starting transfers between devices, swapped(): lax.ppermute(x, axis, [(i, i ^ 1 << bit) for i in range(lax.axis_size(axi...  46.4 us
    pallas_call x2, Pallas kernels, experts_late(): pl.pallas_call(functools.partial(late_kernel, units, orders, sum_orders,...  27.4 us
    ppermute x10, waiting for transfers between devices, ahead(): return lax.ppermute(x, ('section', 'expert'), perm)  24.8 us
    ppermute x10, starting transfers between devices, ahead(): return lax.ppermute(x, ('section', 'expert'), perm)  15.6 us
    pallas_call x2, Pallas kernels, experts_early(): pl.pallas_call(functools.partial(early_kernel, units, orders, feats), nam...  12.4 us
  transfers between devices with their start and end apart: 57, of which 35 were waited for; matrix products, arithmetic and copies ran while one was open for 2% of the time, Pallas kernels for 20%

profile of v3, /device:TPU:0, one launch (start us, length us, event | category | flops | bytes accessed | tf_op | source)
XLA Modules:
  0.0 212.0 jit_solution(11242958729989867837)
XLA Ops:
  5.7 3.0 %collective-permute-start.5 = (bf16[1,128,640]{2,1,0:T(8,128)(2,1)S(1)}, bf16[1,128,640]{2,1,0:T(8,128)(2,1)S(1)}, u32[]{:S(2)}, u32[]{:S(2)}) collective-permute-start(bf16[1,128,640]{2,1,0:T(8,128)(2,1)S(1)} %get-tuple-element.90.a_ref), channel_id=1, source_target_pairs={{0,8},{8,0},{16,24},{24,16},{1,9},{9,1},{17,25},{25,17},{2,10},{10... | collective-permute-start | bytes 491528 | tf_op jit(solution)/shard_map/ppermute | solution.py:44
  13.0 2.6 %collective-permute-start.9 = (f32[8,512]{1,0:T(8,128)S(1)}, f32[8,512]{1,0:T(8,128)S(1)}, u32[]{:S(2)}, u32[]{:S(2)}) collective-permute-start(f32[8,512]{1,0:T(8,128)S(1)} %get-tuple-element.96.slots_ref), channel_id=1, source_target_pairs={{0,16},{4,20},{8,24},{12,28},{16,0},{20,4},{24,8},{28,12},{1,17},{... | collective-permute-start | bytes 49160 | tf_op jit(solution)/shard_map/ppermute | solution.py:54
  20.0 4.4 %collective-permute-done.7.b_ref = bf16[2,128,640]{2,1,0:T(8,128)(2,1)S(1)} collective-permute-done((bf16[2,128,640]{2,1,0:T(8,128)(2,1)S(1)}, bf16[2,128,640]{2,1,0:T(8,128)(2,1)S(1)}, u32[]{:S(2)}, u32[]{:S(2)}) %collective-permute-start.7) | collective-permute-done | bytes 327712 | tf_op jit(solution)/shard_map/ppermute | solution.py:44
  28.1 2.7 %collective-permute-start.8 = (bf16[96,1536]{1,0:T(8,128)(2,1)}, bf16[96,1536]{1,0:T(8,128)(2,1)S(1)}, u32[]{:S(2)}, u32[]{:S(2)}) collective-permute-start(bf16[96,1536]{1,0:T(8,128)(2,1)} %slice.184), channel_id=1, source_target_pairs={{0,16},{4,20},{8,24},{12,28},{16,0},{20,4},{24,8},{28,12},{1,17},{... | collective-permute-start | bytes 884744 | tf_op jit(solution)/shard_map/ppermute | solution.py:54
  32.1 6.2 %experts_early.2 = (f32[256,1024]{1,0:T(8,128)S(1)}, f32[256,1024]{1,0:T(8,128)S(1)}, f32[256,128]{1,0:T(8,128)S(1)}) custom-call(s32[1]{0:T(128)} %bitcast.6.me, bf16[4,128,256]{2,1,0:T(8,128)(2,1)S(1)} %join.13.refs_0_, bf16[4,128,640]{2,1,0:T(8,128)(2,1)S(1)} %join.15.refs_1_, bf16[4,128,640]{2,1,0:T(8,128)(2,1)S(1)} %join.17.refs_2_, ...), custom_call_target="tpu_custom_call" | custom-call | flops 3221225472 | bytes 12582912 | tf_op jit(solution)/shard_map/experts_early/pallas_call | solution.py:542
  38.4 3.6 %collective-permute-done.10.refs_3_ = bf16[4,128,256]{2,1,0:T(8,128)(2,1)S(1)} collective-permute-done((bf16[4,128,256]{2,1,0:T(8,128)(2,1)S(1)}, bf16[4,128,256]{2,1,0:T(8,128)(2,1)S(1)}, u32[]{:S(2)}, u32[]{:S(2)}) %collective-permute-start.10) | collective-permute-done | bytes 262176 | tf_op jit(solution)/shard_map/ppermute | solution.py:44
  42.6 14.3 %experts_late.2 = (bf16[4,128,512]{2,1,0:T(8,128)(2,1)S(1)}, bf16[4,128,512]{2,1,0:T(8,128)(2,1)S(1)}, bf16[4,128,512]{2,1,0:T(8,128)(2,1)S(1)}, bf16[4,128,512]...) custom-call(s32[1]{0:T(128)} %bitcast.6.me, ...), custom_call_target="tpu_custom_call" | custom-call | flops 6442450944 | bytes 25165824 | tf_op jit(solution)/shard_map/experts_late/pallas_call | solution.py:574
  56.9 2.4 %collective-permute-done.14 = bf16[112,1536]{1,0:T(8,128)(2,1)S(1)} collective-permute-done((bf16[112,1536]{1,0:T(8,128)(2,1)S(1)}, bf16[112,1536]{1,0:T(8,128)(2,1)S(1)}, u32[]{:S(2)}, u32[]{:S(2)}) %collective-permute-start.14) | collective-permute-done | bytes 344096 | tf_op jit(solution)/shard_map/ppermute | solution.py:54
  63.3 9.7 %collective-permute-done.17 = bf16[4,128,512]{2,1,0:T(8,128)(2,1)S(1)} collective-permute-done((bf16[4,128,512]{2,1,0:T(8,128)(2,1)S(1)}, bf16[4,128,512]{2,1,0:T(8,128)(2,1)S(1)}, u32[]{:S(2)}, u32[]{:S(2)}) %collective-permute-start.17) | collective-permute-done | bytes 524320 | tf_op jit(solution)/shard_map/ppermute | solution.py:44
  74.9 10.1 %collective-permute-done.16 = bf16[4,128,512]{2,1,0:T(8,128)(2,1)S(1)} collective-permute-done((bf16[4,128,512]{2,1,0:T(8,128)(2,1)S(1)}, bf16[4,128,512]{2,1,0:T(8,128)(2,1)S(1)}, u32[]{:S(2)}, u32[]{:S(2)}) %collective-permute-start.16) | collective-permute-done | bytes 524320 | tf_op jit(solution)/shard_map/ppermute | solution.py:44
  85.1 2.5 %collective-permute-start.22 = (bf16[2,128,512]{2,1,0:T(8,128)(2,1)S(1)}, bf16[2,128,512]{2,1,0:T(8,128)(2,1)S(1)}, u32[]{:S(2)}, u32[]{:S(2)}) collective-permute-start(bf16[2,128,512]{2,1,0:T(8,128)(2,1)S(1)} %slice.336), channel_id=1, source_target_pairs={{0,8},{8,0},{16,24},{24,16},{1,9},{9,1},{17,25},{25,17},{2,10},{10... | collective-permute-start | bytes 786440 | tf_op jit(solution)/shard_map/ppermute | solution.py:44
  89.2 5.4 %collective-permute-done.22 = bf16[2,128,512]{2,1,0:T(8,128)(2,1)S(1)} collective-permute-done((bf16[2,128,512]{2,1,0:T(8,128)(2,1)S(1)}, bf16[2,128,512]{2,1,0:T(8,128)(2,1)S(1)}, u32[]{:S(2)}, u32[]{:S(2)}) %collective-permute-start.22) | collective-permute-done | bytes 262176 | tf_op jit(solution)/shard_map/ppermute | solution.py:44
  97.4 2.6 %collective-permute-done.24 = bf16[1,128,512]{2,1,0:T(8,128)(2,1)S(1)} collective-permute-done((bf16[1,128,512]{2,1,0:T(8,128)(2,1)S(1)}, bf16[1,128,512]{2,1,0:T(8,128)(2,1)S(1)}, u32[]{:S(2)}, u32[]{:S(2)}) %collective-permute-start.24) | collective-permute-done | bytes 131104 | tf_op jit(solution)/shard_map/ppermute | solution.py:44
  102.5 2.7 %collective-permute-start.28 = (bf16[64,1536]{1,0:T(8,128)(2,1)S(1)}, bf16[64,1536]{1,0:T(8,128)(2,1)S(1)}, u32[]{:S(2)}, u32[]{:S(2)}) collective-permute-start(bf16[64,1536]{1,0:T(8,128)(2,1)S(1)} %get-tuple-element.126), channel_id=1, source_target_pairs={{0,16},{4,20},{8,24},{12,28},{16,0},{20,4},{24,8},{28,12},{1,17},{... | collective-permute-start | bytes 589832 | tf_op jit(solution)/shard_map/ppermute | solution.py:54
  105.2 14.4 %collective-permute-done.28.own_ref = bf16[64,1536]{1,0:T(8,128)(2,1)S(1)} collective-permute-done((bf16[64,1536]{1,0:T(8,128)(2,1)S(1)}, bf16[64,1536]{1,0:T(8,128)(2,1)S(1)}, u32[]{:S(2)}, u32[]{:S(2)}) %collective-permute-start.28) | collective-permute-done | bytes 196640 | tf_op jit(solution)/shard_map/ppermute | solution.py:54
  119.7 2.6 %collective-permute-done.29.other_ref = bf16[64,1536]{1,0:T(8,128)(2,1)S(1)} collective-permute-done((bf16[64,1536]{1,0:T(8,128)(2,1)S(1)}, bf16[64,1536]{1,0:T(8,128)(2,1)S(1)}, u32[]{:S(2)}, u32[]{:S(2)}) %collective-permute-start.29) | collective-permute-done | bytes 196640 | tf_op jit(solution)/shard_map/ppermute | solution.py:54
  125.4 3.7 %collective-permute-done.34.b_ref = bf16[1,128,640]{2,1,0:T(8,128)(2,1)S(1)} collective-permute-done((bf16[1,128,640]{2,1,0:T(8,128)(2,1)S(1)}, bf16[1,128,640]{2,1,0:T(8,128)(2,1)S(1)}, u32[]{:S(2)}, u32[]{:S(2)}) %collective-permute-start.34) | collective-permute-done | bytes 163872 | tf_op jit(solution)/shard_map/ppermute | solution.py:44
  134.7 4.0 %collective-permute-done.37.b_ref = bf16[2,128,640]{2,1,0:T(8,128)(2,1)S(1)} collective-permute-done((bf16[2,128,640]{2,1,0:T(8,128)(2,1)S(1)}, bf16[2,128,640]{2,1,0:T(8,128)(2,1)S(1)}, u32[]{:S(2)}, u32[]{:S(2)}) %collective-permute-start.37) | collective-permute-done | bytes 327712 | tf_op jit(solution)/shard_map/ppermute | solution.py:44
  138.7 3.7 %collective-permute-done.33.own_ref = bf16[64,1536]{1,0:T(8,128)(2,1)S(1)} collective-permute-done((bf16[64,1536]{1,0:T(8,128)(2,1)S(1)}, bf16[64,1536]{1,0:T(8,128)(2,1)S(1)}, u32[]{:S(2)}, u32[]{:S(2)}) %collective-permute-start.33) | collective-permute-done | bytes 196640 | tf_op jit(solution)/shard_map/ppermute | solution.py:54
  144.9 3.3 %collective-permute-start.38 = (bf16[64,1536]{1,0:T(8,128)(2,1)S(1)}, bf16[64,1536]{1,0:T(8,128)(2,1)S(1)}, u32[]{:S(2)}, u32[]{:S(2)}) collective-permute-start(bf16[64,1536]{1,0:T(8,128)(2,1)S(1)} %get-tuple-element.138), channel_id=1, source_target_pairs={{0,16},{4,20},{8,24},{12,28},{16,0},{20,4},{24,8},{28,12},{1,17},{... | collective-permute-start | bytes 589832 | tf_op jit(solution)/shard_map/ppermute | solution.py:54
  148.2 6.2 %experts_early.3 = (f32[256,1024]{1,0:T(8,128)S(1)}, f32[256,1024]{1,0:T(8,128)S(1)}, f32[256,128]{1,0:T(8,128)S(1)}) custom-call(s32[1]{0:T(128)} %bitcast.6.me, bf16[4,128,256]{2,1,0:T(8,128)(2,1)S(1)} %join.19.refs_0_, bf16[4,128,640]{2,1,0:T(8,128)(2,1)S(1)} %join.21.refs_1_, bf16[4,128,640]{2,1,0:T(8,128)(2,1)S(1)} %join.23.refs_2_, ...), custom_call_target="tpu_custom_call" | custom-call | flops 3221225472 | bytes 12582912 | tf_op jit(solution)/shard_map/experts_early/pallas_call | solution.py:542
  154.9 1.9 collective-permute-done.36.refs_3_
  157.5 2.6 %collective-permute-done.39.refs_4_ = bf16[4,128,640]{2,1,0:T(8,128)(2,1)S(1)} collective-permute-done((bf16[4,128,640]{2,1,0:T(8,128)(2,1)S(1)}, bf16[4,128,640]{2,1,0:T(8,128)(2,1)S(1)}, u32[]{:S(2)}, u32[]{:S(2)}) %collective-permute-start.39) | collective-permute-done | bytes 655392 | tf_op jit(solution)/shard_map/ppermute | solution.py:44
  160.1 2.0 collective-permute-start.41
  162.0 13.2 %experts_late.3 = (bf16[4,128,512]{2,1,0:T(8,128)(2,1)S(1)}, bf16[4,128,512]{2,1,0:T(8,128)(2,1)S(1)}, bf16[4,128,512]{2,1,0:T(8,128)(2,1)S(1)}, bf16[4,128,512]...) custom-call(s32[1]{0:T(128)} %bitcast.6.me, ...), custom_call_target="tpu_custom_call" | custom-call | flops 6442450944 | bytes 25165824 | tf_op jit(solution)/shard_map/experts_late/pallas_call | solution.py:574
  177.6 2.5 %collective-permute-start.43 = (bf16[4,128,512]{2,1,0:T(8,128)(2,1)S(1)}, bf16[4,128,512]{2,1,0:T(8,128)(2,1)S(1)}, u32[]{:S(2)}, u32[]{:S(2)}) collective-permute-start(bf16[4,128,512]{2,1,0:T(8,128)(2,1)S(1)} %get-tuple-element.150), channel_id=1, source_target_pairs={{0,8},{8,0},{16,24},{24,16},{1,9},{9,1},{17,25},{25,17},{2,10},{10... | collective-permute-start | bytes 1572872 | tf_op jit(solution)/shard_map/ppermute | solution.py:44
  180.2 9.0 %collective-permute-done.45 = bf16[4,128,512]{2,1,0:T(8,128)(2,1)S(1)} collective-permute-done((bf16[4,128,512]{2,1,0:T(8,128)(2,1)S(1)}, bf16[4,128,512]{2,1,0:T(8,128)(2,1)S(1)}, u32[]{:S(2)}, u32[]{:S(2)}) %collective-permute-start.45) | collective-permute-done | bytes 524320 | tf_op jit(solution)/shard_map/ppermute | solution.py:44
  191.6 1.9 collective-permute-start.51
  198.4 1.8 collective-permute-start.53
  200.9 1.9 collective-permute-start.50
  203.5 1.9 collective-permute-done.52
  207.8 2.3 %collective-permute-done.47 = f32[16,512]{1,0:T(8,128)S(1)} collective-permute-done((f32[16,512]{1,0:T(8,128)S(1)}, f32[16,512]{1,0:T(8,128)S(1)}, u32[]{:S(2)}, u32[]{:S(2)}) %collective-permute-start.47) | collective-permute-done | bytes 32800 | tf_op jit(solution)/shard_map/ppermute | solution.py:44
  (177 shorter events, 60.4 us)
Async XLA Ops:
  5.7 10.0 %collective-permute-start.5 = (bf16[1,128,640]{2,1,0:T(8,128)(2,1)S(1)}, bf16[1,128,640]{2,1,0:T(8,128)(2,1)S(1)}, u32[]{:S(2)}, u32[]{:S(2)}) collective-permute-start(bf16[1,128,640]{2,1,0:T(8,128)(2,1)S(1)} %get-tuple-element.90.a_ref), channel_id=1, source_target_pairs={{0,8},{8,0},{16,24},{24,16},{1,9},{9,1},{17,25},{25,17},{2,10},{10... | collective-permute-start | bytes 491528 | tf_op jit(solution)/shard_map/ppermute | solution.py:44
  13.0 11.5 %collective-permute-start.9 = (f32[8,512]{1,0:T(8,128)S(1)}, f32[8,512]{1,0:T(8,128)S(1)}, u32[]{:S(2)}, u32[]{:S(2)}) collective-permute-start(f32[8,512]{1,0:T(8,128)S(1)} %get-tuple-element.96.slots_ref), channel_id=1, source_target_pairs={{0,16},{4,20},{8,24},{12,28},{16,0},{20,4},{24,8},{28,12},{1,17},{... | collective-permute-start | bytes 49160 | tf_op jit(solution)/shard_map/ppermute | solution.py:54
  17.3 8.1 %collective-permute-start.6 = (bf16[2,128,640]{2,1,0:T(8,128)(2,1)S(1)}, bf16[2,128,640]{2,1,0:T(8,128)(2,1)S(1)}, u32[]{:S(2)}, u32[]{:S(2)}) collective-permute-start(bf16[2,128,640]{2,1,0:T(8,128)(2,1)S(1)} %join.14.a_ref), channel_id=1, source_target_pairs={{0,8},{8,0},{16,24},{24,16},{1,9},{9,1},{17,25},{25,17},{2,10},{10... | collective-permute-start | bytes 983048 | tf_op jit(solution)/shard_map/ppermute | solution.py:44
  18.5 9.5 %collective-permute-start.11 = (f32[16,512]{1,0:T(8,128)S(1)}, f32[16,512]{1,0:T(8,128)S(1)}, u32[]{:S(2)}, u32[]{:S(2)}) collective-permute-start(f32[16,512]{1,0:T(8,128)S(1)} %fusion.8), channel_id=1, source_target_pairs={{0,2},{1,3},{2,0},{3,1},{4,6},{5,7},{6,4},{7,5},{8,10},{9,11},{10,... | collective-permute-start | bytes 98312 | tf_op jit(solution)/shard_map/ppermute | solution.py:44
  24.5 17.5 %collective-permute-start.13 = (bf16[4,128,640]{2,1,0:T(8,128)(2,1)S(1)}, bf16[4,128,640]{2,1,0:T(8,128)(2,1)}, u32[]{:S(2)}, u32[]{:S(2)}) collective-permute-start(bf16[4,128,640]{2,1,0:T(8,128)(2,1)S(1)} %join.17.refs_2_), channel_id=1, source_target_pairs={{0,2},{1,3},{2,0},{3,1},{4,6},{5,7},{6,4},{7,5},{8,10},{9,11},{10,... | collective-permute-start | bytes 1966088 | tf_op jit(solution)/shard_map/ppermute | solution.py:44
  25.5 16.5 %collective-permute-start.12 = (bf16[4,128,640]{2,1,0:T(8,128)(2,1)S(1)}, bf16[4,128,640]{2,1,0:T(8,128)(2,1)}, u32[]{:S(2)}, u32[]{:S(2)}) collective-permute-start(bf16[4,128,640]{2,1,0:T(8,128)(2,1)S(1)} %join.15.refs_1_), channel_id=1, source_target_pairs={{0,1},{1,0},{2,3},{3,2},{4,5},{5,4},{6,7},{7,6},{8,9},{9,8},{10,11... | collective-permute-start | bytes 1966088 | tf_op jit(solution)/shard_map/ppermute | solution.py:44
  28.1 13.9 %collective-permute-start.8 = (bf16[96,1536]{1,0:T(8,128)(2,1)}, bf16[96,1536]{1,0:T(8,128)(2,1)S(1)}, u32[]{:S(2)}, u32[]{:S(2)}) collective-permute-start(bf16[96,1536]{1,0:T(8,128)(2,1)} %slice.184), channel_id=1, source_target_pairs={{0,16},{4,20},{8,24},{12,28},{16,0},{20,4},{24,8},{28,12},{1,17},{... | collective-permute-start | bytes 884744 | tf_op jit(solution)/shard_map/ppermute | solution.py:54
  30.8 11.2 %collective-permute-start.10 = (bf16[4,128,256]{2,1,0:T(8,128)(2,1)S(1)}, bf16[4,128,256]{2,1,0:T(8,128)(2,1)S(1)}, u32[]{:S(2)}, u32[]{:S(2)}) collective-permute-start(bf16[4,128,256]{2,1,0:T(8,128)(2,1)S(1)} %join.13.refs_0_), channel_id=1, source_target_pairs={{0,8},{8,0},{16,24},{24,16},{1,9},{9,1},{17,25},{25,17},{2,10},{10... | collective-permute-start | bytes 786440 | tf_op jit(solution)/shard_map/ppermute | solution.py:44
  42.0 17.3 %collective-permute-start.14 = (bf16[112,1536]{1,0:T(8,128)(2,1)S(1)}, bf16[112,1536]{1,0:T(8,128)(2,1)S(1)}, u32[]{:S(2)}, u32[]{:S(2)}) collective-permute-start(bf16[112,1536]{1,0:T(8,128)(2,1)S(1)} %copy-done.5), channel_id=1, source_target_pairs={{0,16},{4,20},{8,24},{12,28},{16,0},{20,4},{24,8},{28,12},{1,17},{... | collective-permute-start | bytes 1032200 | tf_op jit(solution)/shard_map/ppermute | solution.py:54
  59.3 13.7 %collective-permute-start.17 = (bf16[4,128,512]{2,1,0:T(8,128)(2,1)S(1)}, bf16[4,128,512]{2,1,0:T(8,128)(2,1)S(1)}, u32[]{:S(2)}, u32[]{:S(2)}) collective-permute-start(bf16[4,128,512]{2,1,0:T(8,128)(2,1)S(1)} %get-tuple-element.116), channel_id=1, source_target_pairs={{0,2},{1,3},{2,0},{3,1},{4,6},{5,7},{6,4},{7,5},{8,10},{9,11},{10,... | collective-permute-start | bytes 1572872 | tf_op jit(solution)/shard_map/ppermute | solution.py:44
  60.9 13.6 %collective-permute-start.19 = (bf16[4,128,512]{2,1,0:T(8,128)(2,1)S(1)}, bf16[4,128,512]{2,1,0:T(8,128)(2,1)S(1)}, u32[]{:S(2)}, u32[]{:S(2)}) collective-permute-start(bf16[4,128,512]{2,1,0:T(8,128)(2,1)S(1)} %get-tuple-element.119), channel_id=1, source_target_pairs={{0,1},{1,0},{2,3},{3,2},{4,5},{5,4},{6,7},{7,6},{8,9},{9,8},{10,11... | collective-permute-start | bytes 1572872 | tf_op jit(solution)/shard_map/ppermute | solution.py:44
  61.5 27.7 %collective-permute-start.15 = (bf16[192,1536]{1,0:T(8,128)(2,1)S(1)}, bf16[192,1536]{1,0:T(8,128)(2,1)S(1)}, u32[]{:S(2)}, u32[]{:S(2)}) collective-permute-start(bf16[192,1536]{1,0:T(8,128)(2,1)S(1)} %slice.190), channel_id=1, source_target_pairs={{0,16},{4,20},{8,24},{12,28},{16,0},{20,4},{24,8},{28,12},{1,17},{... | collective-permute-start | bytes 1769480 | tf_op jit(solution)/shard_map/ppermute | solution.py:54
  61.7 23.3 %collective-permute-start.16 = (bf16[4,128,512]{2,1,0:T(8,128)(2,1)S(1)}, bf16[4,128,512]{2,1,0:T(8,128)(2,1)S(1)}, u32[]{:S(2)}, u32[]{:S(2)}) collective-permute-start(bf16[4,128,512]{2,1,0:T(8,128)(2,1)S(1)} %get-tuple-element.115), channel_id=1, source_target_pairs={{0,8},{8,0},{16,24},{24,16},{1,9},{9,1},{17,25},{25,17},{2,10},{10... | collective-permute-start | bytes 1572872 | tf_op jit(solution)/shard_map/ppermute | solution.py:44
  74.5 14.6 %collective-permute-start.20 = (bf16[2,128,512]{2,1,0:T(8,128)(2,1)S(1)}, bf16[2,128,512]{2,1,0:T(8,128)(2,1)S(1)}, u32[]{:S(2)}, u32[]{:S(2)}) collective-permute-start(bf16[2,128,512]{2,1,0:T(8,128)(2,1)S(1)} %slice.337), channel_id=1, source_target_pairs={{0,1},{1,0},{2,3},{3,2},{4,5},{5,4},{6,7},{7,6},{8,9},{9,8},{10,11... | collective-permute-start | bytes 786440 | tf_op jit(solution)/shard_map/ppermute | solution.py:44
  85.1 9.5 %collective-permute-start.22 = (bf16[2,128,512]{2,1,0:T(8,128)(2,1)S(1)}, bf16[2,128,512]{2,1,0:T(8,128)(2,1)S(1)}, u32[]{:S(2)}, u32[]{:S(2)}) collective-permute-start(bf16[2,128,512]{2,1,0:T(8,128)(2,1)S(1)} %slice.336), channel_id=1, source_target_pairs={{0,8},{8,0},{16,24},{24,16},{1,9},{9,1},{17,25},{25,17},{2,10},{10... | collective-permute-start | bytes 786440 | tf_op jit(solution)/shard_map/ppermute | solution.py:44
  102.5 17.1 %collective-permute-start.28 = (bf16[64,1536]{1,0:T(8,128)(2,1)S(1)}, bf16[64,1536]{1,0:T(8,128)(2,1)S(1)}, u32[]{:S(2)}, u32[]{:S(2)}) collective-permute-start(bf16[64,1536]{1,0:T(8,128)(2,1)S(1)} %get-tuple-element.126), channel_id=1, source_target_pairs={{0,16},{4,20},{8,24},{12,28},{16,0},{20,4},{24,8},{28,12},{1,17},{... | collective-permute-start | bytes 589832 | tf_op jit(solution)/shard_map/ppermute | solution.py:54
  105.2 17.1 %collective-permute-start.29 = (bf16[64,1536]{1,0:T(8,128)(2,1)S(1)}, bf16[64,1536]{1,0:T(8,128)(2,1)S(1)}, u32[]{:S(2)}, u32[]{:S(2)}) collective-permute-start(bf16[64,1536]{1,0:T(8,128)(2,1)S(1)} %get-tuple-element.127), channel_id=1, source_target_pairs={{0,20},{4,16},{8,28},{12,24},{16,4},{20,0},{24,12},{28,8},{1,21},{... | collective-permute-start | bytes 589832 | tf_op jit(solution)/shard_map/ppermute | solution.py:54
  122.6 8.3 %collective-permute-start.31 = (bf16[1,128,640]{2,1,0:T(8,128)(2,1)S(1)}, bf16[1,128,640]{2,1,0:T(8,128)(2,1)S(1)}, u32[]{:S(2)}, u32[]{:S(2)}) collective-permute-start(bf16[1,128,640]{2,1,0:T(8,128)(2,1)S(1)} %get-tuple-element.129.a_ref), channel_id=1, source_target_pairs={{0,2},{1,3},{2,0},{3,1},{4,6},{5,7},{6,4},{7,5},{8,10},{9,11},{10,... | collective-permute-start | bytes 491528 | tf_op jit(solution)/shard_map/ppermute | solution.py:44
  129.2 9.5 %collective-permute-start.37 = (bf16[2,128,640]{2,1,0:T(8,128)(2,1)S(1)}, bf16[2,128,640]{2,1,0:T(8,128)(2,1)S(1)}, u32[]{:S(2)}, u32[]{:S(2)}) collective-permute-start(bf16[2,128,640]{2,1,0:T(8,128)(2,1)S(1)} %join.22.a_ref), channel_id=1, source_target_pairs={{0,1},{1,0},{2,3},{3,2},{4,5},{5,4},{6,7},{7,6},{8,9},{9,8},{10,11... | collective-permute-start | bytes 983048 | tf_op jit(solution)/shard_map/ppermute | solution.py:44
  131.0 13.5 %collective-permute-start.35 = (bf16[2,128,640]{2,1,0:T(8,128)(2,1)S(1)}, bf16[2,128,640]{2,1,0:T(8,128)(2,1)S(1)}, u32[]{:S(2)}, u32[]{:S(2)}) collective-permute-start(bf16[2,128,640]{2,1,0:T(8,128)(2,1)S(1)} %join.20.a_ref), channel_id=1, source_target_pairs={{0,8},{8,0},{16,24},{24,16},{1,9},{9,1},{17,25},{25,17},{2,10},{10... | collective-permute-start | bytes 983048 | tf_op jit(solution)/shard_map/ppermute | solution.py:44
  131.7 10.7 %collective-permute-start.33 = (bf16[64,1536]{1,0:T(8,128)(2,1)S(1)}, bf16[64,1536]{1,0:T(8,128)(2,1)S(1)}, u32[]{:S(2)}, u32[]{:S(2)}) collective-permute-start(bf16[64,1536]{1,0:T(8,128)(2,1)S(1)} %get-tuple-element.133), channel_id=1, source_target_pairs={{0,16},{4,20},{8,24},{12,28},{16,0},{20,4},{24,8},{28,12},{1,17},{... | collective-permute-start | bytes 589832 | tf_op jit(solution)/shard_map/ppermute | solution.py:54
  133.3 9.1 %collective-permute-start.32 = (bf16[2,128,256]{2,1,0:T(8,128)(2,1)S(1)}, bf16[2,128,256]{2,1,0:T(8,128)(2,1)S(1)}, u32[]{:S(2)}, u32[]{:S(2)}) collective-permute-start(bf16[2,128,256]{2,1,0:T(8,128)(2,1)S(1)} %join.18.a_ref), channel_id=1, source_target_pairs={{0,2},{1,3},{2,0},{3,1},{4,6},{5,7},{6,4},{7,5},{8,10},{9,11},{10,... | collective-permute-start | bytes 393224 | tf_op jit(solution)/shard_map/ppermute | solution.py:44
  142.4 15.1 %collective-permute-start.40 = (bf16[4,128,640]{2,1,0:T(8,128)(2,1)S(1)}, bf16[4,128,640]{2,1,0:T(8,128)(2,1)S(1)}, u32[]{:S(2)}, u32[]{:S(2)}) collective-permute-start(bf16[4,128,640]{2,1,0:T(8,128)(2,1)S(1)} %join.23.refs_2_), channel_id=1, source_target_pairs={{0,2},{1,3},{2,0},{3,1},{4,6},{5,7},{6,4},{7,5},{8,10},{9,11},{10,... | collective-permute-start | bytes 1966088 | tf_op jit(solution)/shard_map/ppermute | solution.py:44
  144.5 15.6 %collective-permute-start.39 = (bf16[4,128,640]{2,1,0:T(8,128)(2,1)S(1)}, bf16[4,128,640]{2,1,0:T(8,128)(2,1)S(1)}, u32[]{:S(2)}, u32[]{:S(2)}) collective-permute-start(bf16[4,128,640]{2,1,0:T(8,128)(2,1)S(1)} %join.21.refs_1_), channel_id=1, source_target_pairs={{0,1},{1,0},{2,3},{3,2},{4,5},{5,4},{6,7},{7,6},{8,9},{9,8},{10,11... | collective-permute-start | bytes 1966088 | tf_op jit(solution)/shard_map/ppermute | solution.py:44
  144.9 10.0 %collective-permute-start.38 = (bf16[64,1536]{1,0:T(8,128)(2,1)S(1)}, bf16[64,1536]{1,0:T(8,128)(2,1)S(1)}, u32[]{:S(2)}, u32[]{:S(2)}) collective-permute-start(bf16[64,1536]{1,0:T(8,128)(2,1)S(1)} %get-tuple-element.138), channel_id=1, source_target_pairs={{0,16},{4,20},{8,24},{12,28},{16,0},{20,4},{24,8},{28,12},{1,17},{... | collective-permute-start | bytes 589832 | tf_op jit(solution)/shard_map/ppermute | solution.py:54
  148.2 8.7 %collective-permute-start.36 = (bf16[4,128,256]{2,1,0:T(8,128)(2,1)S(1)}, bf16[4,128,256]{2,1,0:T(8,128)(2,1)S(1)}, u32[]{:S(2)}, u32[]{:S(2)}) collective-permute-start(bf16[4,128,256]{2,1,0:T(8,128)(2,1)S(1)} %join.19.refs_0_), channel_id=1, source_target_pairs={{0,8},{8,0},{16,24},{24,16},{1,9},{9,1},{17,25},{25,17},{2,10},{10... | collective-permute-start | bytes 786440 | tf_op jit(solution)/shard_map/ppermute | solution.py:44
  160.1 16.2 %collective-permute-start.41 = (bf16[112,1536]{1,0:T(8,128)(2,1)S(1)}, bf16[112,1536]{1,0:T(8,128)(2,1)S(1)}, u32[]{:S(2)}, u32[]{:S(2)}) collective-permute-start(bf16[112,1536]{1,0:T(8,128)(2,1)S(1)} %copy-done.4), channel_id=1, source_target_pairs={{0,16},{4,20},{8,24},{12,28},{16,0},{20,4},{24,8},{28,12},{1,17},{... | collective-permute-start | bytes 1032200 | tf_op jit(solution)/shard_map/ppermute | solution.py:54
  176.2 12.9 %collective-permute-start.45 = (bf16[4,128,512]{2,1,0:T(8,128)(2,1)S(1)}, bf16[4,128,512]{2,1,0:T(8,128)(2,1)S(1)}, u32[]{:S(2)}, u32[]{:S(2)}) collective-permute-start(bf16[4,128,512]{2,1,0:T(8,128)(2,1)S(1)} %get-tuple-element.154), channel_id=1, source_target_pairs={{0,2},{1,3},{2,0},{3,1},{4,6},{5,7},{6,4},{7,5},{8,10},{9,11},{10,... | collective-permute-start | bytes 1572872 | tf_op jit(solution)/shard_map/ppermute | solution.py:44
  177.2 16.9 %collective-permute-start.42 = (f32[8,512]{1,0:T(8,128)S(1)}, f32[8,512]{1,0:T(8,128)S(1)}, u32[]{:S(2)}, u32[]{:S(2)}) collective-permute-start(f32[8,512]{1,0:T(8,128)S(1)} %get-tuple-element.145), channel_id=1, source_target_pairs={{0,16},{4,20},{8,24},{12,28},{16,0},{20,4},{24,8},{28,12},{1,17},{... | collective-permute-start | bytes 49160 | tf_op jit(solution)/shard_map/ppermute | solution.py:54
  177.3 13.1 %collective-permute-start.44 = (bf16[4,128,512]{2,1,0:T(8,128)(2,1)S(1)}, bf16[4,128,512]{2,1,0:T(8,128)(2,1)S(1)}, u32[]{:S(2)}, u32[]{:S(2)}) collective-permute-start(bf16[4,128,512]{2,1,0:T(8,128)(2,1)S(1)} %get-tuple-element.152), channel_id=1, source_target_pairs={{0,1},{1,0},{2,3},{3,2},{4,5},{5,4},{6,7},{7,6},{8,9},{9,8},{10,11... | collective-permute-start | bytes 1572872 | tf_op jit(solution)/shard_map/ppermute | solution.py:44
  177.6 14.0 %collective-permute-start.43 = (bf16[4,128,512]{2,1,0:T(8,128)(2,1)S(1)}, bf16[4,128,512]{2,1,0:T(8,128)(2,1)S(1)}, u32[]{:S(2)}, u32[]{:S(2)}) collective-permute-start(bf16[4,128,512]{2,1,0:T(8,128)(2,1)S(1)} %get-tuple-element.150), channel_id=1, source_target_pairs={{0,8},{8,0},{16,24},{24,16},{1,9},{9,1},{17,25},{25,17},{2,10},{10... | collective-permute-start | bytes 1572872 | tf_op jit(solution)/shard_map/ppermute | solution.py:44
  195.6 10.5 %collective-permute-start.46 = (f32[16,512]{1,0:T(8,128)S(1)}, f32[16,512]{1,0:T(8,128)S(1)}, u32[]{:S(2)}, u32[]{:S(2)}) collective-permute-start(f32[16,512]{1,0:T(8,128)S(1)} %get-tuple-element.157), channel_id=1, source_target_pairs={{0,1},{1,0},{2,3},{3,2},{4,5},{5,4},{6,7},{7,6},{8,9},{9,8},{10,11... | collective-permute-start | bytes 98312 | tf_op jit(solution)/shard_map/ppermute | solution.py:44
  (31 other events, 180.9 us)

commit v4 on v3

--- a/solution.py
+++ b/solution.py
@@ -68,19 +68,21 @@
     return places == slot_row
 
 
-def prologue_kernel(core, lens, ids_ref, x_ref, slots_ref, own_ref, other_ref):
-    rows = ids_ref.shape[1]
+def prologue_kernel(place_ref, lens, ids_ref, x_hbm, slots_ref, own_ref, other_ref, x_ref, sem):
+    copy = pltpu.make_async_copy(x_hbm, x_ref, sem)
+    copy.start()
+    rows = ids_ref.shape[2]
     groups_len = rows // SEQ_LEN
     place = lax.broadcasted_iota(jnp.int32, (1, rows), 1)
-    me = core[0]
+    me = place_ref[0]
     named = []
     for step in range(2):
         limit = jnp.zeros((1, rows), jnp.int32)
         for q in range(groups_len):
-            limit = jnp.where(place // SEQ_LEN == q, lens[step * groups_len + q], limit)
+            limit = jnp.where(place // SEQ_LEN == q, lens[place_ref[1 + step], q], limit)
         live = place % SEQ_LEN < limit
-        first = ids_ref[2 * step : 2 * step + 1, :]
-        second = ids_ref[2 * step + 1 : 2 * step + 2, :]
+        first = ids_ref[step, 0:1, :]
+        second = ids_ref[step, 1:2, :]
         for which in range(2):
             expert = me if which == 0 else 1 - me
             hit = ((first == expert) | (second == expert)) & live
@@ -97,13 +99,14 @@
         [one_hot_rows(slots[0:1]), one_hot_rows(slots[1:2])], axis=0
     )
     table = jnp.where(table, 1.0, 0.0).astype(bf16)
+    copy.wait()
     for a, b in cuts(x_ref.shape[1], OUT_PARTS):
         got = jnp.dot(table, x_ref[:, a:b], preferred_element_type=f32).astype(bf16)
         own_ref[:, a:b] = got[:CAP]
         other_ref[:, a:b] = got[CAP:]
 
 
-def prologue(core, lens, ids_rows, x):
+def prologue(place, lens, ids_rows, x):
     rows, feats = x.shape
     piece = jax.ShapeDtypeStruct((CAP, feats), bf16)
     return pl.pallas_call(
@@ -114,10 +117,11 @@
             pl.BlockSpec(memory_space=pltpu.SMEM),
             pl.BlockSpec(memory_space=pltpu.SMEM),
             pl.BlockSpec(memory_space=pltpu.VMEM),
-            pl.BlockSpec(memory_space=pltpu.VMEM),
+            pl.BlockSpec(memory_space=pltpu.HBM),
         ],
+        scratch_shapes=[pltpu.VMEM((rows, feats), bf16), pltpu.SemaphoreType.DMA(())],
         compiler_params=params(),
-    )(core, lens, ids_rows, x)
+    )(place, lens, ids_rows, x)
 
 
 def in_three(v):
@@ -187,7 +191,7 @@
 
 def prepare_kernel(core, stat_ref, ids_ref, slots_ref, next_ref, x_ref, aux_ref, base_ref, mix_ref):
     me = core[0]
-    w_own, w_other = row_weights(stat_ref[...], ids_ref[0:1, :], ids_ref[1:2, :], me)
+    w_own, w_other = row_weights(stat_ref[...], ids_ref[0, 0:1, :], ids_ref[0, 1:2, :], me)
     s_own, s_other = slots_ref[0:1, :], slots_ref[1:2, :]
     aux_ref[...] = jnp.concatenate(
         [w_own, w_other, s_own, s_other, jnp.zeros((4, w_own.shape[1]), f32)], axis=0
@@ -286,7 +290,7 @@
 def last_kernel(core, x_ref, stat_ref, ids_ref, slots_ref, *refs):
     own, other, out_ref = refs[:OUT_PARTS], refs[OUT_PARTS : 2 * OUT_PARTS], refs[-1]
     me = core[0]
-    weights = row_weights(stat_ref[...], ids_ref[2:3, :], ids_ref[3:4, :], me)
+    weights = row_weights(stat_ref[...], ids_ref[1, 0:1, :], ids_ref[1, 1:2, :], me)
     table = weight_table(weights, (slots_ref[2:3, :], slots_ref[3:4, :]))
     for p, (a, b) in enumerate(cuts(x_ref.shape[1], OUT_PARTS)):
         cols = slice(a, b)
@@ -635,23 +639,18 @@
 
     gain_row = lax.dynamic_index_in_dim(norm_gain, layer, 0, keepdims=True)
     router_t = lax.dynamic_index_in_dim(router, layer, 0, keepdims=False).T
-    ids_rows = jnp.transpose(expert_ids, (0, 2, 1)).reshape(4, rows)
-    lens = jnp.concatenate(
-        [
-            lax.dynamic_index_in_dim(lengths, section, 0, keepdims=False),
-            lax.dynamic_index_in_dim(lengths, (section - 2) % sections, 0, keepdims=False),
-        ]
-    )
+    ids_rows = jnp.transpose(expert_ids, (0, 2, 1))
+    place = jnp.stack([core[0], section, (section - 2) % sections]).astype(jnp.int32)
     orders = sum_orders = out_orders(slices)
     rounds = len(orders[0])
     gate_w, up_w, down_w = w_gate[0, 0], w_up[0, 0], w_down[0, 0]
     pieces = []
     begin = 0
-    for share in (6, 7, 12, 7):
+    for share in (5, 7, 13, 7):
         pieces.append(tokens[begin : begin + rows * share // 32])
         begin += rows * share // 32
 
-    slots, own, other = prologue(core, lens, ids_rows, tokens)
+    slots, own, other = prologue(place, lengths, ids_rows, tokens)
     next_slots = ahead(slots, -2)
     blocks = lay(own, swapped(other, across))
     held, came = gather_round(blocks, None, orders, 0)
@@ -671,11 +670,12 @@
         me, held, came, gain_all, sums, gate_w, up_w, down_w, orders, sum_orders, cuts(feats, OUT_PARTS)
     )
     far.append(ahead(tied(pieces[2], *send), 2))
-    summed, _ = sum_cube(keep, send, sum_orders, {0: [far[1]], rounds - 1: [far[2]]})
+    summed, _ = sum_cube(keep, send, sum_orders, {0: [far[1]]})
 
     mine = [s[:CAP] for s in summed]
     theirs = [swapped(s[CAP:], across) for s in summed]
     to_own, to_other, slab_own, slab_other = repick(mix, base, mine, theirs)
+    to_own, to_other = tied(to_own, far[2]), tied(to_other, far[2])
     blocks = lay(ahead(to_own, 2), ahead(to_other, 2, True))
     slab_own = ahead(tied(slab_own, *blocks), 2)
     held, came = gather_round(blocks, None, orders, 0)

time: 212 us -> 211 us (level)
    ppermute x47, waiting for transfers between devices: 70.8 us -> 68.6 us  [swapped(): lax.ppermute(x, axis, [(i, i ^ 1 << bit) for i in range(lax.axis_size(axi...]
where the time goes in v4:
time: 211 us; the launch traced here: 210 us
  waiting for transfers between devices  94.3 us (45%)
  starting transfers between devices  61.6 us (29%)
  Pallas kernels  46.2 us (22%)
  local copies, waits for them, and re-layouts  5.79 us (3%)
    ppermute x47, waiting for transfers between devices, swapped(): lax.ppermute(x, axis, [(i, i ^ 1 << bit) for i in range(lax.axis_size(axi...  68.6 us
    ppermute x47, starting transfers between devices, swapped(): lax.ppermute(x, axis, [(i, i ^ 1 << bit) for i in range(lax.axis_size(axi...  45.9 us
    pallas_call x2, Pallas kernels, experts_late(): pl.pallas_call(functools.partial(late_kernel, units, orders, sum_orders,...  27.4 us
    ppermute x10, waiting for transfers between devices, ahead(): return lax.ppermute(x, ('section', 'expert'), perm)  25.7 us
    ppermute x10, starting transfers between devices, ahead(): return lax.ppermute(x, ('section', 'expert'), perm)  15.7 us
    pallas_call x2, Pallas kernels, experts_early(): pl.pallas_call(functools.partial(early_kernel, units, orders, feats), nam...  12.4 us
  transfers between devices with their start and end apart: 57, of which 35 were waited for; matrix products, arithmetic and copies ran while one was open for 2% of the time, Pallas kernels for 20%

profile of v4, /device:TPU:0, one launch (start us, length us, event | category | flops | bytes accessed | tf_op | source)
XLA Modules:
  0.0 210.3 jit_solution(2923068721670611726)
XLA Ops:
  5.8 3.0 %collective-permute-start.5 = (bf16[1,128,640]{2,1,0:T(8,128)(2,1)S(1)}, bf16[1,128,640]{2,1,0:T(8,128)(2,1)S(1)}, u32[]{:S(2)}, u32[]{:S(2)}) collective-permute-start(bf16[1,128,640]{2,1,0:T(8,128)(2,1)S(1)} %get-tuple-element.92.a_ref), channel_id=1, source_target_pairs={{0,8},{8,0},{16,24},{24,16},{1,9},{9,1},{17,25},{25,17},{2,10},{10... | collective-permute-start | bytes 491528 | tf_op jit(solution)/shard_map/ppermute | solution.py:44
  13.1 2.6 %collective-permute-start.9 = (f32[8,512]{1,0:T(8,128)S(1)}, f32[8,512]{1,0:T(8,128)S(1)}, u32[]{:S(2)}, u32[]{:S(2)}) collective-permute-start(f32[8,512]{1,0:T(8,128)S(1)} %get-tuple-element.98.slots_ref), channel_id=1, source_target_pairs={{0,16},{4,20},{8,24},{12,28},{16,0},{20,4},{24,8},{28,12},{1,17},{... | collective-permute-start | bytes 49160 | tf_op jit(solution)/shard_map/ppermute | solution.py:54
  20.1 4.4 %collective-permute-done.7.b_ref = bf16[2,128,640]{2,1,0:T(8,128)(2,1)S(1)} collective-permute-done((bf16[2,128,640]{2,1,0:T(8,128)(2,1)S(1)}, bf16[2,128,640]{2,1,0:T(8,128)(2,1)S(1)}, u32[]{:S(2)}, u32[]{:S(2)}) %collective-permute-start.7) | collective-permute-done | bytes 327712 | tf_op jit(solution)/shard_map/ppermute | solution.py:44
  28.2 2.6 %collective-permute-start.8 = (bf16[80,1536]{1,0:T(8,128)(2,1)}, bf16[80,1536]{1,0:T(8,128)(2,1)S(1)}, u32[]{:S(2)}, u32[]{:S(2)}) collective-permute-start(bf16[80,1536]{1,0:T(8,128)(2,1)} %slice.184), channel_id=1, source_target_pairs={{0,16},{4,20},{8,24},{12,28},{16,0},{20,4},{24,8},{28,12},{1,17},{... | collective-permute-start | bytes 737288 | tf_op jit(solution)/shard_map/ppermute | solution.py:54
  32.2 6.2 %experts_early.2 = (f32[256,1024]{1,0:T(8,128)S(1)}, f32[256,1024]{1,0:T(8,128)S(1)}, f32[256,128]{1,0:T(8,128)S(1)}) custom-call(s32[1]{0:T(128)} %bitcast.6.me, bf16[4,128,256]{2,1,0:T(8,128)(2,1)S(1)} %join.13.refs_0_, bf16[4,128,640]{2,1,0:T(8,128)(2,1)S(1)} %join.15.refs_1_, bf16[4,128,640]{2,1,0:T(8,128)(2,1)S(1)} %join.17.refs_2_, ...), custom_call_target="tpu_custom_call" | custom-call | flops 3221225472 | bytes 12582912 | tf_op jit(solution)/shard_map/experts_early/pallas_call | solution.py:546
  41.7 14.2 %experts_late.2 = (bf16[4,128,512]{2,1,0:T(8,128)(2,1)S(1)}, bf16[4,128,512]{2,1,0:T(8,128)(2,1)S(1)}, bf16[4,128,512]{2,1,0:T(8,128)(2,1)S(1)}, bf16[4,128,512]...) custom-call(s32[1]{0:T(128)} %bitcast.6.me, ...), custom_call_target="tpu_custom_call" | custom-call | flops 6442450944 | bytes 25165824 | tf_op jit(solution)/shard_map/experts_late/pallas_call | solution.py:578
  61.8 8.7 %collective-permute-done.17 = bf16[4,128,512]{2,1,0:T(8,128)(2,1)S(1)} collective-permute-done((bf16[4,128,512]{2,1,0:T(8,128)(2,1)S(1)}, bf16[4,128,512]{2,1,0:T(8,128)(2,1)S(1)}, u32[]{:S(2)}, u32[]{:S(2)}) %collective-permute-start.17) | collective-permute-done | bytes 524320 | tf_op jit(solution)/shard_map/ppermute | solution.py:44
  72.4 11.2 %collective-permute-done.16 = bf16[4,128,512]{2,1,0:T(8,128)(2,1)S(1)} collective-permute-done((bf16[4,128,512]{2,1,0:T(8,128)(2,1)S(1)}, bf16[4,128,512]{2,1,0:T(8,128)(2,1)S(1)}, u32[]{:S(2)}, u32[]{:S(2)}) %collective-permute-start.16) | collective-permute-done | bytes 524320 | tf_op jit(solution)/shard_map/ppermute | solution.py:44
  83.6 2.5 %collective-permute-start.22 = (bf16[2,128,512]{2,1,0:T(8,128)(2,1)S(1)}, bf16[2,128,512]{2,1,0:T(8,128)(2,1)S(1)}, u32[]{:S(2)}, u32[]{:S(2)}) collective-permute-start(bf16[2,128,512]{2,1,0:T(8,128)(2,1)S(1)} %slice.336), channel_id=1, source_target_pairs={{0,8},{8,0},{16,24},{24,16},{1,9},{9,1},{17,25},{25,17},{2,10},{10... | collective-permute-start | bytes 786440 | tf_op jit(solution)/shard_map/ppermute | solution.py:44
  87.7 6.7 %collective-permute-done.22 = bf16[2,128,512]{2,1,0:T(8,128)(2,1)S(1)} collective-permute-done((bf16[2,128,512]{2,1,0:T(8,128)(2,1)S(1)}, bf16[2,128,512]{2,1,0:T(8,128)(2,1)S(1)}, u32[]{:S(2)}, u32[]{:S(2)}) %collective-permute-start.22) | collective-permute-done | bytes 262176 | tf_op jit(solution)/shard_map/ppermute | solution.py:44
  96.9 2.9 %collective-permute-done.24 = bf16[1,128,512]{2,1,0:T(8,128)(2,1)S(1)} collective-permute-done((bf16[1,128,512]{2,1,0:T(8,128)(2,1)S(1)}, bf16[1,128,512]{2,1,0:T(8,128)(2,1)S(1)}, u32[]{:S(2)}, u32[]{:S(2)}) %collective-permute-start.24) | collective-permute-done | bytes 131104 | tf_op jit(solution)/shard_map/ppermute | solution.py:44
  102.3 2.3 %collective-permute-start.29 = (bf16[64,1536]{1,0:T(8,128)(2,1)S(1)}, bf16[64,1536]{1,0:T(8,128)(2,1)S(1)}, u32[]{:S(2)}, u32[]{:S(2)}) collective-permute-start(bf16[64,1536]{1,0:T(8,128)(2,1)S(1)} %get-tuple-element.131), channel_id=1, source_target_pairs={{0,20},{4,16},{8,28},{12,24},{16,4},{20,0},{24,12},{28,8},{1,21},{... | collective-permute-start | bytes 589832 | tf_op jit(solution)/shard_map/ppermute | solution.py:54
  105.0 13.5 %collective-permute-done.29.other_ref = bf16[64,1536]{1,0:T(8,128)(2,1)S(1)} collective-permute-done((bf16[64,1536]{1,0:T(8,128)(2,1)S(1)}, bf16[64,1536]{1,0:T(8,128)(2,1)S(1)}, u32[]{:S(2)}, u32[]{:S(2)}) %collective-permute-start.29) | collective-permute-done | bytes 196640 | tf_op jit(solution)/shard_map/ppermute | solution.py:54
  118.5 4.6 %collective-permute-done.28.own_ref = bf16[64,1536]{1,0:T(8,128)(2,1)S(1)} collective-permute-done((bf16[64,1536]{1,0:T(8,128)(2,1)S(1)}, bf16[64,1536]{1,0:T(8,128)(2,1)S(1)}, u32[]{:S(2)}, u32[]{:S(2)}) %collective-permute-start.28) | collective-permute-done | bytes 196640 | tf_op jit(solution)/shard_map/ppermute | solution.py:54
  125.4 3.7 %collective-permute-done.34.b_ref = bf16[1,128,640]{2,1,0:T(8,128)(2,1)S(1)} collective-permute-done((bf16[1,128,640]{2,1,0:T(8,128)(2,1)S(1)}, bf16[1,128,640]{2,1,0:T(8,128)(2,1)S(1)}, u32[]{:S(2)}, u32[]{:S(2)}) %collective-permute-start.34) | collective-permute-done | bytes 163872 | tf_op jit(solution)/shard_map/ppermute | solution.py:44
  134.5 3.2 %collective-permute-done.37.b_ref = bf16[2,128,640]{2,1,0:T(8,128)(2,1)S(1)} collective-permute-done((bf16[2,128,640]{2,1,0:T(8,128)(2,1)S(1)}, bf16[2,128,640]{2,1,0:T(8,128)(2,1)S(1)}, u32[]{:S(2)}, u32[]{:S(2)}) %collective-permute-start.37) | collective-permute-done | bytes 327712 | tf_op jit(solution)/shard_map/ppermute | solution.py:44
  137.7 3.5 %collective-permute-done.33.own_ref = bf16[64,1536]{1,0:T(8,128)(2,1)S(1)} collective-permute-done((bf16[64,1536]{1,0:T(8,128)(2,1)S(1)}, bf16[64,1536]{1,0:T(8,128)(2,1)S(1)}, u32[]{:S(2)}, u32[]{:S(2)}) %collective-permute-start.33) | collective-permute-done | bytes 196640 | tf_op jit(solution)/shard_map/ppermute | solution.py:54
  143.9 2.9 %collective-permute-start.38 = (bf16[64,1536]{1,0:T(8,128)(2,1)S(1)}, bf16[64,1536]{1,0:T(8,128)(2,1)S(1)}, u32[]{:S(2)}, u32[]{:S(2)}) collective-permute-start(bf16[64,1536]{1,0:T(8,128)(2,1)S(1)} %get-tuple-element.142), channel_id=1, source_target_pairs={{0,16},{4,20},{8,24},{12,28},{16,0},{20,4},{24,8},{28,12},{1,17},{... | collective-permute-start | bytes 589832 | tf_op jit(solution)/shard_map/ppermute | solution.py:54
  146.8 6.2 %experts_early.3 = (f32[256,1024]{1,0:T(8,128)S(1)}, f32[256,1024]{1,0:T(8,128)S(1)}, f32[256,128]{1,0:T(8,128)S(1)}) custom-call(s32[1]{0:T(128)} %bitcast.6.me, bf16[4,128,256]{2,1,0:T(8,128)(2,1)S(1)} %join.19.refs_0_, bf16[4,128,640]{2,1,0:T(8,128)(2,1)S(1)} %join.21.refs_1_, bf16[4,128,640]{2,1,0:T(8,128)(2,1)S(1)} %join.23.refs_2_, ...), custom_call_target="tpu_custom_call" | custom-call | flops 3221225472 | bytes 12582912 | tf_op jit(solution)/shard_map/experts_early/pallas_call | solution.py:546
  155.4 3.2 %collective-permute-done.39.refs_4_ = bf16[4,128,640]{2,1,0:T(8,128)(2,1)S(1)} collective-permute-done((bf16[4,128,640]{2,1,0:T(8,128)(2,1)S(1)}, bf16[4,128,640]{2,1,0:T(8,128)(2,1)S(1)}, u32[]{:S(2)}, u32[]{:S(2)}) %collective-permute-start.39) | collective-permute-done | bytes 655392 | tf_op jit(solution)/shard_map/ppermute | solution.py:44
  159.2 13.2 %experts_late.3 = (bf16[4,128,512]{2,1,0:T(8,128)(2,1)S(1)}, bf16[4,128,512]{2,1,0:T(8,128)(2,1)S(1)}, bf16[4,128,512]{2,1,0:T(8,128)(2,1)S(1)}, bf16[4,128,512]...) custom-call(s32[1]{0:T(128)} %bitcast.6.me, ...), custom_call_target="tpu_custom_call" | custom-call | flops 6442450944 | bytes 25165824 | tf_op jit(solution)/shard_map/experts_late/pallas_call | solution.py:578
  172.8 1.9 collective-permute-start.45
  175.0 1.7 collective-permute-start.44
  176.7 1.6 collective-permute-start.43
  178.4 7.7 %collective-permute-done.45 = bf16[4,128,512]{2,1,0:T(8,128)(2,1)S(1)} collective-permute-done((bf16[4,128,512]{2,1,0:T(8,128)(2,1)S(1)}, bf16[4,128,512]{2,1,0:T(8,128)(2,1)S(1)}, u32[]{:S(2)}, u32[]{:S(2)}) %collective-permute-start.45) | collective-permute-done | bytes 524320 | tf_op jit(solution)/shard_map/ppermute | solution.py:44
  189.8 2.1 %collective-permute-start.51 = (bf16[2,128,512]{2,1,0:T(8,128)(2,1)S(1)}, bf16[2,128,512]{2,1,0:T(8,128)(2,1)S(1)}, u32[]{:S(2)}, u32[]{:S(2)}) collective-permute-start(bf16[2,128,512]{2,1,0:T(8,128)(2,1)S(1)} %slice.333), channel_id=1, source_target_pairs={{0,8},{8,0},{16,24},{24,16},{1,9},{9,1},{17,25},{25,17},{2,10},{10... | collective-permute-start | bytes 786440 | tf_op jit(solution)/shard_map/ppermute | solution.py:44
  195.0 1.6 collective-permute-done.51
  196.6 1.7 collective-permute-start.53
  201.7 2.0 collective-permute-done.52
  204.5 1.7 collective-permute-start.47
  206.2 2.3 %collective-permute-done.47 = f32[16,512]{1,0:T(8,128)S(1)} collective-permute-done((f32[16,512]{1,0:T(8,128)S(1)}, f32[16,512]{1,0:T(8,128)S(1)}, u32[]{:S(2)}, u32[]{:S(2)}) %collective-permute-start.47) | collective-permute-done | bytes 32800 | tf_op jit(solution)/shard_map/ppermute | solution.py:44
  208.5 1.8 last.1
  (181 shorter events, 62.2 us)
Async XLA Ops:
  5.8 10.0 %collective-permute-start.5 = (bf16[1,128,640]{2,1,0:T(8,128)(2,1)S(1)}, bf16[1,128,640]{2,1,0:T(8,128)(2,1)S(1)}, u32[]{:S(2)}, u32[]{:S(2)}) collective-permute-start(bf16[1,128,640]{2,1,0:T(8,128)(2,1)S(1)} %get-tuple-element.92.a_ref), channel_id=1, source_target_pairs={{0,8},{8,0},{16,24},{24,16},{1,9},{9,1},{17,25},{25,17},{2,10},{10... | collective-permute-start | bytes 491528 | tf_op jit(solution)/shard_map/ppermute | solution.py:44
  13.1 11.5 %collective-permute-start.9 = (f32[8,512]{1,0:T(8,128)S(1)}, f32[8,512]{1,0:T(8,128)S(1)}, u32[]{:S(2)}, u32[]{:S(2)}) collective-permute-start(f32[8,512]{1,0:T(8,128)S(1)} %get-tuple-element.98.slots_ref), channel_id=1, source_target_pairs={{0,16},{4,20},{8,24},{12,28},{16,0},{20,4},{24,8},{28,12},{1,17},{... | collective-permute-start | bytes 49160 | tf_op jit(solution)/shard_map/ppermute | solution.py:54
  17.4 8.1 %collective-permute-start.6 = (bf16[2,128,640]{2,1,0:T(8,128)(2,1)S(1)}, bf16[2,128,640]{2,1,0:T(8,128)(2,1)S(1)}, u32[]{:S(2)}, u32[]{:S(2)}) collective-permute-start(bf16[2,128,640]{2,1,0:T(8,128)(2,1)S(1)} %join.14.a_ref), channel_id=1, source_target_pairs={{0,8},{8,0},{16,24},{24,16},{1,9},{9,1},{17,25},{25,17},{2,10},{10... | collective-permute-start | bytes 983048 | tf_op jit(solution)/shard_map/ppermute | solution.py:44
  18.6 9.5 %collective-permute-start.11 = (f32[16,512]{1,0:T(8,128)S(1)}, f32[16,512]{1,0:T(8,128)S(1)}, u32[]{:S(2)}, u32[]{:S(2)}) collective-permute-start(f32[16,512]{1,0:T(8,128)S(1)} %fusion.8), channel_id=1, source_target_pairs={{0,2},{1,3},{2,0},{3,1},{4,6},{5,7},{6,4},{7,5},{8,10},{9,11},{10,... | collective-permute-start | bytes 98312 | tf_op jit(solution)/shard_map/ppermute | solution.py:44
  24.6 15.9 %collective-permute-start.13 = (bf16[4,128,640]{2,1,0:T(8,128)(2,1)S(1)}, bf16[4,128,640]{2,1,0:T(8,128)(2,1)}, u32[]{:S(2)}, u32[]{:S(2)}) collective-permute-start(bf16[4,128,640]{2,1,0:T(8,128)(2,1)S(1)} %join.17.refs_2_), channel_id=1, source_target_pairs={{0,2},{1,3},{2,0},{3,1},{4,6},{5,7},{6,4},{7,5},{8,10},{9,11},{10,... | collective-permute-start | bytes 1966088 | tf_op jit(solution)/shard_map/ppermute | solution.py:44
  25.6 14.9 %collective-permute-start.12 = (bf16[4,128,640]{2,1,0:T(8,128)(2,1)S(1)}, bf16[4,128,640]{2,1,0:T(8,128)(2,1)}, u32[]{:S(2)}, u32[]{:S(2)}) collective-permute-start(bf16[4,128,640]{2,1,0:T(8,128)(2,1)S(1)} %join.15.refs_1_), channel_id=1, source_target_pairs={{0,1},{1,0},{2,3},{3,2},{4,5},{5,4},{6,7},{7,6},{8,9},{9,8},{10,11... | collective-permute-start | bytes 1966088 | tf_op jit(solution)/shard_map/ppermute | solution.py:44
  28.2 11.6 %collective-permute-start.8 = (bf16[80,1536]{1,0:T(8,128)(2,1)}, bf16[80,1536]{1,0:T(8,128)(2,1)S(1)}, u32[]{:S(2)}, u32[]{:S(2)}) collective-permute-start(bf16[80,1536]{1,0:T(8,128)(2,1)} %slice.184), channel_id=1, source_target_pairs={{0,16},{4,20},{8,24},{12,28},{16,0},{20,4},{24,8},{28,12},{1,17},{... | collective-permute-start | bytes 737288 | tf_op jit(solution)/shard_map/ppermute | solution.py:54
  30.8 9.6 %collective-permute-start.10 = (bf16[4,128,256]{2,1,0:T(8,128)(2,1)S(1)}, bf16[4,128,256]{2,1,0:T(8,128)(2,1)S(1)}, u32[]{:S(2)}, u32[]{:S(2)}) collective-permute-start(bf16[4,128,256]{2,1,0:T(8,128)(2,1)S(1)} %join.13.refs_0_), channel_id=1, source_target_pairs={{0,8},{8,0},{16,24},{24,16},{1,9},{9,1},{17,25},{25,17},{2,10},{10... | collective-permute-start | bytes 786440 | tf_op jit(solution)/shard_map/ppermute | solution.py:44
  40.5 16.6 %collective-permute-start.14 = (bf16[112,1536]{1,0:T(8,128)(2,1)S(1)}, bf16[112,1536]{1,0:T(8,128)(2,1)S(1)}, u32[]{:S(2)}, u32[]{:S(2)}) collective-permute-start(bf16[112,1536]{1,0:T(8,128)(2,1)S(1)} %copy-done.8), channel_id=1, source_target_pairs={{0,16},{4,20},{8,24},{12,28},{16,0},{20,4},{24,8},{28,12},{1,17},{... | collective-permute-start | bytes 1032200 | tf_op jit(solution)/shard_map/ppermute | solution.py:54
  57.0 13.4 %collective-permute-start.17 = (bf16[4,128,512]{2,1,0:T(8,128)(2,1)S(1)}, bf16[4,128,512]{2,1,0:T(8,128)(2,1)S(1)}, u32[]{:S(2)}, u32[]{:S(2)}) collective-permute-start(bf16[4,128,512]{2,1,0:T(8,128)(2,1)S(1)} %get-tuple-element.118), channel_id=1, source_target_pairs={{0,2},{1,3},{2,0},{3,1},{4,6},{5,7},{6,4},{7,5},{8,10},{9,11},{10,... | collective-permute-start | bytes 1572872 | tf_op jit(solution)/shard_map/ppermute | solution.py:44
  58.5 13.5 %collective-permute-start.19 = (bf16[4,128,512]{2,1,0:T(8,128)(2,1)S(1)}, bf16[4,128,512]{2,1,0:T(8,128)(2,1)S(1)}, u32[]{:S(2)}, u32[]{:S(2)}) collective-permute-start(bf16[4,128,512]{2,1,0:T(8,128)(2,1)S(1)} %get-tuple-element.121), channel_id=1, source_target_pairs={{0,1},{1,0},{2,3},{3,2},{4,5},{5,4},{6,7},{7,6},{8,9},{9,8},{10,11... | collective-permute-start | bytes 1572872 | tf_op jit(solution)/shard_map/ppermute | solution.py:44
  58.9 43.4 %collective-permute-start.15 = (bf16[208,1536]{1,0:T(8,128)(2,1)S(1)}, bf16[208,1536]{1,0:T(8,128)(2,1)S(1)}, u32[]{:S(2)}, u32[]{:S(2)}) collective-permute-start(bf16[208,1536]{1,0:T(8,128)(2,1)S(1)} %slice.190), channel_id=1, source_target_pairs={{0,16},{4,20},{8,24},{12,28},{16,0},{20,4},{24,8},{28,12},{1,17},{... | collective-permute-start | bytes 1916936 | tf_op jit(solution)/shard_map/ppermute | solution.py:54
  60.2 23.4 %collective-permute-start.16 = (bf16[4,128,512]{2,1,0:T(8,128)(2,1)S(1)}, bf16[4,128,512]{2,1,0:T(8,128)(2,1)S(1)}, u32[]{:S(2)}, u32[]{:S(2)}) collective-permute-start(bf16[4,128,512]{2,1,0:T(8,128)(2,1)S(1)} %get-tuple-element.117), channel_id=1, source_target_pairs={{0,8},{8,0},{16,24},{24,16},{1,9},{9,1},{17,25},{25,17},{2,10},{10... | collective-permute-start | bytes 1572872 | tf_op jit(solution)/shard_map/ppermute | solution.py:44
  72.0 15.6 %collective-permute-start.20 = (bf16[2,128,512]{2,1,0:T(8,128)(2,1)S(1)}, bf16[2,128,512]{2,1,0:T(8,128)(2,1)S(1)}, u32[]{:S(2)}, u32[]{:S(2)}) collective-permute-start(bf16[2,128,512]{2,1,0:T(8,128)(2,1)S(1)} %slice.337), channel_id=1, source_target_pairs={{0,1},{1,0},{2,3},{3,2},{4,5},{5,4},{6,7},{7,6},{8,9},{9,8},{10,11... | collective-permute-start | bytes 786440 | tf_op jit(solution)/shard_map/ppermute | solution.py:44
  83.6 10.8 %collective-permute-start.22 = (bf16[2,128,512]{2,1,0:T(8,128)(2,1)S(1)}, bf16[2,128,512]{2,1,0:T(8,128)(2,1)S(1)}, u32[]{:S(2)}, u32[]{:S(2)}) collective-permute-start(bf16[2,128,512]{2,1,0:T(8,128)(2,1)S(1)} %slice.336), channel_id=1, source_target_pairs={{0,8},{8,0},{16,24},{24,16},{1,9},{9,1},{17,25},{25,17},{2,10},{10... | collective-permute-start | bytes 786440 | tf_op jit(solution)/shard_map/ppermute | solution.py:44
  86.3 8.2 %collective-permute-start.18 = (bf16[2,128,512]{2,1,0:T(8,128)(2,1)S(1)}, bf16[2,128,512]{2,1,0:T(8,128)(2,1)S(1)}, u32[]{:S(2)}, u32[]{:S(2)}) collective-permute-start(bf16[2,128,512]{2,1,0:T(8,128)(2,1)S(1)} %slice.338), channel_id=1, source_target_pairs={{0,2},{1,3},{2,0},{3,1},{4,6},{5,7},{6,4},{7,5},{8,10},{9,11},{10,... | collective-permute-start | bytes 786440 | tf_op jit(solution)/shard_map/ppermute | solution.py:44
  102.3 16.3 %collective-permute-start.29 = (bf16[64,1536]{1,0:T(8,128)(2,1)S(1)}, bf16[64,1536]{1,0:T(8,128)(2,1)S(1)}, u32[]{:S(2)}, u32[]{:S(2)}) collective-permute-start(bf16[64,1536]{1,0:T(8,128)(2,1)S(1)} %get-tuple-element.131), channel_id=1, source_target_pairs={{0,20},{4,16},{8,28},{12,24},{16,4},{20,0},{24,12},{28,8},{1,21},{... | collective-permute-start | bytes 589832 | tf_op jit(solution)/shard_map/ppermute | solution.py:54
  104.5 18.5 %collective-permute-start.28 = (bf16[64,1536]{1,0:T(8,128)(2,1)S(1)}, bf16[64,1536]{1,0:T(8,128)(2,1)S(1)}, u32[]{:S(2)}, u32[]{:S(2)}) collective-permute-start(bf16[64,1536]{1,0:T(8,128)(2,1)S(1)} %get-tuple-element.129), channel_id=1, source_target_pairs={{0,16},{4,20},{8,24},{12,28},{16,0},{20,4},{24,8},{28,12},{1,17},{... | collective-permute-start | bytes 589832 | tf_op jit(solution)/shard_map/ppermute | solution.py:54
  129.1 8.6 %collective-permute-start.37 = (bf16[2,128,640]{2,1,0:T(8,128)(2,1)S(1)}, bf16[2,128,640]{2,1,0:T(8,128)(2,1)S(1)}, u32[]{:S(2)}, u32[]{:S(2)}) collective-permute-start(bf16[2,128,640]{2,1,0:T(8,128)(2,1)S(1)} %join.22.a_ref), channel_id=1, source_target_pairs={{0,1},{1,0},{2,3},{3,2},{4,5},{5,4},{6,7},{7,6},{8,9},{9,8},{10,11... | collective-permute-start | bytes 983048 | tf_op jit(solution)/shard_map/ppermute | solution.py:44
  130.6 12.5 %collective-permute-start.35 = (bf16[2,128,640]{2,1,0:T(8,128)(2,1)S(1)}, bf16[2,128,640]{2,1,0:T(8,128)(2,1)S(1)}, u32[]{:S(2)}, u32[]{:S(2)}) collective-permute-start(bf16[2,128,640]{2,1,0:T(8,128)(2,1)S(1)} %join.20.a_ref), channel_id=1, source_target_pairs={{0,8},{8,0},{16,24},{24,16},{1,9},{9,1},{17,25},{25,17},{2,10},{10... | collective-permute-start | bytes 983048 | tf_op jit(solution)/shard_map/ppermute | solution.py:44
  131.7 9.6 %collective-permute-start.33 = (bf16[64,1536]{1,0:T(8,128)(2,1)S(1)}, bf16[64,1536]{1,0:T(8,128)(2,1)S(1)}, u32[]{:S(2)}, u32[]{:S(2)}) collective-permute-start(bf16[64,1536]{1,0:T(8,128)(2,1)S(1)} %get-tuple-element.137), channel_id=1, source_target_pairs={{0,16},{4,20},{8,24},{12,28},{16,0},{20,4},{24,8},{28,12},{1,17},{... | collective-permute-start | bytes 589832 | tf_op jit(solution)/shard_map/ppermute | solution.py:54
  133.1 8.2 %collective-permute-start.32 = (bf16[2,128,256]{2,1,0:T(8,128)(2,1)S(1)}, bf16[2,128,256]{2,1,0:T(8,128)(2,1)S(1)}, u32[]{:S(2)}, u32[]{:S(2)}) collective-permute-start(bf16[2,128,256]{2,1,0:T(8,128)(2,1)S(1)} %join.18.a_ref), channel_id=1, source_target_pairs={{0,2},{1,3},{2,0},{3,1},{4,6},{5,7},{6,4},{7,5},{8,10},{9,11},{10,... | collective-permute-start | bytes 393224 | tf_op jit(solution)/shard_map/ppermute | solution.py:44
  141.3 14.1 %collective-permute-start.40 = (bf16[4,128,640]{2,1,0:T(8,128)(2,1)S(1)}, bf16[4,128,640]{2,1,0:T(8,128)(2,1)S(1)}, u32[]{:S(2)}, u32[]{:S(2)}) collective-permute-start(bf16[4,128,640]{2,1,0:T(8,128)(2,1)S(1)} %join.23.refs_2_), channel_id=1, source_target_pairs={{0,2},{1,3},{2,0},{3,1},{4,6},{5,7},{6,4},{7,5},{8,10},{9,11},{10,... | collective-permute-start | bytes 1966088 | tf_op jit(solution)/shard_map/ppermute | solution.py:44
  143.2 15.4 %collective-permute-start.39 = (bf16[4,128,640]{2,1,0:T(8,128)(2,1)S(1)}, bf16[4,128,640]{2,1,0:T(8,128)(2,1)S(1)}, u32[]{:S(2)}, u32[]{:S(2)}) collective-permute-start(bf16[4,128,640]{2,1,0:T(8,128)(2,1)S(1)} %join.21.refs_1_), channel_id=1, source_target_pairs={{0,1},{1,0},{2,3},{3,2},{4,5},{5,4},{6,7},{7,6},{8,9},{9,8},{10,11... | collective-permute-start | bytes 1966088 | tf_op jit(solution)/shard_map/ppermute | solution.py:44
  143.9 10.3 %collective-permute-start.38 = (bf16[64,1536]{1,0:T(8,128)(2,1)S(1)}, bf16[64,1536]{1,0:T(8,128)(2,1)S(1)}, u32[]{:S(2)}, u32[]{:S(2)}) collective-permute-start(bf16[64,1536]{1,0:T(8,128)(2,1)S(1)} %get-tuple-element.142), channel_id=1, source_target_pairs={{0,16},{4,20},{8,24},{12,28},{16,0},{20,4},{24,8},{28,12},{1,17},{... | collective-permute-start | bytes 589832 | tf_op jit(solution)/shard_map/ppermute | solution.py:54
  146.8 8.6 %collective-permute-start.36 = (bf16[4,128,256]{2,1,0:T(8,128)(2,1)S(1)}, bf16[4,128,256]{2,1,0:T(8,128)(2,1)S(1)}, u32[]{:S(2)}, u32[]{:S(2)}) collective-permute-start(bf16[4,128,256]{2,1,0:T(8,128)(2,1)S(1)} %join.19.refs_0_), channel_id=1, source_target_pairs={{0,8},{8,0},{16,24},{24,16},{1,9},{9,1},{17,25},{25,17},{2,10},{10... | collective-permute-start | bytes 786440 | tf_op jit(solution)/shard_map/ppermute | solution.py:44
  158.6 14.1 %collective-permute-start.41 = (bf16[112,1536]{1,0:T(8,128)(2,1)S(1)}, bf16[112,1536]{1,0:T(8,128)(2,1)S(1)}, u32[]{:S(2)}, u32[]{:S(2)}) collective-permute-start(bf16[112,1536]{1,0:T(8,128)(2,1)S(1)} %copy-done.7), channel_id=1, source_target_pairs={{0,16},{4,20},{8,24},{12,28},{16,0},{20,4},{24,8},{28,12},{1,17},{... | collective-permute-start | bytes 1032200 | tf_op jit(solution)/shard_map/ppermute | solution.py:54
  172.8 13.4 %collective-permute-start.45 = (bf16[4,128,512]{2,1,0:T(8,128)(2,1)S(1)}, bf16[4,128,512]{2,1,0:T(8,128)(2,1)S(1)}, u32[]{:S(2)}, u32[]{:S(2)}) collective-permute-start(bf16[4,128,512]{2,1,0:T(8,128)(2,1)S(1)} %get-tuple-element.158), channel_id=1, source_target_pairs={{0,2},{1,3},{2,0},{3,1},{4,6},{5,7},{6,4},{7,5},{8,10},{9,11},{10,... | collective-permute-start | bytes 1572872 | tf_op jit(solution)/shard_map/ppermute | solution.py:44
  174.7 17.8 %collective-permute-start.42 = (f32[8,512]{1,0:T(8,128)S(1)}, f32[8,512]{1,0:T(8,128)S(1)}, u32[]{:S(2)}, u32[]{:S(2)}) collective-permute-start(f32[8,512]{1,0:T(8,128)S(1)} %get-tuple-element.149), channel_id=1, source_target_pairs={{0,16},{4,20},{8,24},{12,28},{16,0},{20,4},{24,8},{28,12},{1,17},{... | collective-permute-start | bytes 49160 | tf_op jit(solution)/shard_map/ppermute | solution.py:54
  175.0 12.7 %collective-permute-start.44 = (bf16[4,128,512]{2,1,0:T(8,128)(2,1)S(1)}, bf16[4,128,512]{2,1,0:T(8,128)(2,1)S(1)}, u32[]{:S(2)}, u32[]{:S(2)}) collective-permute-start(bf16[4,128,512]{2,1,0:T(8,128)(2,1)S(1)} %get-tuple-element.156), channel_id=1, source_target_pairs={{0,1},{1,0},{2,3},{3,2},{4,5},{5,4},{6,7},{7,6},{8,9},{9,8},{10,11... | collective-permute-start | bytes 1572872 | tf_op jit(solution)/shard_map/ppermute | solution.py:44
  176.7 13.1 %collective-permute-start.43 = (bf16[4,128,512]{2,1,0:T(8,128)(2,1)S(1)}, bf16[4,128,512]{2,1,0:T(8,128)(2,1)S(1)}, u32[]{:S(2)}, u32[]{:S(2)}) collective-permute-start(bf16[4,128,512]{2,1,0:T(8,128)(2,1)S(1)} %get-tuple-element.154), channel_id=1, source_target_pairs={{0,8},{8,0},{16,24},{24,16},{1,9},{9,1},{17,25},{25,17},{2,10},{10... | collective-permute-start | bytes 1572872 | tf_op jit(solution)/shard_map/ppermute | solution.py:44
  194.0 10.5 %collective-permute-start.46 = (f32[16,512]{1,0:T(8,128)S(1)}, f32[16,512]{1,0:T(8,128)S(1)}, u32[]{:S(2)}, u32[]{:S(2)}) collective-permute-start(f32[16,512]{1,0:T(8,128)S(1)} %get-tuple-element.161), channel_id=1, source_target_pairs={{0,1},{1,0},{2,3},{3,2},{4,5},{5,4},{6,7},{7,6},{8,9},{9,8},{10,11... | collective-permute-start | bytes 98312 | tf_op jit(solution)/shard_map/ppermute | solution.py:44
  (34 other events, 196.0 us)

commit v5 on v4

--- a/solution.py
+++ b/solution.py
@@ -664,13 +664,13 @@
     aux, base, mix = prepare(core, stat, ids_rows, slots, next_slots, tied(tokens, *held))
     far_aux = ahead(aux, 2)
 
-    came = [tied(c, far[0], mix) for c in came]
+    came = [tied(c, mix) for c in came]
     far.append(ahead(tied(pieces[1], *came), 2))
     keep, send = experts_late(
         me, held, came, gain_all, sums, gate_w, up_w, down_w, orders, sum_orders, cuts(feats, OUT_PARTS)
     )
     far.append(ahead(tied(pieces[2], *send), 2))
-    summed, _ = sum_cube(keep, send, sum_orders, {0: [far[1]]})
+    summed, _ = sum_cube(keep, send, sum_orders, {0: [far[0], far[1]]})
 
     mine = [s[:CAP] for s in summed]
     theirs = [swapped(s[CAP:], across) for s in summed]

time: 211 us -> 209 us (level)
  transfers between devices with their start and end apart: 57 -> 57, of which waited for: 35 -> 34; matrix products, arithmetic and copies ran while one was open for 2% -> 2% of each run, Pallas kernels for 20% -> 21%
where the time goes in v5:
time: 209 us
  waiting for transfers between devices  92.9 us (44%)
  starting transfers between devices  61.6 us (29%)
  Pallas kernels  46.2 us (22%)
  local copies, waits for them, and re-layouts  5.79 us (3%)
    ppermute x47, waiting for transfers between devices, swapped(): lax.ppermute(x, axis, [(i, i ^ 1 << bit) for i in range(lax.axis_size(axi...  68.6 us
    ppermute x47, starting transfers between devices, swapped(): lax.ppermute(x, axis, [(i, i ^ 1 << bit) for i in range(lax.axis_size(axi...  43.9 us
    pallas_call x2, Pallas kernels, experts_late(): pl.pallas_call(functools.partial(late_kernel, units, orders, sum_orders,...  27.4 us
    ppermute x10, waiting for transfers between devices, ahead(): return lax.ppermute(x, ('section', 'expert'), perm)  24.3 us
    ppermute x10, starting transfers between devices, ahead(): return lax.ppermute(x, ('section', 'expert'), perm)  17.7 us
    pallas_call x2, Pallas kernels, experts_early(): pl.pallas_call(functools.partial(early_kernel, units, orders, feats), nam...  12.4 us
  transfers between devices with their start and end apart: 57, of which 34 were waited for; matrix products, arithmetic and copies ran while one was open for 2% of the time, Pallas kernels for 21%

profile of v5, /device:TPU:0, one launch (start us, length us, event | category | flops | bytes accessed | tf_op | source)
XLA Modules:
  0.0 208.9 jit_solution(667319867176339832)
XLA Ops:
  5.8 3.0 %collective-permute-start.5 = (bf16[1,128,640]{2,1,0:T(8,128)(2,1)S(1)}, bf16[1,128,640]{2,1,0:T(8,128)(2,1)S(1)}, u32[]{:S(2)}, u32[]{:S(2)}) collective-permute-start(bf16[1,128,640]{2,1,0:T(8,128)(2,1)S(1)} %get-tuple-element.92.a_ref), channel_id=1, source_target_pairs={{0,8},{8,0},{16,24},{24,16},{1,9},{9,1},{17,25},{25,17},{2,10},{10... | collective-permute-start | bytes 491528 | tf_op jit(solution)/shard_map/ppermute | solution.py:44
  13.1 2.6 %collective-permute-start.9 = (f32[8,512]{1,0:T(8,128)S(1)}, f32[8,512]{1,0:T(8,128)S(1)}, u32[]{:S(2)}, u32[]{:S(2)}) collective-permute-start(f32[8,512]{1,0:T(8,128)S(1)} %get-tuple-element.98.slots_ref), channel_id=1, source_target_pairs={{0,16},{4,20},{8,24},{12,28},{16,0},{20,4},{24,8},{28,12},{1,17},{... | collective-permute-start | bytes 49160 | tf_op jit(solution)/shard_map/ppermute | solution.py:54
  20.1 4.4 %collective-permute-done.7.b_ref = bf16[2,128,640]{2,1,0:T(8,128)(2,1)S(1)} collective-permute-done((bf16[2,128,640]{2,1,0:T(8,128)(2,1)S(1)}, bf16[2,128,640]{2,1,0:T(8,128)(2,1)S(1)}, u32[]{:S(2)}, u32[]{:S(2)}) %collective-permute-start.7) | collective-permute-done | bytes 327712 | tf_op jit(solution)/shard_map/ppermute | solution.py:44
  29.1 2.6 %collective-permute-start.8 = (bf16[80,1536]{1,0:T(8,128)(2,1)}, bf16[80,1536]{1,0:T(8,128)(2,1)S(1)}, u32[]{:S(2)}, u32[]{:S(2)}) collective-permute-start(bf16[80,1536]{1,0:T(8,128)(2,1)} %slice.184), channel_id=1, source_target_pairs={{0,16},{4,20},{8,24},{12,28},{16,0},{20,4},{24,8},{28,12},{1,17},{... | collective-permute-start | bytes 737288 | tf_op jit(solution)/shard_map/ppermute | solution.py:54
  32.2 6.2 %experts_early.2 = (f32[256,1024]{1,0:T(8,128)S(1)}, f32[256,1024]{1,0:T(8,128)S(1)}, f32[256,128]{1,0:T(8,128)S(1)}) custom-call(s32[1]{0:T(128)} %bitcast.6.me, bf16[4,128,256]{2,1,0:T(8,128)(2,1)S(1)} %join.13.refs_0_, bf16[4,128,640]{2,1,0:T(8,128)(2,1)S(1)} %join.15.refs_1_, bf16[4,128,640]{2,1,0:T(8,128)(2,1)S(1)} %join.17.refs_2_, ...), custom_call_target="tpu_custom_call" | custom-call | flops 3221225472 | bytes 12582912 | tf_op jit(solution)/shard_map/experts_early/pallas_call | solution.py:546
  39.9 1.7 collective-permute-start.14
  41.7 14.2 %experts_late.2 = (bf16[4,128,512]{2,1,0:T(8,128)(2,1)S(1)}, bf16[4,128,512]{2,1,0:T(8,128)(2,1)S(1)}, bf16[4,128,512]{2,1,0:T(8,128)(2,1)S(1)}, bf16[4,128,512]...) custom-call(s32[1]{0:T(128)} %bitcast.6.me, ...), custom_call_target="tpu_custom_call" | custom-call | flops 6442450944 | bytes 25165824 | tf_op jit(solution)/shard_map/experts_late/pallas_call | solution.py:578
  55.9 1.8 collective-permute-start.17
  61.0 8.6 %collective-permute-done.17 = bf16[4,128,512]{2,1,0:T(8,128)(2,1)S(1)} collective-permute-done((bf16[4,128,512]{2,1,0:T(8,128)(2,1)S(1)}, bf16[4,128,512]{2,1,0:T(8,128)(2,1)S(1)}, u32[]{:S(2)}, u32[]{:S(2)}) %collective-permute-start.17) | collective-permute-done | bytes 524320 | tf_op jit(solution)/shard_map/ppermute | solution.py:44
  71.6 11.3 %collective-permute-done.16 = bf16[4,128,512]{2,1,0:T(8,128)(2,1)S(1)} collective-permute-done((bf16[4,128,512]{2,1,0:T(8,128)(2,1)S(1)}, bf16[4,128,512]{2,1,0:T(8,128)(2,1)S(1)}, u32[]{:S(2)}, u32[]{:S(2)}) %collective-permute-start.16) | collective-permute-done | bytes 524320 | tf_op jit(solution)/shard_map/ppermute | solution.py:44
  82.9 2.5 %collective-permute-start.22 = (bf16[2,128,512]{2,1,0:T(8,128)(2,1)S(1)}, bf16[2,128,512]{2,1,0:T(8,128)(2,1)S(1)}, u32[]{:S(2)}, u32[]{:S(2)}) collective-permute-start(bf16[2,128,512]{2,1,0:T(8,128)(2,1)S(1)} %slice.336), channel_id=1, source_target_pairs={{0,8},{8,0},{16,24},{24,16},{1,9},{9,1},{17,25},{25,17},{2,10},{10... | collective-permute-start | bytes 786440 | tf_op jit(solution)/shard_map/ppermute | solution.py:44
  86.3 6.8 %collective-permute-done.22 = bf16[2,128,512]{2,1,0:T(8,128)(2,1)S(1)} collective-permute-done((bf16[2,128,512]{2,1,0:T(8,128)(2,1)S(1)}, bf16[2,128,512]{2,1,0:T(8,128)(2,1)S(1)}, u32[]{:S(2)}, u32[]{:S(2)}) %collective-permute-start.22) | collective-permute-done | bytes 262176 | tf_op jit(solution)/shard_map/ppermute | solution.py:44
  95.2 3.2 %collective-permute-done.24 = bf16[1,128,512]{2,1,0:T(8,128)(2,1)S(1)} collective-permute-done((bf16[1,128,512]{2,1,0:T(8,128)(2,1)S(1)}, bf16[1,128,512]{2,1,0:T(8,128)(2,1)S(1)}, u32[]{:S(2)}, u32[]{:S(2)}) %collective-permute-start.24) | collective-permute-done | bytes 131104 | tf_op jit(solution)/shard_map/ppermute | solution.py:44
  100.9 2.0 collective-permute-start.29
  103.7 13.5 %collective-permute-done.29.other_ref = bf16[64,1536]{1,0:T(8,128)(2,1)S(1)} collective-permute-done((bf16[64,1536]{1,0:T(8,128)(2,1)S(1)}, bf16[64,1536]{1,0:T(8,128)(2,1)S(1)}, u32[]{:S(2)}, u32[]{:S(2)}) %collective-permute-start.29) | collective-permute-done | bytes 196640 | tf_op jit(solution)/shard_map/ppermute | solution.py:54
  117.2 4.6 %collective-permute-done.28.own_ref = bf16[64,1536]{1,0:T(8,128)(2,1)S(1)} collective-permute-done((bf16[64,1536]{1,0:T(8,128)(2,1)S(1)}, bf16[64,1536]{1,0:T(8,128)(2,1)S(1)}, u32[]{:S(2)}, u32[]{:S(2)}) %collective-permute-start.28) | collective-permute-done | bytes 196640 | tf_op jit(solution)/shard_map/ppermute | solution.py:54
  124.1 3.6 %collective-permute-done.34.b_ref = bf16[1,128,640]{2,1,0:T(8,128)(2,1)S(1)} collective-permute-done((bf16[1,128,640]{2,1,0:T(8,128)(2,1)S(1)}, bf16[1,128,640]{2,1,0:T(8,128)(2,1)S(1)}, u32[]{:S(2)}, u32[]{:S(2)}) %collective-permute-start.34) | collective-permute-done | bytes 163872 | tf_op jit(solution)/shard_map/ppermute | solution.py:44
  132.5 3.8 %collective-permute-done.37.b_ref = bf16[2,128,640]{2,1,0:T(8,128)(2,1)S(1)} collective-permute-done((bf16[2,128,640]{2,1,0:T(8,128)(2,1)S(1)}, bf16[2,128,640]{2,1,0:T(8,128)(2,1)S(1)}, u32[]{:S(2)}, u32[]{:S(2)}) %collective-permute-start.37) | collective-permute-done | bytes 327712 | tf_op jit(solution)/shard_map/ppermute | solution.py:44
  136.4 3.5 %collective-permute-done.33.own_ref = bf16[64,1536]{1,0:T(8,128)(2,1)S(1)} collective-permute-done((bf16[64,1536]{1,0:T(8,128)(2,1)S(1)}, bf16[64,1536]{1,0:T(8,128)(2,1)S(1)}, u32[]{:S(2)}, u32[]{:S(2)}) %collective-permute-start.33) | collective-permute-done | bytes 196640 | tf_op jit(solution)/shard_map/ppermute | solution.py:54
  142.5 2.9 %collective-permute-start.38 = (bf16[64,1536]{1,0:T(8,128)(2,1)S(1)}, bf16[64,1536]{1,0:T(8,128)(2,1)S(1)}, u32[]{:S(2)}, u32[]{:S(2)}) collective-permute-start(bf16[64,1536]{1,0:T(8,128)(2,1)S(1)} %get-tuple-element.142), channel_id=1, source_target_pairs={{0,16},{4,20},{8,24},{12,28},{16,0},{20,4},{24,8},{28,12},{1,17},{... | collective-permute-start | bytes 589832 | tf_op jit(solution)/shard_map/ppermute | solution.py:54
  145.5 6.2 %experts_early.3 = (f32[256,1024]{1,0:T(8,128)S(1)}, f32[256,1024]{1,0:T(8,128)S(1)}, f32[256,128]{1,0:T(8,128)S(1)}) custom-call(s32[1]{0:T(128)} %bitcast.6.me, bf16[4,128,256]{2,1,0:T(8,128)(2,1)S(1)} %join.19.refs_0_, bf16[4,128,640]{2,1,0:T(8,128)(2,1)S(1)} %join.21.refs_1_, bf16[4,128,640]{2,1,0:T(8,128)(2,1)S(1)} %join.23.refs_2_, ...), custom_call_target="tpu_custom_call" | custom-call | flops 3221225472 | bytes 12582912 | tf_op jit(solution)/shard_map/experts_early/pallas_call | solution.py:546
  153.8 2.9 %collective-permute-done.39.refs_4_ = bf16[4,128,640]{2,1,0:T(8,128)(2,1)S(1)} collective-permute-done((bf16[4,128,640]{2,1,0:T(8,128)(2,1)S(1)}, bf16[4,128,640]{2,1,0:T(8,128)(2,1)S(1)}, u32[]{:S(2)}, u32[]{:S(2)}) %collective-permute-start.39) | collective-permute-done | bytes 655392 | tf_op jit(solution)/shard_map/ppermute | solution.py:44
  157.6 13.1 %experts_late.3 = (bf16[4,128,512]{2,1,0:T(8,128)(2,1)S(1)}, bf16[4,128,512]{2,1,0:T(8,128)(2,1)S(1)}, bf16[4,128,512]{2,1,0:T(8,128)(2,1)S(1)}, bf16[4,128,512]...) custom-call(s32[1]{0:T(128)} %bitcast.6.me, ...), custom_call_target="tpu_custom_call" | custom-call | flops 6442450944 | bytes 25165824 | tf_op jit(solution)/shard_map/experts_late/pallas_call | solution.py:578
  170.7 1.8 collective-permute-done.41
  175.4 1.6 collective-permute-start.43
  177.1 9.3 %collective-permute-done.45 = bf16[4,128,512]{2,1,0:T(8,128)(2,1)S(1)} collective-permute-done((bf16[4,128,512]{2,1,0:T(8,128)(2,1)S(1)}, bf16[4,128,512]{2,1,0:T(8,128)(2,1)S(1)}, u32[]{:S(2)}, u32[]{:S(2)}) %collective-permute-start.45) | collective-permute-done | bytes 524320 | tf_op jit(solution)/shard_map/ppermute | solution.py:44
  188.4 2.1 %collective-permute-start.51 = (bf16[2,128,512]{2,1,0:T(8,128)(2,1)S(1)}, bf16[2,128,512]{2,1,0:T(8,128)(2,1)S(1)}, u32[]{:S(2)}, u32[]{:S(2)}) collective-permute-start(bf16[2,128,512]{2,1,0:T(8,128)(2,1)S(1)} %slice.333), channel_id=1, source_target_pairs={{0,8},{8,0},{16,24},{24,16},{1,9},{9,1},{17,25},{25,17},{2,10},{10... | collective-permute-start | bytes 786440 | tf_op jit(solution)/shard_map/ppermute | solution.py:44
  195.3 1.7 collective-permute-start.53
  200.4 2.0 collective-permute-done.52
  203.1 1.7 collective-permute-start.47
  204.8 2.3 %collective-permute-done.47 = f32[16,512]{1,0:T(8,128)S(1)} collective-permute-done((f32[16,512]{1,0:T(8,128)S(1)}, f32[16,512]{1,0:T(8,128)S(1)}, u32[]{:S(2)}, u32[]{:S(2)}) %collective-permute-start.47) | collective-permute-done | bytes 32800 | tf_op jit(solution)/shard_map/ppermute | solution.py:44
  207.1 1.8 last.1
  (181 shorter events, 58.9 us)
Async XLA Ops:
  5.8 10.0 %collective-permute-start.5 = (bf16[1,128,640]{2,1,0:T(8,128)(2,1)S(1)}, bf16[1,128,640]{2,1,0:T(8,128)(2,1)S(1)}, u32[]{:S(2)}, u32[]{:S(2)}) collective-permute-start(bf16[1,128,640]{2,1,0:T(8,128)(2,1)S(1)} %get-tuple-element.92.a_ref), channel_id=1, source_target_pairs={{0,8},{8,0},{16,24},{24,16},{1,9},{9,1},{17,25},{25,17},{2,10},{10... | collective-permute-start | bytes 491528 | tf_op jit(solution)/shard_map/ppermute | solution.py:44
  13.1 11.5 %collective-permute-start.9 = (f32[8,512]{1,0:T(8,128)S(1)}, f32[8,512]{1,0:T(8,128)S(1)}, u32[]{:S(2)}, u32[]{:S(2)}) collective-permute-start(f32[8,512]{1,0:T(8,128)S(1)} %get-tuple-element.98.slots_ref), channel_id=1, source_target_pairs={{0,16},{4,20},{8,24},{12,28},{16,0},{20,4},{24,8},{28,12},{1,17},{... | collective-permute-start | bytes 49160 | tf_op jit(solution)/shard_map/ppermute | solution.py:54
  16.4 8.1 %collective-permute-start.7 = (bf16[2,128,640]{2,1,0:T(8,128)(2,1)S(1)}, bf16[2,128,640]{2,1,0:T(8,128)(2,1)S(1)}, u32[]{:S(2)}, u32[]{:S(2)}) collective-permute-start(bf16[2,128,640]{2,1,0:T(8,128)(2,1)S(1)} %join.16.a_ref), channel_id=1, source_target_pairs={{0,1},{1,0},{2,3},{3,2},{4,5},{5,4},{6,7},{7,6},{8,9},{9,8},{10,11... | collective-permute-start | bytes 983048 | tf_op jit(solution)/shard_map/ppermute | solution.py:44
  17.4 8.1 %collective-permute-start.6 = (bf16[2,128,640]{2,1,0:T(8,128)(2,1)S(1)}, bf16[2,128,640]{2,1,0:T(8,128)(2,1)S(1)}, u32[]{:S(2)}, u32[]{:S(2)}) collective-permute-start(bf16[2,128,640]{2,1,0:T(8,128)(2,1)S(1)} %join.14.a_ref), channel_id=1, source_target_pairs={{0,8},{8,0},{16,24},{24,16},{1,9},{9,1},{17,25},{25,17},{2,10},{10... | collective-permute-start | bytes 983048 | tf_op jit(solution)/shard_map/ppermute | solution.py:44
  18.6 9.5 %collective-permute-start.11 = (f32[16,512]{1,0:T(8,128)S(1)}, f32[16,512]{1,0:T(8,128)S(1)}, u32[]{:S(2)}, u32[]{:S(2)}) collective-permute-start(f32[16,512]{1,0:T(8,128)S(1)} %fusion.8), channel_id=1, source_target_pairs={{0,2},{1,3},{2,0},{3,1},{4,6},{5,7},{6,4},{7,5},{8,10},{9,11},{10,... | collective-permute-start | bytes 98312 | tf_op jit(solution)/shard_map/ppermute | solution.py:44
  24.6 14.4 %collective-permute-start.13 = (bf16[4,128,640]{2,1,0:T(8,128)(2,1)S(1)}, bf16[4,128,640]{2,1,0:T(8,128)(2,1)}, u32[]{:S(2)}, u32[]{:S(2)}) collective-permute-start(bf16[4,128,640]{2,1,0:T(8,128)(2,1)S(1)} %join.17.refs_2_), channel_id=1, source_target_pairs={{0,2},{1,3},{2,0},{3,1},{4,6},{5,7},{6,4},{7,5},{8,10},{9,11},{10,... | collective-permute-start | bytes 1966088 | tf_op jit(solution)/shard_map/ppermute | solution.py:44
  25.6 14.3 %collective-permute-start.12 = (bf16[4,128,640]{2,1,0:T(8,128)(2,1)S(1)}, bf16[4,128,640]{2,1,0:T(8,128)(2,1)}, u32[]{:S(2)}, u32[]{:S(2)}) collective-permute-start(bf16[4,128,640]{2,1,0:T(8,128)(2,1)S(1)} %join.15.refs_1_), channel_id=1, source_target_pairs={{0,1},{1,0},{2,3},{3,2},{4,5},{5,4},{6,7},{7,6},{8,9},{9,8},{10,11... | collective-permute-start | bytes 1966088 | tf_op jit(solution)/shard_map/ppermute | solution.py:44
  28.2 10.8 %collective-permute-start.10 = (bf16[4,128,256]{2,1,0:T(8,128)(2,1)S(1)}, bf16[4,128,256]{2,1,0:T(8,128)(2,1)S(1)}, u32[]{:S(2)}, u32[]{:S(2)}) collective-permute-start(bf16[4,128,256]{2,1,0:T(8,128)(2,1)S(1)} %join.13.refs_0_), channel_id=1, source_target_pairs={{0,8},{8,0},{16,24},{24,16},{1,9},{9,1},{17,25},{25,17},{2,10},{10... | collective-permute-start | bytes 786440 | tf_op jit(solution)/shard_map/ppermute | solution.py:44
  29.1 26.8 %collective-permute-start.8 = (bf16[80,1536]{1,0:T(8,128)(2,1)}, bf16[80,1536]{1,0:T(8,128)(2,1)S(1)}, u32[]{:S(2)}, u32[]{:S(2)}) collective-permute-start(bf16[80,1536]{1,0:T(8,128)(2,1)} %slice.184), channel_id=1, source_target_pairs={{0,16},{4,20},{8,24},{12,28},{16,0},{20,4},{24,8},{28,12},{1,17},{... | collective-permute-start | bytes 737288 | tf_op jit(solution)/shard_map/ppermute | solution.py:54
  39.9 16.0 %collective-permute-start.14 = (bf16[112,1536]{1,0:T(8,128)(2,1)S(1)}, bf16[112,1536]{1,0:T(8,128)(2,1)S(1)}, u32[]{:S(2)}, u32[]{:S(2)}) collective-permute-start(bf16[112,1536]{1,0:T(8,128)(2,1)S(1)} %copy-done.8), channel_id=1, source_target_pairs={{0,16},{4,20},{8,24},{12,28},{16,0},{20,4},{24,8},{28,12},{1,17},{... | collective-permute-start | bytes 1032200 | tf_op jit(solution)/shard_map/ppermute | solution.py:54
  55.9 13.7 %collective-permute-start.17 = (bf16[4,128,512]{2,1,0:T(8,128)(2,1)S(1)}, bf16[4,128,512]{2,1,0:T(8,128)(2,1)S(1)}, u32[]{:S(2)}, u32[]{:S(2)}) collective-permute-start(bf16[4,128,512]{2,1,0:T(8,128)(2,1)S(1)} %get-tuple-element.118), channel_id=1, source_target_pairs={{0,2},{1,3},{2,0},{3,1},{4,6},{5,7},{6,4},{7,5},{8,10},{9,11},{10,... | collective-permute-start | bytes 1572872 | tf_op jit(solution)/shard_map/ppermute | solution.py:44
  57.7 12.3 %collective-permute-start.19 = (bf16[4,128,512]{2,1,0:T(8,128)(2,1)S(1)}, bf16[4,128,512]{2,1,0:T(8,128)(2,1)S(1)}, u32[]{:S(2)}, u32[]{:S(2)}) collective-permute-start(bf16[4,128,512]{2,1,0:T(8,128)(2,1)S(1)} %get-tuple-element.121), channel_id=1, source_target_pairs={{0,1},{1,0},{2,3},{3,2},{4,5},{5,4},{6,7},{7,6},{8,9},{9,8},{10,11... | collective-permute-start | bytes 1572872 | tf_op jit(solution)/shard_map/ppermute | solution.py:44
  58.3 42.6 %collective-permute-start.15 = (bf16[208,1536]{1,0:T(8,128)(2,1)S(1)}, bf16[208,1536]{1,0:T(8,128)(2,1)S(1)}, u32[]{:S(2)}, u32[]{:S(2)}) collective-permute-start(bf16[208,1536]{1,0:T(8,128)(2,1)S(1)} %slice.190), channel_id=1, source_target_pairs={{0,16},{4,20},{8,24},{12,28},{16,0},{20,4},{24,8},{28,12},{1,17},{... | collective-permute-start | bytes 1916936 | tf_op jit(solution)/shard_map/ppermute | solution.py:54
  59.6 23.3 %collective-permute-start.16 = (bf16[4,128,512]{2,1,0:T(8,128)(2,1)S(1)}, bf16[4,128,512]{2,1,0:T(8,128)(2,1)S(1)}, u32[]{:S(2)}, u32[]{:S(2)}) collective-permute-start(bf16[4,128,512]{2,1,0:T(8,128)(2,1)S(1)} %get-tuple-element.117), channel_id=1, source_target_pairs={{0,8},{8,0},{16,24},{24,16},{1,9},{9,1},{17,25},{25,17},{2,10},{10... | collective-permute-start | bytes 1572872 | tf_op jit(solution)/shard_map/ppermute | solution.py:44
  70.0 16.2 %collective-permute-start.20 = (bf16[2,128,512]{2,1,0:T(8,128)(2,1)S(1)}, bf16[2,128,512]{2,1,0:T(8,128)(2,1)S(1)}, u32[]{:S(2)}, u32[]{:S(2)}) collective-permute-start(bf16[2,128,512]{2,1,0:T(8,128)(2,1)S(1)} %slice.337), channel_id=1, source_target_pairs={{0,1},{1,0},{2,3},{3,2},{4,5},{5,4},{6,7},{7,6},{8,9},{9,8},{10,11... | collective-permute-start | bytes 786440 | tf_op jit(solution)/shard_map/ppermute | solution.py:44
  82.9 10.1 %collective-permute-start.22 = (bf16[2,128,512]{2,1,0:T(8,128)(2,1)S(1)}, bf16[2,128,512]{2,1,0:T(8,128)(2,1)S(1)}, u32[]{:S(2)}, u32[]{:S(2)}) collective-permute-start(bf16[2,128,512]{2,1,0:T(8,128)(2,1)S(1)} %slice.336), channel_id=1, source_target_pairs={{0,8},{8,0},{16,24},{24,16},{1,9},{9,1},{17,25},{25,17},{2,10},{10... | collective-permute-start | bytes 786440 | tf_op jit(solution)/shard_map/ppermute | solution.py:44
  100.9 16.3 %collective-permute-start.29 = (bf16[64,1536]{1,0:T(8,128)(2,1)S(1)}, bf16[64,1536]{1,0:T(8,128)(2,1)S(1)}, u32[]{:S(2)}, u32[]{:S(2)}) collective-permute-start(bf16[64,1536]{1,0:T(8,128)(2,1)S(1)} %get-tuple-element.131), channel_id=1, source_target_pairs={{0,20},{4,16},{8,28},{12,24},{16,4},{20,0},{24,12},{28,8},{1,21},{... | collective-permute-start | bytes 589832 | tf_op jit(solution)/shard_map/ppermute | solution.py:54
  102.9 18.8 %collective-permute-start.28 = (bf16[64,1536]{1,0:T(8,128)(2,1)S(1)}, bf16[64,1536]{1,0:T(8,128)(2,1)S(1)}, u32[]{:S(2)}, u32[]{:S(2)}) collective-permute-start(bf16[64,1536]{1,0:T(8,128)(2,1)S(1)} %get-tuple-element.129), channel_id=1, source_target_pairs={{0,16},{4,20},{8,24},{12,28},{16,0},{20,4},{24,8},{28,12},{1,17},{... | collective-permute-start | bytes 589832 | tf_op jit(solution)/shard_map/ppermute | solution.py:54
  127.7 8.6 %collective-permute-start.37 = (bf16[2,128,640]{2,1,0:T(8,128)(2,1)S(1)}, bf16[2,128,640]{2,1,0:T(8,128)(2,1)S(1)}, u32[]{:S(2)}, u32[]{:S(2)}) collective-permute-start(bf16[2,128,640]{2,1,0:T(8,128)(2,1)S(1)} %join.22.a_ref), channel_id=1, source_target_pairs={{0,1},{1,0},{2,3},{3,2},{4,5},{5,4},{6,7},{7,6},{8,9},{9,8},{10,11... | collective-permute-start | bytes 983048 | tf_op jit(solution)/shard_map/ppermute | solution.py:44
  129.0 12.5 %collective-permute-start.35 = (bf16[2,128,640]{2,1,0:T(8,128)(2,1)S(1)}, bf16[2,128,640]{2,1,0:T(8,128)(2,1)S(1)}, u32[]{:S(2)}, u32[]{:S(2)}) collective-permute-start(bf16[2,128,640]{2,1,0:T(8,128)(2,1)S(1)} %join.20.a_ref), channel_id=1, source_target_pairs={{0,8},{8,0},{16,24},{24,16},{1,9},{9,1},{17,25},{25,17},{2,10},{10... | collective-permute-start | bytes 983048 | tf_op jit(solution)/shard_map/ppermute | solution.py:44
  130.4 9.4 %collective-permute-start.33 = (bf16[64,1536]{1,0:T(8,128)(2,1)S(1)}, bf16[64,1536]{1,0:T(8,128)(2,1)S(1)}, u32[]{:S(2)}, u32[]{:S(2)}) collective-permute-start(bf16[64,1536]{1,0:T(8,128)(2,1)S(1)} %get-tuple-element.137), channel_id=1, source_target_pairs={{0,16},{4,20},{8,24},{12,28},{16,0},{20,4},{24,8},{28,12},{1,17},{... | collective-permute-start | bytes 589832 | tf_op jit(solution)/shard_map/ppermute | solution.py:54
  131.8 8.1 %collective-permute-start.32 = (bf16[2,128,256]{2,1,0:T(8,128)(2,1)S(1)}, bf16[2,128,256]{2,1,0:T(8,128)(2,1)S(1)}, u32[]{:S(2)}, u32[]{:S(2)}) collective-permute-start(bf16[2,128,256]{2,1,0:T(8,128)(2,1)S(1)} %join.18.a_ref), channel_id=1, source_target_pairs={{0,2},{1,3},{2,0},{3,1},{4,6},{5,7},{6,4},{7,5},{8,10},{9,11},{10,... | collective-permute-start | bytes 393224 | tf_op jit(solution)/shard_map/ppermute | solution.py:44
  139.9 14.0 %collective-permute-start.40 = (bf16[4,128,640]{2,1,0:T(8,128)(2,1)S(1)}, bf16[4,128,640]{2,1,0:T(8,128)(2,1)S(1)}, u32[]{:S(2)}, u32[]{:S(2)}) collective-permute-start(bf16[4,128,640]{2,1,0:T(8,128)(2,1)S(1)} %join.23.refs_2_), channel_id=1, source_target_pairs={{0,2},{1,3},{2,0},{3,1},{4,6},{5,7},{6,4},{7,5},{8,10},{9,11},{10,... | collective-permute-start | bytes 1966088 | tf_op jit(solution)/shard_map/ppermute | solution.py:44
  141.6 15.2 %collective-permute-start.39 = (bf16[4,128,640]{2,1,0:T(8,128)(2,1)S(1)}, bf16[4,128,640]{2,1,0:T(8,128)(2,1)S(1)}, u32[]{:S(2)}, u32[]{:S(2)}) collective-permute-start(bf16[4,128,640]{2,1,0:T(8,128)(2,1)S(1)} %join.21.refs_1_), channel_id=1, source_target_pairs={{0,1},{1,0},{2,3},{3,2},{4,5},{5,4},{6,7},{7,6},{8,9},{9,8},{10,11... | collective-permute-start | bytes 1966088 | tf_op jit(solution)/shard_map/ppermute | solution.py:44
  142.5 10.0 %collective-permute-start.38 = (bf16[64,1536]{1,0:T(8,128)(2,1)S(1)}, bf16[64,1536]{1,0:T(8,128)(2,1)S(1)}, u32[]{:S(2)}, u32[]{:S(2)}) collective-permute-start(bf16[64,1536]{1,0:T(8,128)(2,1)S(1)} %get-tuple-element.142), channel_id=1, source_target_pairs={{0,16},{4,20},{8,24},{12,28},{16,0},{20,4},{24,8},{28,12},{1,17},{... | collective-permute-start | bytes 589832 | tf_op jit(solution)/shard_map/ppermute | solution.py:54
  145.5 8.4 %collective-permute-start.36 = (bf16[4,128,256]{2,1,0:T(8,128)(2,1)S(1)}, bf16[4,128,256]{2,1,0:T(8,128)(2,1)S(1)}, u32[]{:S(2)}, u32[]{:S(2)}) collective-permute-start(bf16[4,128,256]{2,1,0:T(8,128)(2,1)S(1)} %join.19.refs_0_), channel_id=1, source_target_pairs={{0,8},{8,0},{16,24},{24,16},{1,9},{9,1},{17,25},{25,17},{2,10},{10... | collective-permute-start | bytes 786440 | tf_op jit(solution)/shard_map/ppermute | solution.py:44
  156.7 15.8 %collective-permute-start.41 = (bf16[112,1536]{1,0:T(8,128)(2,1)S(1)}, bf16[112,1536]{1,0:T(8,128)(2,1)S(1)}, u32[]{:S(2)}, u32[]{:S(2)}) collective-permute-start(bf16[112,1536]{1,0:T(8,128)(2,1)S(1)} %copy-done.7), channel_id=1, source_target_pairs={{0,16},{4,20},{8,24},{12,28},{16,0},{20,4},{24,8},{28,12},{1,17},{... | collective-permute-start | bytes 1032200 | tf_op jit(solution)/shard_map/ppermute | solution.py:54
  172.5 13.8 %collective-permute-start.45 = (bf16[4,128,512]{2,1,0:T(8,128)(2,1)S(1)}, bf16[4,128,512]{2,1,0:T(8,128)(2,1)S(1)}, u32[]{:S(2)}, u32[]{:S(2)}) collective-permute-start(bf16[4,128,512]{2,1,0:T(8,128)(2,1)S(1)} %get-tuple-element.158), channel_id=1, source_target_pairs={{0,2},{1,3},{2,0},{3,1},{4,6},{5,7},{6,4},{7,5},{8,10},{9,11},{10,... | collective-permute-start | bytes 1572872 | tf_op jit(solution)/shard_map/ppermute | solution.py:44
  172.5 18.5 %collective-permute-start.42 = (f32[8,512]{1,0:T(8,128)S(1)}, f32[8,512]{1,0:T(8,128)S(1)}, u32[]{:S(2)}, u32[]{:S(2)}) collective-permute-start(f32[8,512]{1,0:T(8,128)S(1)} %get-tuple-element.149), channel_id=1, source_target_pairs={{0,16},{4,20},{8,24},{12,28},{16,0},{20,4},{24,8},{28,12},{1,17},{... | collective-permute-start | bytes 49160 | tf_op jit(solution)/shard_map/ppermute | solution.py:54
  174.1 12.5 %collective-permute-start.44 = (bf16[4,128,512]{2,1,0:T(8,128)(2,1)S(1)}, bf16[4,128,512]{2,1,0:T(8,128)(2,1)S(1)}, u32[]{:S(2)}, u32[]{:S(2)}) collective-permute-start(bf16[4,128,512]{2,1,0:T(8,128)(2,1)S(1)} %get-tuple-element.156), channel_id=1, source_target_pairs={{0,1},{1,0},{2,3},{3,2},{4,5},{5,4},{6,7},{7,6},{8,9},{9,8},{10,11... | collective-permute-start | bytes 1572872 | tf_op jit(solution)/shard_map/ppermute | solution.py:44
  175.4 13.1 %collective-permute-start.43 = (bf16[4,128,512]{2,1,0:T(8,128)(2,1)S(1)}, bf16[4,128,512]{2,1,0:T(8,128)(2,1)S(1)}, u32[]{:S(2)}, u32[]{:S(2)}) collective-permute-start(bf16[4,128,512]{2,1,0:T(8,128)(2,1)S(1)} %get-tuple-element.154), channel_id=1, source_target_pairs={{0,8},{8,0},{16,24},{24,16},{1,9},{9,1},{17,25},{25,17},{2,10},{10... | collective-permute-start | bytes 1572872 | tf_op jit(solution)/shard_map/ppermute | solution.py:44
  192.6 10.5 %collective-permute-start.46 = (f32[16,512]{1,0:T(8,128)S(1)}, f32[16,512]{1,0:T(8,128)S(1)}, u32[]{:S(2)}, u32[]{:S(2)}) collective-permute-start(f32[16,512]{1,0:T(8,128)S(1)} %get-tuple-element.161), channel_id=1, source_target_pairs={{0,1},{1,0},{2,3},{3,2},{4,5},{5,4},{6,7},{7,6},{8,9},{9,8},{10,11... | collective-permute-start | bytes 98312 | tf_op jit(solution)/shard_map/ppermute | solution.py:44
  (34 other events, 194.5 us)
